TPU v7x, 512 devices: a whole 4x8x8 slice. The times are simulated.
512 devices in a mesh: group: 16 (over y, core), mp: 32 (over z, x).
Axes of the slice: x: 4, y: 8, z: 8, core: 2. Of those that a mesh axis runs over, the one named last changes fastest.
Arguments:
- resident_state: float32 [256, 16, 16384], P('group', None, 'mp'), may hold values from -4 to 4
- resident_conv: bfloat16 [256, 3, 16384], P('group', None, 'mp'), may hold values from -6 to 6
- migrate_from: int32 [256], P('group'), may hold values from 0 to 255, as said below
- decode_inputs: bfloat16 [256, 4, 16384], P('group', None, 'mp'), may hold values from -6 to 6
- decode_gates: bfloat16 [256, 4, 16384], P('group', None, 'mp'), may hold values from -6 to 6
- prompt_inputs: bfloat16 [128, 16, 16384], P('group', None, 'mp'), may hold values from -6 to 6
- prompt_gates: bfloat16 [128, 16, 16384], P('group', None, 'mp'), may hold values from -6 to 6
- prompt_length: int32 [128], P('group'), may hold values from 1 to 16, as said below
- prompt_dest: int32 [128, 1], P('group'), may hold values from 0 to 15; in each aligned block of 8 rows (0 to 7, 8 to 15, ...) at most 2 rows name the same one
- conv_weight: float32 [4, 16384], P(None, 'mp'), may hold values from -3 to 3
- conv_bias: float32 [16384], P('mp'), may hold values from -3 to 3
- rank_weight: bfloat16 [16384, 512], P('mp'), may hold values from -0.046875 to 0.046875
- select_weight: bfloat16 [16384, 32], P('mp'), may hold values from -0.09375 to 0.09375
- step_weight: bfloat16 [512, 16384], P(None, 'mp'), may hold values from -0.25 to 0.25
- step_bias: float32 [16384], P('mp'), may hold values from -4 to -1
- decay_log: float32 [16, 16384], P(None, 'mp'), may hold values from 0 to 3
- skip_gain: float32 [16384], P('mp'), may hold values from 0.5 to 1.5
Outputs:
- decode_out: bfloat16 [256, 4, 16384], P('group', None, 'mp')
- final_state: float32 [256, 16, 16384], P('group', None, 'mp')
- final_conv: bfloat16 [256, 3, 16384], P('group', None, 'mp')
- prefill_out: bfloat16 [128, 16, 16384], P('group', None, 'mp')
- prompt_state: float32 [512, 16, 16384], P('group', None, 'mp')
- prompt_conv: bfloat16 [512, 3, 16384], P('group', None, 'mp')
Inputs may be any that keep to these rules, and one draw needn't show every extreme that they name: `migrate_from`: A permutation of the 256 requests over the 256 slots; slot s of group q is entry q * 16 + s. In every group exactly 4 slots hold a request other than their own, and exactly 4 of its requests leave their slots. `prompt_length`: every group holds a prompt of length 16. `prompt_dest`: of the 8 prompts of one group, at most 2 go to one destination.
All inputs are finite; a program needn't handle non-finite values.
Results may differ from a plain program's by a relative error of at most 0.0085.
Values may be sent and summed in bfloat16 or wider, within the bound.
No kernel may reach another device: no remote copies, remote signals or barrier semaphores. Data moves between devices by JAX's collectives and lax.ppermute only.
A program may use at most 64 MiB of HBM per device.

v0:
```python
import jax
import jax.numpy as jnp
from jax import lax
from jax.sharding import PartitionSpec as P

MIG = 4
PAIR = 2


EPS = 1e-06


def local_features(inputs, history, conv_weight, conv_bias, rank_weight, select_weight):
    steps_count = inputs.shape[1]
    history_len = history.shape[1]
    padded = jnp.concatenate([history.astype(jnp.float32), inputs.astype(jnp.float32)], axis=1)
    conv_sum = conv_bias
    for offset in range(history_len + 1):
        conv_sum = conv_sum + conv_weight[offset] * padded[:, offset : offset + steps_count]
    conved = jax.nn.silu(conv_sum).astype(jnp.bfloat16)
    flat_rows = conved.reshape(-1, conved.shape[2])
    low_part = jnp.dot(flat_rows, rank_weight, preferred_element_type=jnp.float32)
    select_part = jnp.dot(flat_rows, select_weight, preferred_element_type=jnp.float32)
    return (padded, conved, low_part, select_part)


def mixer(inputs, gate_rows, history, start_state, lengths, params):
    (
        conv_weight,
        conv_bias,
        rank_weight,
        select_weight,
        step_weight,
        step_bias,
        decay_log,
        skip_gain,
    ) = params
    padded, conved, low_part, select_part = local_features(
        inputs, history, conv_weight, conv_bias, rank_weight, select_weight
    )
    low_rank, selects = lax.psum((low_part, select_part), "mp")
    item_count, steps_count, channels = conved.shape
    normed = (
        low_rank * lax.rsqrt(jnp.mean(low_rank * low_rank, axis=-1, keepdims=True) + EPS)
    ).astype(jnp.bfloat16)
    step_size = jax.nn.softplus(
        jnp.dot(normed, step_weight, preferred_element_type=jnp.float32) + step_bias
    )
    step_size = step_size.reshape(item_count, steps_count, channels)
    live_rows = jnp.arange(steps_count, dtype=jnp.int32)[None, :] < lengths[:, None]
    step_size = jnp.where(live_rows[:, :, None], step_size, 0.0)
    states = selects.shape[1] // 2
    b_rows = selects[:, :states].reshape(item_count, steps_count, states)
    c_rows = selects[:, states:].reshape(item_count, steps_count, states)
    decay_rate = -jnp.exp(decay_log)

    def block_scan(block_items):
        state_blk, step_blk, conv_blk, b_blk, c_blk, gate_blk, live_blk = block_items
        outputs_init = jnp.zeros(conv_blk.shape, jnp.bfloat16)

        def advance(position, carry):
            carried, written = carry
            step_t = lax.dynamic_index_in_dim(step_blk, position, 1, keepdims=False)
            conv_t = lax.dynamic_index_in_dim(conv_blk, position, 1, keepdims=False).astype(
                jnp.float32
            )
            b_t = lax.dynamic_index_in_dim(b_blk, position, 1, keepdims=False)
            c_t = lax.dynamic_index_in_dim(c_blk, position, 1, keepdims=False)
            gate_t = lax.dynamic_index_in_dim(gate_blk, position, 1, keepdims=False).astype(
                jnp.float32
            )
            live_t = lax.dynamic_index_in_dim(live_blk, position, 1, keepdims=False)
            carried = (
                jnp.exp(step_t[:, None, :] * decay_rate) * carried
                + (step_t * conv_t)[:, None, :] * b_t[:, :, None]
            )
            values_out = jnp.sum(c_t[:, :, None] * carried, axis=1) + skip_gain * conv_t
            result = jnp.where(live_t[:, None], values_out * jax.nn.silu(gate_t), 0.0).astype(
                jnp.bfloat16
            )
            written = lax.dynamic_update_index_in_dim(written, result, position, 1)
            return (carried, written)

        last_state, outputs = lax.fori_loop(
            0, conv_blk.shape[1], advance, (state_blk, outputs_init)
        )
        return (outputs, last_state)

    group_size = 2
    grouped = tuple(
        (
            arr.reshape((item_count // group_size, group_size) + arr.shape[1:])
            for arr in (start_state, step_size, conved, b_rows, c_rows, gate_rows, live_rows)
        )
    )
    outputs, finals = lax.map(block_scan, grouped)
    outputs = outputs.reshape(item_count, steps_count, channels)
    finals = finals.reshape(item_count, states, channels)
    history_len = history.shape[1]
    tail_rows = jax.vmap(lambda row, count: lax.dynamic_slice_in_dim(row, count, history_len, 0))(
        padded, lengths
    )
    return (outputs, finals, tail_rows.astype(jnp.bfloat16))


def on_device(
    resident_state,
    resident_conv,
    migrate_from,
    decode_inputs,
    decode_gates,
    prompt_inputs,
    prompt_gates,
    prompt_length,
    prompt_dest,
    conv_weight,
    conv_bias,
    rank_weight,
    select_weight,
    step_weight,
    step_bias,
    decay_log,
    skip_gain,
):
    params = (
        conv_weight,
        conv_bias,
        rank_weight,
        select_weight,
        step_weight,
        step_bias,
        decay_log,
        skip_gain,
    )
    groups = lax.axis_size("group")
    own_group = lax.axis_index("group")
    local_reqs = resident_state.shape[0]
    states = resident_state.shape[1]
    channels = resident_state.shape[2]
    history_len = resident_conv.shape[1]
    plan = lax.all_gather(migrate_from, "group", axis=0, tiled=True)
    everyone = jnp.arange(plan.shape[0], dtype=jnp.int32)
    moved_slot = plan != everyone
    leaving = jnp.any((plan[:, None] == everyone[None, :]) & moved_slot[:, None], axis=0)
    leave_int = leaving.astype(jnp.int32).reshape(groups, local_reqs)
    leave_rank = (jnp.cumsum(leave_int, axis=1) - leave_int).reshape(-1)
    own_start = own_group * local_reqs
    own_leaving = lax.dynamic_slice_in_dim(leaving, own_start, local_reqs)
    own_rank = lax.dynamic_slice_in_dim(leave_rank, own_start, local_reqs)
    pick = (own_rank[None, :] == jnp.arange(MIG, dtype=jnp.int32)[:, None]) & own_leaving[None, :]
    packed_state = jnp.einsum(
        "kr,rsi->ksi", pick.astype(jnp.float32), resident_state, precision=lax.Precision.HIGHEST
    )
    packed_conv = jnp.einsum(
        "kr,rsi->ksi", pick.astype(jnp.bfloat16), resident_conv, preferred_element_type=jnp.float32
    ).astype(jnp.bfloat16)
    arrived_state = lax.all_gather(
        packed_state.astype(jnp.bfloat16), "group", axis=0, tiled=True
    ).astype(packed_state.dtype)
    arrived_conv = lax.all_gather(packed_conv, "group", axis=0, tiled=True)
    own_sources = lax.dynamic_slice_in_dim(plan, own_start, local_reqs)
    own_moved = own_sources != own_start + jnp.arange(local_reqs, dtype=jnp.int32)
    position = own_sources // local_reqs * MIG + leave_rank[own_sources]
    take = (position[:, None] == jnp.arange(groups * MIG, dtype=jnp.int32)[None, :]) & own_moved[
        :, None
    ]
    taken_state = jnp.einsum(
        "rk,ksi->rsi", take.astype(jnp.float32), arrived_state, precision=lax.Precision.HIGHEST
    )
    taken_conv = jnp.einsum(
        "rk,ksi->rsi", take.astype(jnp.bfloat16), arrived_conv, preferred_element_type=jnp.float32
    ).astype(jnp.bfloat16)
    start_state = jnp.where(own_moved[:, None, None], taken_state, resident_state)
    start_conv = jnp.where(own_moved[:, None, None], taken_conv, resident_conv)
    decode_lengths = jnp.full((local_reqs,), decode_inputs.shape[1], jnp.int32)
    decode_out, final_state, final_conv = mixer(
        decode_inputs, decode_gates, start_conv, start_state, decode_lengths, params
    )
    prompt_count, steps_count = (prompt_inputs.shape[0], prompt_inputs.shape[1])
    destination = prompt_dest[:, 0]
    dest_hot = (destination[:, None] == jnp.arange(groups, dtype=jnp.int32)[None, :]).astype(
        jnp.int32
    )
    rank_in = jnp.sum((jnp.cumsum(dest_hot, axis=0) - dest_hot) * dest_hot, axis=1)
    slot = destination * PAIR + rank_in
    send_pick = slot[None, :] == jnp.arange(groups * PAIR, dtype=jnp.int32)[:, None]
    pick_bf = send_pick.astype(jnp.bfloat16)
    send_rows = jnp.einsum(
        "np,pli->nli", pick_bf, prompt_inputs, preferred_element_type=jnp.float32
    ).astype(jnp.bfloat16)
    send_gates = jnp.einsum(
        "np,pli->nli", pick_bf, prompt_gates, preferred_element_type=jnp.float32
    ).astype(jnp.bfloat16)
    send_len = jnp.dot(send_pick.astype(jnp.float32), prompt_length.astype(jnp.float32)).astype(
        jnp.bfloat16
    )
    got_rows, got_gates, got_len = (
        lax.all_to_all(
            send_rows.reshape(groups, PAIR, steps_count, channels),
            "group",
            split_axis=0,
            concat_axis=0,
            tiled=True,
        ),
        lax.all_to_all(
            send_gates.reshape(groups, PAIR, steps_count, channels),
            "group",
            split_axis=0,
            concat_axis=0,
            tiled=True,
        ),
        lax.all_to_all(
            send_len.reshape(groups, PAIR), "group", split_axis=0, concat_axis=0, tiled=True
        ),
    )
    served = groups * PAIR
    served_len = got_len.reshape(-1).astype(jnp.int32)
    empty_conv = jnp.zeros((served, history_len, channels), jnp.bfloat16)
    empty_state = jnp.zeros((served, states, channels), jnp.float32)
    served_out, prompt_state, prompt_conv = mixer(
        got_rows.reshape(served, steps_count, channels),
        got_gates.reshape(served, steps_count, channels),
        empty_conv,
        empty_state,
        served_len,
        params,
    )
    returned = lax.all_to_all(
        served_out.reshape(groups, PAIR, steps_count, channels),
        "group",
        split_axis=0,
        concat_axis=0,
        tiled=True,
    )
    prefill_out = jnp.einsum(
        "np,nli->pli",
        pick_bf,
        returned.reshape(served, steps_count, channels),
        preferred_element_type=jnp.float32,
    ).astype(jnp.bfloat16)
    return (decode_out, final_state, final_conv, prefill_out, prompt_state, prompt_conv)


def solution(mesh):
    return jax.shard_map(
        on_device,
        mesh=mesh,
        in_specs=(
            P("group", None, "mp"),
            P("group", None, "mp"),
            P("group"),
            P("group", None, "mp"),
            P("group", None, "mp"),
            P("group", None, "mp"),
            P("group", None, "mp"),
            P("group"),
            P("group", None),
            P(None, "mp"),
            P("mp"),
            P("mp", None),
            P("mp", None),
            P(None, "mp"),
            P("mp"),
            P(None, "mp"),
            P("mp"),
        ),
        out_specs=(
            P("group", None, "mp"),
            P("group", None, "mp"),
            P("group", None, "mp"),
            P("group", None, "mp"),
            P("group", None, "mp"),
            P("group", None, "mp"),
        ),
        check_vma=False,
    )
```

profile of v0, /device:TPU:1, one launch (start us, length us, event | category | flops | bytes accessed | tf_op | source)
XLA Modules:
  0.0 588.9 jit_solution(679832897727173695)
XLA Ops:
  8.1 1.3 dynamic-slice
  10.9 12.3 %all-reduce.2 = s32[256]{0:T(256)S(1)} all-reduce(s32[256]{0:T(256)S(1)} %dynamic-update-slice), channel_id=1, replica_groups=mesh['group'=16,'mp'=32] {'group'}, use_global_device_ids=true, to_apply=%add.2 | all-reduce | flops 256 | bytes 2048
  23.9 1.6 convolution_convert_fusion.3
  28.4 1.3 convolution_convert_fusion.1
  29.9 1.3 copy.172
  31.3 9.9 %all-to-all-start.1 = ((bf16[16,2,16,512]{3,1,2,0:T(2,128)(2,1)}), bf16[16,2,16,512]{3,1,2,0:T(2,128)(2,1)S(1)}, u32[]{:S(2)}, u32[]{:S(2)}) async-start(bf16[16,2,16,512]{3,1,2,0:T(2,128)(2,1)} %copy.172), calls=%async_computation.1 | async-start | bytes 1048576 | tf_op jit(solution)/shard_map/all_to_all | solution.py:198
  42.4 27.5 %all_gather.11 = bf16[64,3,512]{2,1,0:T(4,128)(2,1)S(1)} all-gather(bf16[4,3,512]{2,1,0:T(4,128)(2,1)S(1)} %copy.156), channel_id=1, replica_groups=mesh['group'=16,'mp'=32] {'group'}, dimensions={0}, use_global_device_ids=true | all-gather | bytes 208896 | tf_op jit(solution)/shard_map/all_gather | solution.py:160
  71.3 119.7 %psum.29 = f32[64,32]{0,1:T(8,128)S(1)} all-reduce(f32[64,32]{0,1:T(8,128)S(1)} %fusion.69), channel_id=1, replica_groups=mesh['group'=16,'mp'=32] {'mp'}, use_global_device_ids=true, to_apply=%region_4.5 | all-reduce | flops 2048 | bytes 16384 | tf_op jit(solution)/shard_map/psum | solution.py:41
  193.0 1.3 copy.180
  195.2 33.2 %all-to-all-start = ((bf16[16,1,2]{2,1,0:T(2,128)(2,1)}), bf16[16,1,2]{2,1,0:T(2,128)(2,1)S(1)}, u32[]{:S(2)}, u32[]{:S(2)}) async-start(bf16[16,1,2]{2,1,0:T(2,128)(2,1)} %all_to_all.20), calls=%async_computation | async-start | bytes 16384 | tf_op jit(solution)/shard_map/all_to_all | solution.py:212
  230.9 1.4 fusion.70
  233.1 1.4 gather_fusion.1
  235.3 6.4 %all-to-all-start.2 = ((bf16[16,2,16,512]{3,1,2,0:T(2,128)(2,1)}), bf16[16,2,16,512]{3,1,2,0:T(2,128)(2,1)S(1)}, u32[]{:S(2)}, u32[]{:S(2)}) async-start(bf16[16,2,16,512]{3,1,2,0:T(2,128)(2,1)} %copy.180), calls=%async_computation.2 | async-start | bytes 1048576 | tf_op jit(solution)/shard_map/all_to_all | solution.py:205
  243.3 1.6 gather_fusion.2
  244.9 2.6 convolution_select_fusion
  247.8 135.7 %all-reduce.6.cloned.1.call-done = (f32[64,512]{1,0:T(8,128)}, f32[512,512]{1,0:T(8,128)}, f32[512,32]{0,1:T(8,128)}) async-done(((f32[64,512]{1,0:T(8,128)}, f32[512,512]{1,0:T(8,128)}, f32[512,32]{0,1:T(8,128)}), (f32[64,512]{1,0:T(8,128)}, f32[512,512]{1,0:T(8,128)}, f32[512,32]{0,1:T(8,128)})) %all-reduce.6.cloned.1.call-update) | async-done | bytes 1245200 | tf_op jit(solution)/shard_map/psum | solution.py:41
  384.7 1.2 compare_select_fusion.1
  385.9 1.4 fusion.65
  387.4 1.8 reshape_reshape.15
  389.2 1.8 reshape_reshape.14
  391.2 1.6 compare_select_fusion
  393.8 144.2 %while.58 = (s32[]{:T(128)}, bf16[16,2,16,512]{3,1,2,0:T(2,128)(2,1)}, f32[16,2,16,512]{3,2,1,0:T(8,128)}, f32[16,2,16,512]{3,1,2,0:T(2,128)S(1)}, bf16[16,2,16,...) while((s32[]{:T(128)}, ...), condition=%wide.region_19.20_spmd, body=%wide.region_15.19_spmd.sunk | while | flops 126981 | bytes 679696 | solution.py:96
  395.6 6.0 %while.60 = (s32[]{:T(128)}, f32[2,16,512]{2,1,0:T(8,128)S(1)}, bf16[2,16,512]{2,0,1:T(2,128)(2,1)S(1)}, f32[2,16,512]{2,0,1:T(2,128)S(1)}, f32[16,512]{1,0:T(8,...) while((s32[]{:T(128)}, f32[2,16,512]{2,1,0:T(8,128)S(1)}, ...), condition=%wide.region_18.18_spmd.clone, body=%wide.region_16.17_spmd.clone.sunk | while | flops 126979 | bytes 204199 | solution.py:84
  404.6 6.0 %while.60 = (s32[]{:T(128)}, f32[2,16,512]{2,1,0:T(8,128)S(1)}, bf16[2,16,512]{2,0,1:T(2,128)(2,1)S(1)}, f32[2,16,512]{2,0,1:T(2,128)S(1)}, f32[16,512]{1,0:T(8,...) while((s32[]{:T(128)}, f32[2,16,512]{2,1,0:T(8,128)S(1)}, ...), condition=%wide.region_18.18_spmd.clone, body=%wide.region_16.17_spmd.clone.sunk | while | flops 126979 | bytes 204199 | solution.py:84
  413.6 6.0 %while.60 = (s32[]{:T(128)}, f32[2,16,512]{2,1,0:T(8,128)S(1)}, bf16[2,16,512]{2,0,1:T(2,128)(2,1)S(1)}, f32[2,16,512]{2,0,1:T(2,128)S(1)}, f32[16,512]{1,0:T(8,...) while((s32[]{:T(128)}, f32[2,16,512]{2,1,0:T(8,128)S(1)}, ...), condition=%wide.region_18.18_spmd.clone, body=%wide.region_16.17_spmd.clone.sunk | while | flops 126979 | bytes 204199 | solution.py:84
  422.6 6.0 %while.60 = (s32[]{:T(128)}, f32[2,16,512]{2,1,0:T(8,128)S(1)}, bf16[2,16,512]{2,0,1:T(2,128)(2,1)S(1)}, f32[2,16,512]{2,0,1:T(2,128)S(1)}, f32[16,512]{1,0:T(8,...) while((s32[]{:T(128)}, f32[2,16,512]{2,1,0:T(8,128)S(1)}, ...), condition=%wide.region_18.18_spmd.clone, body=%wide.region_16.17_spmd.clone.sunk | while | flops 126979 | bytes 204199 | solution.py:84
  431.6 6.0 %while.60 = (s32[]{:T(128)}, f32[2,16,512]{2,1,0:T(8,128)S(1)}, bf16[2,16,512]{2,0,1:T(2,128)(2,1)S(1)}, f32[2,16,512]{2,0,1:T(2,128)S(1)}, f32[16,512]{1,0:T(8,...) while((s32[]{:T(128)}, f32[2,16,512]{2,1,0:T(8,128)S(1)}, ...), condition=%wide.region_18.18_spmd.clone, body=%wide.region_16.17_spmd.clone.sunk | while | flops 126979 | bytes 204199 | solution.py:84
  440.6 6.0 %while.60 = (s32[]{:T(128)}, f32[2,16,512]{2,1,0:T(8,128)S(1)}, bf16[2,16,512]{2,0,1:T(2,128)(2,1)S(1)}, f32[2,16,512]{2,0,1:T(2,128)S(1)}, f32[16,512]{1,0:T(8,...) while((s32[]{:T(128)}, f32[2,16,512]{2,1,0:T(8,128)S(1)}, ...), condition=%wide.region_18.18_spmd.clone, body=%wide.region_16.17_spmd.clone.sunk | while | flops 126979 | bytes 204199 | solution.py:84
  449.6 6.0 %while.60 = (s32[]{:T(128)}, f32[2,16,512]{2,1,0:T(8,128)S(1)}, bf16[2,16,512]{2,0,1:T(2,128)(2,1)S(1)}, f32[2,16,512]{2,0,1:T(2,128)S(1)}, f32[16,512]{1,0:T(8,...) while((s32[]{:T(128)}, f32[2,16,512]{2,1,0:T(8,128)S(1)}, ...), condition=%wide.region_18.18_spmd.clone, body=%wide.region_16.17_spmd.clone.sunk | while | flops 126979 | bytes 204199 | solution.py:84
  458.6 6.0 %while.60 = (s32[]{:T(128)}, f32[2,16,512]{2,1,0:T(8,128)S(1)}, bf16[2,16,512]{2,0,1:T(2,128)(2,1)S(1)}, f32[2,16,512]{2,0,1:T(2,128)S(1)}, f32[16,512]{1,0:T(8,...) while((s32[]{:T(128)}, f32[2,16,512]{2,1,0:T(8,128)S(1)}, ...), condition=%wide.region_18.18_spmd.clone, body=%wide.region_16.17_spmd.clone.sunk | while | flops 126979 | bytes 204199 | solution.py:84
  467.6 6.0 %while.60 = (s32[]{:T(128)}, f32[2,16,512]{2,1,0:T(8,128)S(1)}, bf16[2,16,512]{2,0,1:T(2,128)(2,1)S(1)}, f32[2,16,512]{2,0,1:T(2,128)S(1)}, f32[16,512]{1,0:T(8,...) while((s32[]{:T(128)}, f32[2,16,512]{2,1,0:T(8,128)S(1)}, ...), condition=%wide.region_18.18_spmd.clone, body=%wide.region_16.17_spmd.clone.sunk | while | flops 126979 | bytes 204199 | solution.py:84
  476.6 6.0 %while.60 = (s32[]{:T(128)}, f32[2,16,512]{2,1,0:T(8,128)S(1)}, bf16[2,16,512]{2,0,1:T(2,128)(2,1)S(1)}, f32[2,16,512]{2,0,1:T(2,128)S(1)}, f32[16,512]{1,0:T(8,...) while((s32[]{:T(128)}, f32[2,16,512]{2,1,0:T(8,128)S(1)}, ...), condition=%wide.region_18.18_spmd.clone, body=%wide.region_16.17_spmd.clone.sunk | while | flops 126979 | bytes 204199 | solution.py:84
  485.7 6.0 %while.60 = (s32[]{:T(128)}, f32[2,16,512]{2,1,0:T(8,128)S(1)}, bf16[2,16,512]{2,0,1:T(2,128)(2,1)S(1)}, f32[2,16,512]{2,0,1:T(2,128)S(1)}, f32[16,512]{1,0:T(8,...) while((s32[]{:T(128)}, f32[2,16,512]{2,1,0:T(8,128)S(1)}, ...), condition=%wide.region_18.18_spmd.clone, body=%wide.region_16.17_spmd.clone.sunk | while | flops 126979 | bytes 204199 | solution.py:84
  494.7 6.0 %while.60 = (s32[]{:T(128)}, f32[2,16,512]{2,1,0:T(8,128)S(1)}, bf16[2,16,512]{2,0,1:T(2,128)(2,1)S(1)}, f32[2,16,512]{2,0,1:T(2,128)S(1)}, f32[16,512]{1,0:T(8,...) while((s32[]{:T(128)}, f32[2,16,512]{2,1,0:T(8,128)S(1)}, ...), condition=%wide.region_18.18_spmd.clone, body=%wide.region_16.17_spmd.clone.sunk | while | flops 126979 | bytes 204199 | solution.py:84
  503.7 6.0 %while.60 = (s32[]{:T(128)}, f32[2,16,512]{2,1,0:T(8,128)S(1)}, bf16[2,16,512]{2,0,1:T(2,128)(2,1)S(1)}, f32[2,16,512]{2,0,1:T(2,128)S(1)}, f32[16,512]{1,0:T(8,...) while((s32[]{:T(128)}, f32[2,16,512]{2,1,0:T(8,128)S(1)}, ...), condition=%wide.region_18.18_spmd.clone, body=%wide.region_16.17_spmd.clone.sunk | while | flops 126979 | bytes 204199 | solution.py:84
  512.7 6.0 %while.60 = (s32[]{:T(128)}, f32[2,16,512]{2,1,0:T(8,128)S(1)}, bf16[2,16,512]{2,0,1:T(2,128)(2,1)S(1)}, f32[2,16,512]{2,0,1:T(2,128)S(1)}, f32[16,512]{1,0:T(8,...) while((s32[]{:T(128)}, f32[2,16,512]{2,1,0:T(8,128)S(1)}, ...), condition=%wide.region_18.18_spmd.clone, body=%wide.region_16.17_spmd.clone.sunk | while | flops 126979 | bytes 204199 | solution.py:84
  521.7 6.0 %while.60 = (s32[]{:T(128)}, f32[2,16,512]{2,1,0:T(8,128)S(1)}, bf16[2,16,512]{2,0,1:T(2,128)(2,1)S(1)}, f32[2,16,512]{2,0,1:T(2,128)S(1)}, f32[16,512]{1,0:T(8,...) while((s32[]{:T(128)}, f32[2,16,512]{2,1,0:T(8,128)S(1)}, ...), condition=%wide.region_18.18_spmd.clone, body=%wide.region_16.17_spmd.clone.sunk | while | flops 126979 | bytes 204199 | solution.py:84
  530.7 6.0 %while.60 = (s32[]{:T(128)}, f32[2,16,512]{2,1,0:T(8,128)S(1)}, bf16[2,16,512]{2,0,1:T(2,128)(2,1)S(1)}, f32[2,16,512]{2,0,1:T(2,128)S(1)}, f32[16,512]{1,0:T(8,...) while((s32[]{:T(128)}, f32[2,16,512]{2,1,0:T(8,128)S(1)}, ...), condition=%wide.region_18.18_spmd.clone, body=%wide.region_16.17_spmd.clone.sunk | while | flops 126979 | bytes 204199 | solution.py:84
  538.0 12.3 %all-to-all-start.3 = ((bf16[16,2,16,512]{3,1,2,0:T(2,128)(2,1)}), bf16[16,2,16,512]{3,1,2,0:T(2,128)(2,1)S(1)}, u32[]{:S(2)}, u32[]{:S(2)}) async-start(bf16[16,2,16,512]{3,1,2,0:T(2,128)(2,1)} %get-tuple-element.1445), calls=%async_computation.3 | async-start | bytes 1048576 | tf_op jit(solution)/shard_map/all_to_all | solution.py:228
  550.5 29.3 %while.56 = (s32[]{:T(128)}, bf16[8,2,4,512]{3,2,1,0:T(4,128)(2,1)S(1)}, f32[8,2,16,512]{3,2,1,0:T(8,128)}, f32[8,2,16,512]{3,2,1,0:T(8,128)S(1)}, f32[8,2,4,512...) while((s32[]{:T(128)}, ...), condition=%wide.region_9.10_spmd, body=%wide.region_5.9_spmd.sunk | while | flops 110596 | bytes 566978 | solution.py:96
  551.9 1.6 while.59
  555.6 1.6 while.59
  559.3 1.6 while.59
  562.9 1.6 while.59
  566.6 1.6 while.59
  570.3 1.6 while.59
  573.9 1.6 while.59
  577.6 1.6 while.59
  (2103 shorter events, 190.2 us)
Async XLA Ops:
  8.0 186.3 %copy-start = (bf16[512,512]{1,0:T(8,128)(2,1)S(1)}, bf16[512,512]{1,0:T(8,128)(2,1)}, u32[]{:S(2)}) copy-start(bf16[512,512]{1,0:T(8,128)(2,1)} %param.36) | copy-start | bytes 1572868
  8.0 236.8 %all-gather.2.cloned.1.call-start = ((), (), s32[]{:S(2)}) async-start(), calls=%async_computation.4 | async-start | bytes 1114112 | tf_op jit(solution)/shard_map/all_gather | solution.py:157
  31.3 10.9 %copy-start.12 = (f32[4,512]{1,0:T(4,128)S(1)}, f32[4,512]{1,0:T(4,128)}, u32[]{:S(2)}) copy-start(f32[4,512]{1,0:T(4,128)} %param.34) | copy-start | bytes 24580
  31.3 10.9 %copy-start.5 = (bf16[16,3,512]{2,0,1:T(8,128)(2,1)S(1)}, bf16[16,3,512]{2,0,1:T(8,128)(2,1)}, u32[]{:S(2)}) copy-start(bf16[16,3,512]{2,0,1:T(8,128)(2,1)} %param.26) | copy-start | bytes 147460
  31.3 11.1 %copy-start.9 = (bf16[16,4,512]{2,1,0:T(4,128)(2,1)S(1)}, bf16[16,4,512]{2,1,0:T(4,128)(2,1)}, u32[]{:S(2)}) copy-start(bf16[16,4,512]{2,1,0:T(4,128)(2,1)} %param.28) | copy-start | bytes 196612
  31.3 38.8 %copy-start.11 = (f32[512]{0:T(512)S(1)}, f32[512]{0:T(512)}, u32[]{:S(2)}) copy-start(f32[512]{0:T(512)} %param.35) | copy-start | bytes 6148
  31.3 163.9 %all-to-all-start.1 = ((bf16[16,2,16,512]{3,1,2,0:T(2,128)(2,1)}), bf16[16,2,16,512]{3,1,2,0:T(2,128)(2,1)S(1)}, u32[]{:S(2)}, u32[]{:S(2)}) async-start(bf16[16,2,16,512]{3,1,2,0:T(2,128)(2,1)} %copy.172), calls=%async_computation.1 | async-start | bytes 1048576 | tf_op jit(solution)/shard_map/all_to_all | solution.py:198
  41.2 28.9 %copy-start.17 = (s32[8]{0:T(128)S(1)}, s32[8]{0:T(128)}, u32[]{:S(2)}) copy-start(s32[8]{0:T(128)} %param.32) | copy-start | bytes 100
  41.4 29.8 %copy-start.7 = (bf16[512,32]{0,1:T(8,128)(2,1)S(1)}, bf16[512,32]{0,1:T(8,128)(2,1)}, u32[]{:S(2)}) copy-start(bf16[512,32]{0,1:T(8,128)(2,1)} %param.37) | copy-start | bytes 98308
  42.1 150.3 %copy-start.8 = (bf16[8,16,512]{2,1,0:T(8,128)(2,1)S(1)}, bf16[8,16,512]{2,1,0:T(8,128)(2,1)}, u32[]{:S(2)}) copy-start(bf16[8,16,512]{2,1,0:T(8,128)(2,1)} %param.31) | copy-start | bytes 393220
  195.2 40.2 %all-to-all-start = ((bf16[16,1,2]{2,1,0:T(2,128)(2,1)}), bf16[16,1,2]{2,1,0:T(2,128)(2,1)S(1)}, u32[]{:S(2)}, u32[]{:S(2)}) async-start(bf16[16,1,2]{2,1,0:T(2,128)(2,1)} %all_to_all.20), calls=%async_computation | async-start | bytes 16384 | tf_op jit(solution)/shard_map/all_to_all | solution.py:212
  228.4 155.2 %all-reduce.6.cloned.1.call-start = ((), (), s32[]{:S(2)}) async-start(), calls=%async_computation.5 | async-start | bytes 2490368 | tf_op jit(solution)/shard_map/psum | solution.py:41
  232.4 0.8 copy-start.10
  232.4 0.8 copy-start.6
  235.3 158.4 %all-to-all-start.2 = ((bf16[16,2,16,512]{3,1,2,0:T(2,128)(2,1)}), bf16[16,2,16,512]{3,1,2,0:T(2,128)(2,1)S(1)}, u32[]{:S(2)}, u32[]{:S(2)}) async-start(bf16[16,2,16,512]{3,1,2,0:T(2,128)(2,1)} %copy.180), calls=%async_computation.2 | async-start | bytes 1048576 | tf_op jit(solution)/shard_map/all_to_all | solution.py:205
  243.2 1.7 copy-start.2
  247.5 137.2 %copy-start.4 = (bf16[512,512]{1,0:T(8,128)(2,1)S(1)}, bf16[512,512]{1,0:T(8,128)(2,1)}, u32[]{:S(2)}) copy-start(bf16[512,512]{1,0:T(8,128)(2,1)} %param.38) | copy-start | bytes 1572868
  247.5 137.2 %copy-start.13 = (f32[512]{0:T(512)S(1)}, f32[512]{0:T(512)}, u32[]{:S(2)}) copy-start(f32[512]{0:T(512)} %param.39) | copy-start | bytes 6148
  383.6 7.5 %copy-start.3 = (f32[512,512]{1,0:T(8,128)S(1)}, f32[512,512]{1,0:T(8,128)}, u32[]{:S(2)}) copy-start(f32[512,512]{1,0:T(8,128)} %get-tuple-element.883) | copy-start | bytes 3145732
  392.8 0.9 copy-start.1
  538.0 12.3 %copy-start.14 = (pred[4]{0:T(512)(128)(4,1)S(1)}, pred[4]{0:T(512)(128)(4,1)}, u32[]{:S(2)}) copy-start(pred[4]{0:T(512)(128)(4,1)} %iota_compare_fusion.8) | copy-start | bytes 16
  538.0 12.5 %copy-start.15 = (bf16[8,2,4,512]{3,2,1,0:T(4,128)(2,1)S(1)}, bf16[8,2,4,512]{3,2,1,0:T(4,128)(2,1)}, u32[]{:S(2)}) copy-start(bf16[8,2,4,512]{3,2,1,0:T(4,128)(2,1)} %custom-call.9) | copy-start | bytes 196612
  538.0 41.8 %all-to-all-start.3 = ((bf16[16,2,16,512]{3,1,2,0:T(2,128)(2,1)}), bf16[16,2,16,512]{3,1,2,0:T(2,128)(2,1)S(1)}, u32[]{:S(2)}, u32[]{:S(2)}) async-start(bf16[16,2,16,512]{3,1,2,0:T(2,128)(2,1)} %get-tuple-element.1445), calls=%async_computation.3 | async-start | bytes 1048576 | tf_op jit(solution)/shard_map/all_to_all | solution.py:228
  579.8 0.7 copy-start.16
Sparse Core Ops, SparseCore 0:
  26.3 48.0 all-gather.1
Sparse Core Ops, SparseCore 1:
  233.2 150.3 all-reduce.5
where the time goes:
time: 593 us; the launch traced here: 589 us
  blocking collectives  159 us (27%)
  local copies, waits for them, and re-layouts  140 us (24%)
  waiting for transfers between devices  137 us (23%)
  starting transfers between devices  62 us (10%)
  other arithmetic  58.4 us (10%)
  between operations  16.6 us (3%)
  matrix products  12.8 us (2%)
    psum x1, waiting for transfers between devices, mixer(): low_rank, selects = lax.psum((low_part, select_part), 'mp')  136 us
    psum x1, blocking collectives, mixer(): low_rank, selects = lax.psum((low_part, select_part), 'mp')  120 us
    dynamic_slice x576, local copies, waits for them, and re-layouts, advance(): live_t = lax.dynamic_index_in_dim(live_blk, position, 1, keepdims=False)  53.1 us
    all_to_all x1, starting transfers between devices, on_device(): lax.all_to_all(send_len.reshape(groups, PAIR), 'group', split_axis=0, con...  33.2 us
    reduce_sum x288, other arithmetic, advance(): values_out = jnp.sum(c_t[:, :, None] * carried, axis=1) + skip_gain * conv_t  27.6 us
    all_gather x1, blocking collectives, on_device(): arrived_conv = lax.all_gather(packed_conv, 'group', axis=0, tiled=True)  27.5 us
    dynamic_update_slice x48, local copies, waits for them, and re-layouts, mixer(): outputs, finals = lax.map(block_scan, grouped)  25.5 us
    dynamic_update_slice x288, other arithmetic, advance(): written = lax.dynamic_update_index_in_dim(written, result, position, 1)  22.4 us
  transfers between devices with their start and end apart: 6, of which 2 were waited for; matrix products, arithmetic and copies ran while one was open for 11% of the time, Pallas kernels for 0%

commit v1 on v0

v1 whole, which is shorter than its diff:
```python
import jax
import jax.numpy as jnp
from jax import lax
from jax.experimental import pallas as pl
from jax.experimental.pallas import tpu as pltpu
from jax.sharding import PartitionSpec as P

MIG = 4
PAIR = 2
EPS = 1e-06
LANES = 128
ROWS0 = 24
LOG2E = 1.4426950408889634

F32 = jnp.float32
BF16 = jnp.bfloat16
VMEM = pl.BlockSpec(memory_space=pltpu.VMEM)
SMEM = pl.BlockSpec(memory_space=pltpu.SMEM)
PARAMS = pltpu.CompilerParams(vmem_limit_bytes=40 * 1024 * 1024)


def silu(x):
    return x / (1.0 + jnp.exp(-x))


def softplus(x):
    return jnp.maximum(x, 0.0) + jnp.log1p(jnp.exp(-jnp.abs(x)))


def iota(shape, dim):
    return lax.broadcasted_iota(jnp.int32, shape, dim)


def from_scalars(ref, count, shape):
    rows = iota(shape, 0)
    out = jnp.zeros(shape, jnp.int32)
    for i in range(count):
        out = jnp.where(rows == i, ref[i], out)
    return out


def slots_of(dest_ref, count):
    dests = [dest_ref[i, 0] for i in range(count)]
    ranks = []
    for i in range(count):
        rank = jnp.int32(0)
        for j in range(i):
            rank = rank + (dests[j] == dests[i]).astype(jnp.int32)
        ranks.append(rank)
    return dests, ranks


def pack_kernel(mig_ref, dest_ref, len_ref, conv_ref, state_ref, u_ref, pay_ref, state_out_ref, scr):
    groups = pay_ref.shape[0]
    reqs = conv_ref.shape[0]
    prompts, steps, channels = u_ref.shape
    own = lax.axis_index("group")
    count = jnp.int32(0)
    picks = [jnp.int32(0) for _ in range(MIG)]
    for r in range(reqs):
        moved = mig_ref[r] != own * reqs + r
        for k in range(MIG):
            picks[k] = jnp.where(moved & (count == k), r, picks[k])
        count = count + moved.astype(jnp.int32)
    base = scr.at[groups]
    base[...] = jnp.zeros(base.shape, F32)
    lane = iota((1, channels), 1) - own * ROWS0
    ids = jnp.zeros((1, channels), jnp.int32)
    code = jnp.zeros((1, channels), jnp.int32)
    for k in range(MIG):
        state_out_ref[k] = state_ref[picks[k]].astype(BF16)
        hist = conv_ref[picks[k]].astype(F32)
        for j in range(3):
            base[4 * j + k : 4 * j + k + 1, :] = hist[j : j + 1, :]
            here = lane == 4 * j + k
            ids = jnp.where(here, own * reqs + picks[k], ids)
            code = jnp.where(here, j + 1, code)
    base[12:13, :] = ids.astype(F32)
    base[13:14, :] = code.astype(F32)
    for d in range(groups):
        scr[d] = base[...]
    dests, ranks = slots_of(dest_ref, prompts)
    rows = iota((steps, channels), 0)
    for i in range(prompts):
        u = u_ref[i].astype(F32)
        tails = [
            jnp.sum(jnp.where(rows == len_ref[i] - 3 + j, u, 0.0), axis=0, keepdims=True)
            for j in range(3)
        ]
        for q in range(PAIR):

            @pl.when(ranks[i] == q)
            def _():
                for j in range(3):
                    at = 16 + 3 * q + j
                    scr[dests[i], at : at + 1, :] = tails[j]

    for d in range(groups):
        pay_ref[d] = scr[d].astype(BF16)


def put_lanes(ref, start, value):
    for l in range(ref.shape[0]):
        ref[l, start : start + value.shape[0], :] = value[:, l * LANES : (l + 1) * LANES]


def project(x, rank_ref, select_ref):
    low = jnp.dot(x, rank_ref[...], preferred_element_type=F32)
    sel = jnp.dot(x, select_ref[...], preferred_element_type=F32)
    return low, sel


def put_partials(pay_ref, first, low, sel):
    rank = low.shape[1]
    wide = jnp.concatenate(
        [sel, jnp.zeros((sel.shape[0], pay_ref.shape[2] - rank - sel.shape[1]), F32)], axis=1
    )
    for j in range(low.shape[0] // 8):
        pay_ref[first + j, :, :rank] = low[8 * j : 8 * j + 8].astype(BF16)
        pay_ref[first + j, :, rank:] = wide[8 * j : 8 * j + 8].astype(BF16)


def prompt_kernel(u_ref, cw_ref, cb_ref, rank_ref, select_ref, pay_ref, x_ref, scr, x_scr):
    prompts, steps, channels = u_ref.shape
    for i in range(prompts):
        put_lanes(scr, i * steps, u_ref[i].astype(F32))
    for l in range(channels // LANES):
        cols = slice(l * LANES, (l + 1) * LANES)
        taps = [cw_ref[k : k + 1, cols] for k in range(4)]
        bias = cb_ref[:, cols]
        window = [jnp.zeros((prompts, LANES), F32) for _ in range(3)]
        for t in range(steps):
            window.append(scr[l, pl.ds(t, prompts, stride=steps), :])
            acc = bias
            for k in range(4):
                acc = acc + taps[k] * window[t + k]
            x_scr[t * prompts : (t + 1) * prompts, cols] = silu(acc)
    x = x_scr[...].astype(BF16)
    x_ref[...] = x
    low, sel = project(x, rank_ref, select_ref)
    put_partials(pay_ref, 0, low, sel)


def decode_kernel(
    mig_ref, got_ref, conv_ref, u_ref, cw_ref, cb_ref, rank_ref, select_ref, prompt_pay_ref,
    pay_ref, x_ref, pos_ref, final_conv_ref, prompt_conv_ref, cand, scr, x_scr,
):
    groups = got_ref.shape[0]
    reqs, steps, channels = u_ref.shape
    own = lax.axis_index("group")
    ids = jnp.zeros((8, channels), F32)
    for s in range(groups):
        block = got_ref[s].astype(F32)
        cand[s * ROWS0 : (s + 1) * ROWS0, :] = block
        ids = ids + block[8:16]
        for q in range(PAIR):
            prompt_conv_ref[s * PAIR + q] = block[16 + 3 * q : 19 + 3 * q].astype(BF16)
    table = groups * ROWS0
    cand[table:, :] = jnp.zeros((channels - table, channels), F32)
    for r in range(reqs):
        cand[table + 8 * r : table + 8 * r + 3, :] = conv_ref[r].astype(F32)
        u = u_ref[r].astype(F32)
        put_lanes(scr, 8 * r, u)
        final_conv_ref[r] = u[1:4].astype(BF16)
    shape = (reqs, channels)
    lane = iota(shape, 1)
    row = iota(shape, 0)
    wanted = from_scalars(mig_ref, reqs, shape)
    moved = wanted != own * reqs + row
    codes = jnp.broadcast_to(ids[5:6], shape)
    found = moved & (jnp.broadcast_to(ids[4:5], shape) == wanted.astype(F32))
    pool = cand[...].astype(BF16)
    hist = []
    for j in range(3):
        hit = (found & (codes == j + 1.0)) | ((~moved) & (lane == table + 8 * row + j))
        hist.append(jnp.dot(hit.astype(BF16), pool, preferred_element_type=F32))
    first = jnp.where(found & (codes == 1.0), lane, 0)
    at = jnp.sum(first.astype(F32), axis=1, keepdims=True).astype(jnp.int32)
    pos_ref[...] = jnp.broadcast_to(jnp.where(moved[:, :1], at, -1), pos_ref.shape)
    for l in range(channels // LANES):
        cols = slice(l * LANES, (l + 1) * LANES)
        taps = [cw_ref[k : k + 1, cols] for k in range(4)]
        bias = cb_ref[:, cols]
        window = [hist[j][:, cols] for j in range(3)]
        for t in range(steps):
            window.append(scr[l, pl.ds(t, reqs, stride=8), :])
            acc = bias
            for k in range(4):
                acc = acc + taps[k] * window[t + k]
            x_scr[t * reqs : (t + 1) * reqs, cols] = silu(acc)
    x = x_scr[...].astype(BF16)
    x_ref[...] = x
    low, sel = project(x, rank_ref, select_ref)
    first_block = prompt_pay_ref.shape[0]
    pay_ref[:first_block] = prompt_pay_ref[...]
    put_partials(pay_ref, first_block, low, sel)
    used = first_block + x.shape[0] // 8
    pay_ref[used:] = jnp.zeros((pay_ref.shape[0] - used,) + pay_ref.shape[1:], BF16)


def norm_kernel(part_ref, out_ref):
    blocks, rows, width = part_ref.shape
    total = part_ref[0].astype(F32)
    for j in range(1, blocks):
        total = total + part_ref[j].astype(F32)
    rank = (width // LANES - 1) * LANES
    low = total[:, :rank]
    normed = low * lax.rsqrt(jnp.mean(low * low, axis=-1, keepdims=True) + EPS)
    for j in range(blocks):
        out_ref[j, :, :rank] = normed.astype(BF16)
        out_ref[j, :, rank:] = total[:, rank:].astype(BF16)


def steps_of(rows_ref, step_w_ref, step_b_ref, low_scr, step_scr):
    for j in range(low_scr.shape[0] // 8):
        low_scr[8 * j : 8 * j + 8, :] = rows_ref[j].astype(F32)
    rank = step_w_ref.shape[0]
    normed = low_scr[:, :rank].astype(BF16)
    step_scr[...] = softplus(
        jnp.dot(normed, step_w_ref[...], preferred_element_type=F32) + step_b_ref[...]
    )
    return rank


def scan(
    t, items, live, x, gate_scr, gate_stride, low_scr, step_scr, rank, decay_scr, skip_ref, h_scr,
    y_scr, y_stride,
):
    states = decay_scr.shape[1] // 8
    start = pl.multiple_of(t * items, 8)
    for g in range(items // 8):
        rows = pl.ds(start + 8 * g, 8)
        alive = None if live is None else live[8 * g : 8 * g + 8]
        sel = low_scr[rows, rank:]
        lanes = range(h_scr.shape[0])
        step, drive, conved, y = [], [], [], []
        for l in lanes:
            cols = slice(l * LANES, (l + 1) * LANES)
            step_l = step_scr[rows, cols]
            if alive is not None:
                step_l = jnp.where(alive, step_l, 0.0)
            conved_l = x[rows, cols]
            step.append(step_l)
            conved.append(conved_l)
            drive.append(step_l * conved_l)
            y.append(skip_ref[:, cols] * conved_l)
        for n in range(states):
            b = jnp.broadcast_to(sel[:, n : n + 1], (8, LANES))
            c = jnp.broadcast_to(sel[:, states + n : states + n + 1], (8, LANES))
            at = slice(n * items + 8 * g, n * items + 8 * g + 8)
            for l in lanes:
                keep = jnp.exp2(step[l] * decay_scr[l, 8 * n : 8 * n + 8, :])
                h = keep * h_scr[l, at, :] + drive[l] * b
                h_scr[l, at, :] = h
                y[l] = y[l] + c * h
        for l in lanes:
            gate = gate_scr[l, pl.ds(8 * g * gate_stride + t, 8, stride=gate_stride), :]
            out = y[l] * silu(gate)
            if alive is not None:
                out = jnp.where(alive, out, 0.0)
            y_scr[l, pl.ds(8 * g * y_stride + t, 8, stride=y_stride), :] = out


def put_decay(decay_ref, decay_scr):
    decay = jnp.exp(decay_ref[...]) * -LOG2E
    for n in range(decay.shape[0]):
        put_lanes(decay_scr, 8 * n, jnp.broadcast_to(decay[n : n + 1], (8, decay.shape[1])))


def prefill_kernel(
    len_ref, dest_ref, rows_ref, x_ref, gate_ref, step_w_ref, step_b_ref, decay_ref, skip_ref,
    out_ref, pay_ref, low_scr, step_scr, x_scr, gate_scr, decay_scr, h_scr, y_scr,
):
    prompts, steps, channels = gate_ref.shape
    states = decay_ref.shape[0]
    rank = steps_of(rows_ref, step_w_ref, step_b_ref, low_scr, step_scr)
    x_scr[...] = x_ref[...].astype(F32)
    for i in range(prompts):
        put_lanes(gate_scr, i * steps, gate_ref[i].astype(F32))
    put_decay(decay_ref, decay_scr)
    h_scr[...] = jnp.zeros(h_scr.shape, F32)
    lengths = from_scalars(len_ref, prompts, (prompts, LANES))

    @pl.loop(0, steps)
    def _(t):
        scan(
            t, prompts, t < lengths, x_scr, gate_scr, steps, low_scr, step_scr, rank, decay_scr,
            skip_ref, h_scr, y_scr, steps,
        )

    dests, ranks = slots_of(dest_ref, prompts)
    pay_ref[...] = jnp.zeros(pay_ref.shape, BF16)
    for i in range(prompts):
        for l in range(channels // LANES):
            cols = slice(l * LANES, (l + 1) * LANES)
            out_ref[i, :, cols] = y_scr[l, i * steps : (i + 1) * steps, :].astype(BF16)
            final = h_scr[l, pl.ds(i, states, stride=prompts), :]
            pay_ref[dests[i] * PAIR + ranks[i], :, cols] = final.astype(BF16)


def decode_scan_kernel(
    pos_ref, rows_ref, x_ref, gate_ref, state_ref, moved_ref, step_w_ref, step_b_ref, decay_ref,
    skip_ref, out_ref, final_ref, low_scr, step_scr, x_scr, gate_scr, decay_scr, h_scr, y_scr,
):
    reqs, steps, channels = gate_ref.shape
    states = decay_ref.shape[0]
    rank = steps_of(rows_ref, step_w_ref, step_b_ref, low_scr, step_scr)
    x_scr[...] = x_ref[...].astype(F32)
    put_decay(decay_ref, decay_scr)
    for r in range(reqs):
        put_lanes(gate_scr, 8 * r, gate_ref[r].astype(F32))
        code = pos_ref[r, 0]
        for l in range(channels // LANES):
            cols = slice(l * LANES, (l + 1) * LANES)

            @pl.when(code < 0)
            def _():
                h_scr[l, pl.ds(r, states, stride=reqs), :] = state_ref[r, :, cols]

            @pl.when(code >= 0)
            def _():
                source = lax.div(code, ROWS0)
                at = source * MIG + (code - source * ROWS0)
                h_scr[l, pl.ds(r, states, stride=reqs), :] = moved_ref[at, :, cols].astype(F32)

    @pl.loop(0, steps)
    def _(t):
        scan(
            t, reqs, None, x_scr, gate_scr, 8, low_scr, step_scr, rank, decay_scr, skip_ref,
            h_scr, y_scr, 8,
        )

    for r in range(reqs):
        for l in range(channels // LANES):
            cols = slice(l * LANES, (l + 1) * LANES)
            out_ref[r, :, cols] = y_scr[l, 8 * r : 8 * r + steps, :].astype(BF16)
            final_ref[r, :, cols] = h_scr[l, pl.ds(r, states, stride=reqs), :]


def exchange(value, axis):
    return lax.all_to_all(value, axis, split_axis=0, concat_axis=0, tiled=True)


def on_device(
    resident_state,
    resident_conv,
    migrate_from,
    decode_inputs,
    decode_gates,
    prompt_inputs,
    prompt_gates,
    prompt_length,
    prompt_dest,
    conv_weight,
    conv_bias,
    rank_weight,
    select_weight,
    step_weight,
    step_bias,
    decay_log,
    skip_gain,
):
    groups = lax.axis_size("group")
    peers = lax.axis_size("mp")
    reqs, states, channels = resident_state.shape
    prompts, steps, _ = prompt_inputs.shape
    decode_steps = decode_inputs.shape[1]
    tiles = channels // LANES
    rank = rank_weight.shape[1]
    width = rank + LANES
    prompt_rows = prompts * steps
    decode_rows = reqs * decode_steps
    bias_row = conv_bias.reshape(1, channels)
    step_bias_row = step_bias.reshape(1, channels)
    skip_row = skip_gain.reshape(1, channels)

    def struct(shape, dtype):
        return jax.ShapeDtypeStruct(shape, dtype)

    def scratch(shape):
        return pltpu.VMEM(shape, F32)

    send_conv, send_state = pl.pallas_call(
        pack_kernel,
        out_shape=(
            struct((groups, ROWS0, channels), BF16),
            struct((MIG, states, channels), BF16),
        ),
        in_specs=[SMEM] * 3 + [VMEM] * 3,
        out_specs=(VMEM, VMEM),
        scratch_shapes=[scratch((groups + 1, ROWS0, channels))],
        compiler_params=PARAMS,
        name="pack",
    )(migrate_from, prompt_dest, prompt_length, resident_conv, resident_state, prompt_inputs)
    got_conv = exchange(send_conv, "group")
    got_state = lax.all_gather(send_state, "group", axis=0, tiled=True)

    prompt_pay, prompt_x = pl.pallas_call(
        prompt_kernel,
        out_shape=(
            struct((prompt_rows // 8, 8, width), BF16),
            struct((prompt_rows, channels), BF16),
        ),
        in_specs=[VMEM] * 5,
        out_specs=(VMEM, VMEM),
        scratch_shapes=[scratch((tiles, prompt_rows, LANES)), scratch((prompt_rows, channels))],
        compiler_params=PARAMS,
        name="prompt_features",
    )(prompt_inputs, conv_weight, bias_row, rank_weight, select_weight)

    pay, decode_x, position, final_conv, prompt_conv = pl.pallas_call(
        decode_kernel,
        out_shape=(
            struct((peers, 8, width), BF16),
            struct((decode_rows, channels), BF16),
            struct((reqs, LANES), jnp.int32),
            struct(resident_conv.shape, BF16),
            struct((groups * PAIR, 3, channels), BF16),
        ),
        in_specs=[SMEM] + [VMEM] * 8,
        out_specs=(VMEM,) * 5,
        scratch_shapes=[
            scratch((channels, channels)),
            scratch((tiles, reqs * 8, LANES)),
            scratch((decode_rows, channels)),
        ],
        compiler_params=PARAMS,
        name="decode_features",
    )(
        migrate_from, got_conv, resident_conv, decode_inputs, conv_weight, bias_row, rank_weight,
        select_weight, prompt_pay,
    )

    parts = exchange(pay, "mp")
    shares = pl.pallas_call(
        norm_kernel,
        out_shape=struct((peers, 8, width), BF16),
        in_specs=[VMEM],
        out_specs=VMEM,
        compiler_params=PARAMS,
        name="sum_norm",
    )(parts)
    rows = exchange(shares, "mp")

    prompt_blocks = prompt_rows // 8
    decode_blocks = decode_rows // 8
    prefill_out, send_final = pl.pallas_call(
        prefill_kernel,
        out_shape=(
            struct(prompt_inputs.shape, BF16),
            struct((groups * PAIR, states, channels), BF16),
        ),
        grid=(1,),
        in_specs=[SMEM] * 2
        + [pl.BlockSpec((prompt_blocks, 8, width), lambda i: (0, 0, 0))]
        + [VMEM] * 6,
        out_specs=(VMEM, VMEM),
        scratch_shapes=[
            scratch((prompt_rows, width)),
            scratch((prompt_rows, channels)),
            scratch((prompt_rows, channels)),
            scratch((tiles, prompt_rows, LANES)),
            scratch((tiles, 8 * states, LANES)),
            scratch((tiles, prompts * states, LANES)),
            scratch((tiles, prompt_rows, LANES)),
        ],
        compiler_params=PARAMS,
        name="prefill_scan",
    )(
        prompt_length, prompt_dest, rows, prompt_x, prompt_gates, step_weight, step_bias_row,
        decay_log, skip_row,
    )
    got_final = exchange(send_final.reshape(groups, PAIR, states, channels), "group")

    first = prompt_blocks // decode_blocks
    decode_out, final_state = pl.pallas_call(
        decode_scan_kernel,
        out_shape=(struct(decode_inputs.shape, BF16), struct(resident_state.shape, F32)),
        grid=(1,),
        in_specs=[SMEM]
        + [pl.BlockSpec((decode_blocks, 8, width), lambda i: (first, 0, 0))]
        + [VMEM] * 8,
        out_specs=(VMEM, VMEM),
        scratch_shapes=[
            scratch((decode_rows, width)),
            scratch((decode_rows, channels)),
            scratch((decode_rows, channels)),
            scratch((tiles, reqs * 8, LANES)),
            scratch((tiles, 8 * states, LANES)),
            scratch((tiles, reqs * states, LANES)),
            scratch((tiles, reqs * 8, LANES)),
        ],
        compiler_params=PARAMS,
        name="decode_scan",
    )(
        position, rows, decode_x, decode_gates, resident_state, got_state, step_weight,
        step_bias_row, decay_log, skip_row,
    )
    prompt_state = got_final.astype(F32).reshape(groups * PAIR, states, channels)
    return (decode_out, final_state, final_conv, prefill_out, prompt_state, prompt_conv)


def solution(mesh):
    whole = P("group", None, "mp")
    return jax.shard_map(
        on_device,
        mesh=mesh,
        in_specs=(
            whole,
            whole,
            P("group"),
            whole,
            whole,
            whole,
            whole,
            P("group"),
            P("group", None),
            P(None, "mp"),
            P("mp"),
            P("mp", None),
            P("mp", None),
            P(None, "mp"),
            P("mp"),
            P(None, "mp"),
            P("mp"),
        ),
        out_specs=(whole,) * 6,
        check_vma=False,
    )
```

time: 593 us -> 118 us (0.20)
  blocking collectives: 159 us -> 16.8 us
  local copies, waits for them, and re-layouts: 140 us -> 7.83 us
  waiting for transfers between devices: 137 us -> 38.5 us
  other arithmetic: 58.4 us -> 1.14 us
  starting transfers between devices: 62 us -> 27.6 us
  matrix products: 12.8 us -> 0 us
  Pallas kernels: 0 us -> 11.7 us
    psum x1 -> x0, waiting for transfers between devices: 136 us -> none  [mixer(): low_rank, selects = lax.psum((low_part, select_part), 'mp')]
    psum x1 -> x0, blocking collectives: 120 us -> none  [mixer(): low_rank, selects = lax.psum((low_part, select_part), 'mp')]
    dynamic_slice x674 -> x0, local copies, waits for them, and re-layouts: 73.7 us -> none  [the longest x576 53.1 us: advance(): live_t = lax.dynamic_index_in_dim(live_blk, position, 1, keepdims=False)]
    all_to_all x4 -> x3, waiting for transfers between devices: 0.84 us -> 37.8 us  [exchange(): return lax.all_to_all(value, axis, split_axis=0, concat_axis=0, tiled=True)]
    all_to_all x4 -> x3, starting transfers between devices: 61.9 us -> 27.6 us  [exchange(): return lax.all_to_all(value, axis, split_axis=0, concat_axis=0, tiled=True)]
    reduce_sum x291 -> x0, other arithmetic: 29.7 us -> none  [the longest x288 27.6 us: advance(): values_out = jnp.sum(c_t[:, :, None] * carried, axis=1) + skip_gain * conv_t]
    all_gather x1 -> x0, blocking collectives: 27.5 us -> none  [on_device(): arrived_conv = lax.all_gather(packed_conv, 'group', axis=0, tiled=True)]
    dynamic_update_slice x48 -> x0, local copies, waits for them, and re-layouts: 25.5 us -> none  [mixer(): outputs, finals = lax.map(block_scan, grouped)]
  transfers between devices with their start and end apart: 6 -> 4, of which waited for: 2 -> 3; matrix products, arithmetic and copies ran while one was open for 11% -> 1% of each run, Pallas kernels for 0% -> 7%
where the time goes in v1:
time: 118 us
  waiting for transfers between devices  38.5 us (33%)
  starting transfers between devices  27.6 us (23%)
  blocking collectives  16.8 us (14%)
  between operations  14.2 us (12%)
  Pallas kernels  11.7 us (10%)
  local copies, waits for them, and re-layouts  7.83 us (7%)
    all_to_all x3, waiting for transfers between devices, exchange(): return lax.all_to_all(value, axis, split_axis=0, concat_axis=0, tiled=True)  37.8 us
    all_to_all x3, starting transfers between devices, exchange(): return lax.all_to_all(value, axis, split_axis=0, concat_axis=0, tiled=True)  27.6 us
    all_to_all x1, blocking collectives, exchange(): return lax.all_to_all(value, axis, split_axis=0, concat_axis=0, tiled=True)  16.8 us
    unnamed x41, local copies, waits for them, and re-layouts  7.83 us
    pallas_call x1, Pallas kernels, on_device(): pl.pallas_call(prefill_kernel, out_shape=(struct(prompt_inputs.shape, BF1...  4.14 us
    pallas_call x1, Pallas kernels, on_device(): pl.pallas_call(decode_scan_kernel, out_shape=(struct(decode_inputs.shape,...  3.4 us
  transfers between devices with their start and end apart: 4, of which 3 were waited for; matrix products, arithmetic and copies ran while one was open for 1% of the time, Pallas kernels for 7%

profile of v1, /device:TPU:1, one launch (start us, length us, event | category | flops | bytes accessed | tf_op | source)
XLA Modules:
  0.0 117.8 jit_solution(4539627325369077800)
XLA Ops:
  7.2 0.7 copy.31.dest_ref
  7.9 0.0 copy-start.15
  7.9 0.0 copy-start.16
  7.9 0.9 copy.32.conv_ref
  8.8 0.0 copy-done.15
  8.8 0.0 copy-done.16
  8.8 0.0 copy-start
  8.8 1.0 copy-done
  9.8 0.9 copy-done.5
  10.7 1.8 %pack.1 = (bf16[16,24,512]{2,1,0:T(8,128)(2,1)}, bf16[4,16,512]{2,1,0:T(8,128)(2,1)}) custom-call(s32[16]{0:T(128)S(1)} %copy-done.15, s32[8,1]{1,0:T(8,128)S(1)} %copy.31.dest_ref, s32[8]{0:T(128)S(1)} %copy-done.16, bf16[16,3,512]{2,1,0:T(4,128)(2,1)S(1)} %copy.32.conv_ref, f32[16,16,512]{2,1,0:T(8,128)S(1)} %copy-done, bf16[8,16,512]{2,1,0:T(8,128)(2,1)S(1)} %copy-done.5), custom_call_target="tpu_custom_call" | custom-call | tf_op jit(solution)/shard_map/pack/pallas_call | solution.py:383
  12.5 10.4 %all-to-all-start = ((bf16[16,24,512]{2,1,0:T(8,128)(2,1)}), bf16[16,24,512]{2,1,0:T(8,128)(2,1)S(1)}, u32[]{:S(2)}, u32[]{:S(2)}) async-start(bf16[16,24,512]{2,1,0:T(8,128)(2,1)} %get-tuple-element.19), calls=%async_computation | async-start | bytes 786432 | tf_op jit(solution)/shard_map/all_to_all | solution.py:341
  22.9 0.0 copy-done.17
  22.9 0.0 copy-start.6
  22.9 0.0 copy-start.11
  22.9 0.0 copy-start.12
  22.9 0.1 copy.35.select_ref
  23.0 0.0 copy-done.3
  23.0 0.7 copy-done.6
  23.8 0.0 copy-done.11
  23.8 0.0 copy-done.12
  23.8 0.4 prompt_features.1
  24.2 13.2 %all-to-all-done.got_ref = bf16[16,24,512]{2,1,0:T(8,128)(2,1)S(1)} async-done(((bf16[16,24,512]{2,1,0:T(8,128)(2,1)}), bf16[16,24,512]{2,1,0:T(8,128)(2,1)S(1)}, u32[]{:S(2)}, u32[]{:S(2)}) %all-to-all-start) | async-done | bytes 393248 | tf_op jit(solution)/shard_map/all_to_all | solution.py:341
  37.4 0.0 copy-done.9
  37.4 1.9 %decode_features.1 = (bf16[32,8,640]{2,1,0:T(8,128)(2,1)}, bf16[64,512]{1,0:T(8,128)(2,1)S(1)}, s32[16,128]{1,0:T(8,128)S(1)}, bf16[16,3,512]{2,1,0:T(4,128)(2,1)S(1)}, bf16[32,3,512]{2,1,0:T(4,128)(2,1)S(1)}) custom-call(s32[16]{0:T(128)S(1)} %copy-done.15, bf16[16,24,512]{2,1,0:T(8,128)(2,1)S(1)} %all-to-all-done.got_ref, ...), custom_call_target="tpu_custom_call" | custom-call | tf_op jit(solution)/shard_map/decode_features/pallas_call | solution.py:411
  39.3 11.3 %all-to-all-start.1 = ((bf16[32,8,640]{2,1,0:T(8,128)(2,1)}), bf16[32,8,640]{2,1,0:T(8,128)(2,1)S(1)}, u32[]{:S(2)}, u32[]{:S(2)}) async-start(bf16[32,8,640]{2,1,0:T(8,128)(2,1)} %get-tuple-element.22), calls=%async_computation.1 | async-start | bytes 655360 | tf_op jit(solution)/shard_map/all_to_all | solution.py:341
  50.6 0.0 all-gather.2.cloned.1.call-start
  50.7 0.7 all-gather.2.cloned.1.call-update
  51.3 0.0 copy-start.2
  51.4 13.3 %all-to-all-done.1.part_ref = bf16[32,8,640]{2,1,0:T(8,128)(2,1)S(1)} async-done(((bf16[32,8,640]{2,1,0:T(8,128)(2,1)}), bf16[32,8,640]{2,1,0:T(8,128)(2,1)S(1)}, u32[]{:S(2)}, u32[]{:S(2)}) %all-to-all-start.1) | async-done | bytes 327712 | tf_op jit(solution)/shard_map/all_to_all | solution.py:341
  64.6 0.1 sum_norm.1
  64.8 0.0 copy-start.7
  64.8 0.0 copy-start.8
  64.8 16.8 %all_to_all.20.rows_ref = bf16[32,8,640]{2,1,0:T(8,128)(2,1)S(1)} all-to-all(bf16[32,8,640]{2,1,0:T(8,128)(2,1)S(1)} %sum_norm.1), channel_id=1, replica_groups=mesh['group'=16,'mp'=32] {'mp'}, dimensions={0} | all-to-all | bytes 655360 | tf_op jit(solution)/shard_map/all_to_all | solution.py:341
  81.6 0.0 copy-done.2
  81.7 0.0 copy-done.7
  81.7 0.0 copy-done.8
  81.7 0.7 copy-done.14
  82.3 0.0 copy-done.13
  82.3 4.1 %prefill_scan.1 = (bf16[8,16,512]{2,1,0:T(8,128)(2,1)}, bf16[32,16,512]{2,1,0:T(8,128)(2,1)}) custom-call(s32[8]{0:T(128)S(1)} %copy-done.16, s32[8,1]{1,0:T(8,128)S(1)} %copy.31.dest_ref, bf16[32,8,640]{2,1,0:T(8,128)(2,1)S(1)} %all_to_all.20.rows_ref, bf16[128,512]{1,0:T(8,128)(2,1)S(1)} %get-tuple-element.28.x_ref, bf16[8,16,512]{2,1,0:T(8,128)(2,1)S(1)} %copy-done.8, ...), custom_call_target="tpu_custom_call" | custom-call | tf_op jit(solution)/shard_map/prefill_scan/pallas_call | solution.py:447
  86.5 5.9 %all-to-all-start.3 = ((bf16[16,2,16,512]{3,2,1,0:T(8,128)(2,1)}), bf16[16,2,16,512]{3,2,1,0:T(8,128)(2,1)S(1)}, u32[]{:S(2)}, u32[]{:S(2)}) async-start(bf16[16,2,16,512]{3,2,1,0:T(8,128)(2,1)} %bitcast.3), calls=%async_computation.3 | async-start | bytes 1048576 | tf_op jit(solution)/shard_map/all_to_all | solution.py:341
  92.4 0.6 copy.37
  93.1 0.7 copy.38
  93.7 0.0 copy-done.1
  93.7 0.2 copy-done.10
  93.9 1.2 %copy-done.4 = bf16[64,16,512]{2,1,0:T(8,128)(2,1)S(1)} copy-done((bf16[64,16,512]{2,1,0:T(8,128)(2,1)S(1)}, bf16[64,16,512]{2,1,0:T(8,128)(2,1)}, u32[]{:S(2)}) %copy-start.4) | copy-done | bytes 1048600
  95.1 3.4 %decode_scan.1 = (bf16[16,4,512]{2,1,0:T(4,128)(2,1)}, f32[16,16,512]{2,1,0:T(8,128)}) custom-call(s32[16,128]{1,0:T(8,128)S(1)} %get-tuple-element.21.pos_ref, bf16[32,8,640]{2,1,0:T(8,128)(2,1)S(1)} %all_to_all.20.rows_ref, bf16[64,512]{1,0:T(8,128)(2,1)S(1)} %get-tuple-element.23.x_ref, bf16[16,4,512]{2,1,0:T(4,128)(2,1)S(1)} %copy-done.10, ...), custom_call_target="tpu_custom_call" | custom-call | tf_op jit(solution)/shard_map/decode_scan/pallas_call | solution.py:476
  98.5 11.3 %all-to-all-done.3 = bf16[16,2,16,512]{3,2,1,0:T(8,128)(2,1)S(1)} async-done(((bf16[16,2,16,512]{3,2,1,0:T(8,128)(2,1)}), bf16[16,2,16,512]{3,2,1,0:T(8,128)(2,1)S(1)}, u32[]{:S(2)}, u32[]{:S(2)}) %all-to-all-start.3) | async-done | bytes 524320 | tf_op jit(solution)/shard_map/all_to_all | solution.py:341
  109.8 1.1 bitcast_convert_fusion
  (10 shorter events, 0.0 us)
Async XLA Ops:
  7.9 0.9 copy-start.15
  7.9 0.9 copy-start.16
  8.8 1.0 copy-start
  9.8 0.9 copy-start.5
  12.5 10.5 %copy-start.3 = (bf16[512,512]{1,0:T(8,128)(2,1)S(1)}, bf16[512,512]{1,0:T(8,128)(2,1)}, u32[]{:S(2)}) copy-start(bf16[512,512]{1,0:T(8,128)(2,1)} %rank_ref.3) | copy-start | bytes 1572868
  12.5 10.4 %copy-start.17 = (bf16[512,32]{0,1:T(8,128)(2,1)S(1)}, bf16[512,32]{0,1:T(8,128)(2,1)}, u32[]{:S(2)}) copy-start(bf16[512,32]{0,1:T(8,128)(2,1)} %param.29) | copy-start | bytes 98308
  12.5 24.9 %all-to-all-start = ((bf16[16,24,512]{2,1,0:T(8,128)(2,1)}), bf16[16,24,512]{2,1,0:T(8,128)(2,1)S(1)}, u32[]{:S(2)}, u32[]{:S(2)}) async-start(bf16[16,24,512]{2,1,0:T(8,128)(2,1)} %get-tuple-element.19), calls=%async_computation | async-start | bytes 786432 | tf_op jit(solution)/shard_map/all_to_all | solution.py:341
  22.9 0.9 copy-start.6
  22.9 0.9 copy-start.11
  22.9 0.9 copy-start.12
  23.8 13.6 %copy-start.9 = (bf16[16,4,512]{2,1,0:T(4,128)(2,1)S(1)}, bf16[16,4,512]{2,1,0:T(4,128)(2,1)}, u32[]{:S(2)}) copy-start(bf16[16,4,512]{2,1,0:T(4,128)(2,1)} %u_ref.5) | copy-start | bytes 196612
  39.3 25.3 %all-to-all-start.1 = ((bf16[32,8,640]{2,1,0:T(8,128)(2,1)}), bf16[32,8,640]{2,1,0:T(8,128)(2,1)S(1)}, u32[]{:S(2)}, u32[]{:S(2)}) async-start(bf16[32,8,640]{2,1,0:T(8,128)(2,1)} %get-tuple-element.22), calls=%async_computation.1 | async-start | bytes 655360 | tf_op jit(solution)/shard_map/all_to_all | solution.py:341
  50.6 43.1 %all-gather.2.cloned.1.call-start = ((), (), s32[]{:S(2)}) async-start(), calls=%async_computation.4 | async-start | bytes 1114112 | tf_op jit(solution)/shard_map/all_gather | solution.py:396
  51.3 30.3 %copy-start.2 = (bf16[512,512]{1,0:T(8,128)(2,1)S(1)}, bf16[512,512]{1,0:T(8,128)(2,1)}, u32[]{:S(2)}) copy-start(bf16[512,512]{1,0:T(8,128)(2,1)} %step_w_ref.3) | copy-start | bytes 1572868
  64.8 16.9 %copy-start.7 = (f32[16,512]{1,0:T(8,128)S(1)}, f32[16,512]{1,0:T(8,128)}, u32[]{:S(2)}) copy-start(f32[16,512]{1,0:T(8,128)} %decay_ref.3) | copy-start | bytes 98308
  64.8 16.8 %copy-start.8 = (bf16[8,16,512]{2,1,0:T(8,128)(2,1)S(1)}, bf16[8,16,512]{2,1,0:T(8,128)(2,1)}, u32[]{:S(2)}) copy-start(bf16[8,16,512]{2,1,0:T(8,128)(2,1)} %gate_ref.3) | copy-start | bytes 393220
  81.6 0.7 copy-start.14
  81.6 0.7 copy-start.13
  86.5 7.2 %copy-start.1 = (f32[16,16,512]{2,1,0:T(8,128)S(1)}, f32[16,16,512]{2,1,0:T(8,128)}, u32[]{:S(2)}) copy-start(f32[16,16,512]{2,1,0:T(8,128)} %state_ref.3) | copy-start | bytes 1572868
  86.5 23.3 %all-to-all-start.3 = ((bf16[16,2,16,512]{3,2,1,0:T(8,128)(2,1)}), bf16[16,2,16,512]{3,2,1,0:T(8,128)(2,1)S(1)}, u32[]{:S(2)}, u32[]{:S(2)}) async-start(bf16[16,2,16,512]{3,2,1,0:T(8,128)(2,1)} %bitcast.3), calls=%async_computation.3 | async-start | bytes 1048576 | tf_op jit(solution)/shard_map/all_to_all | solution.py:341
  93.1 0.8 copy-start.10
  93.9 1.2 %copy-start.4 = (bf16[64,16,512]{2,1,0:T(8,128)(2,1)S(1)}, bf16[64,16,512]{2,1,0:T(8,128)(2,1)}, u32[]{:S(2)}) copy-start(bf16[64,16,512]{2,1,0:T(8,128)(2,1)} %all-gather.2.cloned.1.call-done.moved_ref) | copy-start | bytes 3145732
Sparse Core Ops, SparseCore 0:
  54.1 37.8 all-gather.1

commit v2 on v1

v2 whole, which is shorter than its diff:
```python
import jax
import jax.numpy as jnp
from jax import lax
from jax.experimental import pallas as pl
from jax.experimental.pallas import tpu as pltpu
from jax.sharding import PartitionSpec as P

MIG = 4
PAIR = 2
EPS = 1e-06
LANES = 128
ROWS0 = 24
PROMPT_GROUPS = 16
STATE_ROW = 14
TAIL_ROW = 18
LOG2E = 1.4426950408889634

F32 = jnp.float32
BF16 = jnp.bfloat16
VMEM = pl.BlockSpec(memory_space=pltpu.VMEM)
SMEM = pl.BlockSpec(memory_space=pltpu.SMEM)
PARAMS = pltpu.CompilerParams(vmem_limit_bytes=40 * 1024 * 1024)
ALL_VMEM = pltpu.CompilerParams(vmem_limit_bytes=60 * 1024 * 1024)


def silu(x):
    return x / (1.0 + jnp.exp(-x))


def softplus(x):
    return jnp.maximum(x, 0.0) + jnp.log1p(jnp.exp(-jnp.abs(x)))


def iota(shape, dim):
    return lax.broadcasted_iota(jnp.int32, shape, dim)


def from_scalars(ref, count, shape):
    rows = iota(shape, 0)
    out = jnp.zeros(shape, jnp.int32)
    for i in range(count):
        out = jnp.where(rows == i, ref[i], out)
    return out


def slots_of(dest_ref, count):
    dests = [dest_ref[i] for i in range(count)]
    ranks = []
    for i in range(count):
        rank = jnp.int32(0)
        for j in range(i):
            rank = rank + (dests[j] == dests[i]).astype(jnp.int32)
        ranks.append(rank)
    return dests, ranks


def picks_of(mig_ref, reqs):
    own = lax.axis_index("group")
    count = jnp.int32(0)
    picks = [jnp.int32(0) for _ in range(MIG)]
    for r in range(reqs):
        moved = mig_ref[r] != own * reqs + r
        for k in range(MIG):
            picks[k] = jnp.where(moved & (count == k), r, picks[k])
        count = count + moved.astype(jnp.int32)
    return own, picks


def pack_kernel(
    mig_ref, dest_ref, len_ref, conv_ref, state_ref, u_ref, pay_ref, scr, conv_scr, u_scr, held, sems
):
    groups = pay_ref.shape[0]
    _, reqs, channels = conv_ref.shape
    prompts, steps, _ = u_ref.shape
    states = state_ref.shape[1]
    own, picks = picks_of(mig_ref, reqs)
    copies = [
        pltpu.make_async_copy(state_ref.at[picks[k]], held.at[k], sems.at[k]) for k in range(MIG)
    ]
    for copy in copies:
        copy.start()
    base = scr.at[groups]
    base[...] = jnp.zeros(base.shape, F32)
    lane = iota((1, channels), 1)
    ids = jnp.zeros((1, channels), jnp.int32)
    wanted = jnp.zeros((1, channels), jnp.int32)
    for j in range(3):
        conv_scr[j * reqs : (j + 1) * reqs, :] = conv_ref[j].astype(F32)
    for k in range(MIG):
        for at in (k, 4 + k, 8 + k, STATE_ROW + k):
            ids = jnp.where(lane == own * ROWS0 + at, own * reqs + picks[k], ids)
        wanted = jnp.where(lane == own * MIG + k, mig_ref[picks[k]], wanted)
        for j in range(3):
            at = 4 * j + k
            base[at : at + 1, :] = conv_scr[pl.ds(j * reqs + picks[k], 1), :]
    base[12:13, :] = ids.astype(F32)
    base[13:14, :] = wanted.astype(F32)
    for d in range(groups):
        scr[d] = base[...]
    dests, ranks = slots_of(dest_ref, prompts)
    pad = u_scr.shape[0] // prompts
    for i in range(prompts):
        u_scr[i * pad : i * pad + 8, :] = jnp.zeros((8, channels), F32)
        u_scr[i * pad + 8 : i * pad + 8 + steps, :] = u_ref[i].astype(F32)
    for i in range(prompts):
        tails = [u_scr[pl.ds(i * pad + 5 + j + len_ref[i], 1), :] for j in range(3)]
        for q in range(PAIR):

            @pl.when(ranks[i] == q)
            def _():
                for j in range(3):
                    at = TAIL_ROW + 3 * q + j
                    scr[dests[i], at : at + 1, :] = tails[j]

    for copy in copies:
        copy.wait()
    for k in range(MIG):
        for n in range(states):
            scr[n, STATE_ROW + k : STATE_ROW + k + 1, :] = held[k, n : n + 1, :]
    for d in range(groups):
        pay_ref[d] = scr[d].astype(BF16)


def put_lanes(ref, start, value):
    for l in range(ref.shape[0]):
        ref[l, start : start + value.shape[0], :] = value[:, l * LANES : (l + 1) * LANES]


def project(x, rank_ref, select_ref):
    low = jnp.dot(x, rank_ref[...], preferred_element_type=F32)
    sel = lax.dot_general(
        x, select_ref[...], (((1,), (1,)), ((), ())), preferred_element_type=F32
    )
    return low, sel


def put_tiles(scr, first, low, sel):
    tiles = low.shape[1] // LANES
    width = sel.shape[1]
    share = LANES // width
    for g in range(low.shape[0] // 8):
        rows = slice(8 * g, 8 * g + 8)
        for l in range(tiles):
            owner, place = divmod((first + g) * tiles + l, 3)
            scr[owner, 8 * place : 8 * place + 8, :] = low[rows, l * LANES : (l + 1) * LANES]
        owner, place = divmod(first + g, share)
        scr[owner, 24:32, place * width : (place + 1) * width] = sel[rows]


def take_tiles(rows_ref, first, low_scr, sel_scr):
    count, channels = low_scr.shape
    tiles = channels // LANES
    for g in range(count // 8):
        rows = slice(8 * g, 8 * g + 8)
        for l in range(tiles):
            owner, place = divmod((first + g) * tiles + l, 3)
            low_scr[rows, l * LANES : (l + 1) * LANES] = rows_ref[owner].astype(F32)[
                8 * place : 8 * place + 8
            ]
        owner, place = divmod(first + g, 4)
        pair = rows_ref[owner].astype(F32)[24:32]
        sel_scr[rows, :] = pltpu.roll(pair, (LANES - 32 * place) % LANES, 1) if place else pair


def prompt_kernel(
    u_ref, cw_ref, cb_ref, rank_ref, select_ref, low_ref, sel_ref, x_ref, scr, x_scr
):
    prompts, steps, channels = u_ref.shape
    for i in range(prompts):
        put_lanes(scr, i * steps, u_ref[i].astype(F32))
    for l in range(channels // LANES):
        cols = slice(l * LANES, (l + 1) * LANES)
        taps = [cw_ref[k : k + 1, cols] for k in range(4)]
        bias = cb_ref[:, cols]
        window = [jnp.zeros((prompts, LANES), F32) for _ in range(3)]
        for t in range(steps):
            window.append(scr[l, pl.ds(t, prompts, stride=steps), :])
            acc = bias
            for k in range(4):
                acc = acc + taps[k] * window[t + k]
            x_scr[t * prompts : (t + 1) * prompts, cols] = silu(acc)
    x = x_scr[...].astype(BF16)
    x_ref[...] = x
    low, sel = project(x, rank_ref, select_ref)
    low_ref[...] = low
    sel_ref[...] = sel


def decode_kernel(
    mig_ref, got_ref, conv_ref, u_ref, cw_ref, cb_ref, rank_ref, select_ref, prompt_low_ref,
    prompt_sel_ref, pay_ref, x_ref, pass_ref, final_conv_ref, prompt_conv_ref, pool_scr, pay_scr,
    scr, x_scr,
):
    groups = got_ref.shape[0]
    reqs, steps, channels = u_ref.shape
    table = groups * ROWS0
    own = lax.axis_index("group")
    marks = jnp.zeros((8, channels), F32)
    for s in range(groups):
        block = got_ref[s].astype(F32)
        pool_scr[s * ROWS0 : (s + 1) * ROWS0, :] = block
        marks = marks + block[8:16]
        for q in range(PAIR):
            for j in range(3):
                at = TAIL_ROW + 3 * q + j
                prompt_conv_ref[j, s * PAIR + q : s * PAIR + q + 1, :] = block[at : at + 1]
    for r in range(reqs):
        put_lanes(scr, 8 * r, u_ref[r].astype(F32))
    pool = pool_scr[...].astype(BF16)
    ids = marks[4:5, :table]
    place = lax.rem(iota((1, table), 1), ROWS0)
    moves = groups * MIG
    square = (moves, LANES)
    wanted = jnp.sum(
        jnp.where(
            iota(square, 0) == iota(square, 1), jnp.broadcast_to(marks[5:6, :LANES], square), 0.0
        ),
        axis=1,
        keepdims=True,
    )
    passed = (wanted == ids) & (place >= STATE_ROW) & (place < STATE_ROW + MIG)
    relay = jnp.dot(jnp.where(passed, 1.0, 0.0).astype(BF16), pool, preferred_element_type=F32)
    for d in range(groups):
        own_rows = relay[d * MIG : (d + 1) * MIG]
        pass_ref[d] = jnp.concatenate([own_rows, own_rows], axis=0).astype(BF16)
    wide = (reqs, channels)
    moved_wide = from_scalars(mig_ref, reqs, wide) != own * reqs + iota(wide, 0)
    shape = (reqs, table)
    needs = from_scalars(mig_ref, reqs, shape)
    found = (needs != own * reqs + iota(shape, 0)) & (
        jnp.broadcast_to(ids, shape) == needs.astype(F32)
    )
    hist = []
    for j in range(3):
        hit = jnp.where(found & (place >= 4 * j) & (place < 4 * j + 4), 1.0, 0.0).astype(BF16)
        taken = jnp.dot(hit, pool, preferred_element_type=F32)
        hist.append(jnp.where(moved_wide, taken, conv_ref[j].astype(F32)))
    for l in range(channels // LANES):
        cols = slice(l * LANES, (l + 1) * LANES)
        taps = [cw_ref[k : k + 1, cols] for k in range(4)]
        bias = cb_ref[:, cols]
        window = [hist[j][:, cols] for j in range(3)]
        for t in range(steps):
            window.append(scr[l, pl.ds(t, reqs, stride=8), :])
            acc = bias
            for k in range(4):
                acc = acc + taps[k] * window[t + k]
            x_scr[t * reqs : (t + 1) * reqs, cols] = silu(acc)
        for j in range(3):
            final_conv_ref[j, :, cols] = window[steps + j].astype(BF16)
    x = x_scr[...].astype(BF16)
    x_ref[...] = x
    low, sel = project(x, rank_ref, select_ref)
    prompt_groups = prompt_low_ref.shape[0] // 8
    pay_scr[...] = jnp.zeros(pay_scr.shape, F32)
    put_tiles(pay_scr, 0, prompt_low_ref[...], prompt_sel_ref[...])
    put_tiles(pay_scr, prompt_groups, low, sel)
    pay_ref[...] = pay_scr[...].astype(BF16)


def sum_kernel(got_ref, out_ref):
    total = got_ref[0].astype(F32)
    for j in range(1, got_ref.shape[0]):
        total = total + got_ref[j].astype(F32)
    own_rows = total.astype(BF16)
    for j in range(out_ref.shape[0]):
        out_ref[j] = own_rows


def steps_of(low_scr, step_w_ref, step_b):
    low = low_scr[...]
    scale = lax.rsqrt(jnp.mean(low * low, axis=-1, keepdims=True) + EPS)
    raw = jnp.dot(low.astype(BF16), step_w_ref[...], preferred_element_type=F32)
    return softplus(raw * scale + step_b)


def scan(t, items, live, x, gate, sel, step, decay, skip, h_scr, y_scr, y_stride):
    states = decay.shape[1] // 8
    for g in range(items // 8):
        rows = slice(t * items + 8 * g, t * items + 8 * g + 8)
        alive = None if live is None else live[8 * g : 8 * g + 8]
        pair = sel[rows, :]
        lanes = range(h_scr.shape[0])
        steps, drive, y = [], [], []
        for l in lanes:
            cols = slice(l * LANES, (l + 1) * LANES)
            step_l = step[rows, cols]
            if alive is not None:
                step_l = jnp.where(alive, step_l, 0.0)
            x_l = x[rows, cols]
            steps.append(step_l)
            drive.append(step_l * x_l)
            y.append(skip[:, cols] * x_l)
        for n in range(states):
            b = jnp.broadcast_to(pair[:, n : n + 1], (8, LANES))
            c = jnp.broadcast_to(pair[:, states + n : states + n + 1], (8, LANES))
            at = slice(n * items + 8 * g, n * items + 8 * g + 8)
            for l in lanes:
                keep = jnp.exp2(steps[l] * decay[l, 8 * n : 8 * n + 8, :])
                h = keep * h_scr[l, at, :] + drive[l] * b
                h_scr[l, at, :] = h
                y[l] = y[l] + c * h
        for l in lanes:
            cols = slice(l * LANES, (l + 1) * LANES)
            out = y[l] * gate[rows, cols]
            if alive is not None:
                out = jnp.where(alive, out, 0.0)
            y_scr[l, pl.ds(8 * g * y_stride + t, 8, stride=y_stride), :] = out


def prompt_prepare_kernel(
    gate_ref, decay_ref, step_b_ref, skip_ref, gate_out_ref, decay_out_ref, rows_out_ref, scr
):
    prompts, steps, channels = gate_ref.shape
    rows_out_ref[0:1, :] = step_b_ref[...]
    rows_out_ref[1:2, :] = skip_ref[...]
    decay = jnp.exp(decay_ref[...]) * -LOG2E
    for n in range(decay.shape[0]):
        put_lanes(decay_out_ref, 8 * n, jnp.broadcast_to(decay[n : n + 1], (8, channels)))
    for i in range(prompts):
        put_lanes(scr, i * steps, silu(gate_ref[i].astype(F32)))
    for l in range(channels // LANES):
        cols = slice(l * LANES, (l + 1) * LANES)
        for t in range(steps):
            gate_out_ref[t * prompts : (t + 1) * prompts, cols] = scr[
                l, pl.ds(t, prompts, stride=steps), :
            ]


def prefill_kernel(
    len_ref, dest_ref, rows_ref, x_ref, gate_ref, step_w_ref, decay_ref, extra_ref, relay_ref,
    out_ref, pay_ref, low_scr, sel_scr, step_scr, x_scr, h_scr, y_scr,
):
    prompts, steps, channels = out_ref.shape
    states = decay_ref.shape[1] // 8
    take_tiles(rows_ref, 0, low_scr, sel_scr)
    step_scr[...] = steps_of(low_scr, step_w_ref, extra_ref[0:1, :])
    x_scr[...] = x_ref[...].astype(F32)
    h_scr[...] = jnp.zeros(h_scr.shape, F32)
    lengths = from_scalars(len_ref, prompts, (prompts, LANES))
    skip = extra_ref[1:2, :]
    for t in range(steps):
        scan(
            t, prompts, t < lengths, x_scr, gate_ref, sel_scr, step_scr, decay_ref, skip, h_scr,
            y_scr, steps,
        )
    dests, ranks = slots_of(dest_ref, prompts)
    groups = pay_ref.shape[0]
    slots = PAIR * states
    for d in range(groups):
        pay_ref[d, :slots, :] = jnp.zeros((slots, channels), BF16)
        pay_ref[d, slots:, :] = relay_ref[d]
    for i in range(prompts):
        final = []
        for l in range(channels // LANES):
            cols = slice(l * LANES, (l + 1) * LANES)
            out_ref[i, :, cols] = y_scr[l, i * steps : (i + 1) * steps, :].astype(BF16)
            final.append(h_scr[l, pl.ds(i, states, stride=prompts), :])
        for q in range(PAIR):

            @pl.when(ranks[i] == q)
            def _():
                for l in range(channels // LANES):
                    cols = slice(l * LANES, (l + 1) * LANES)
                    pay_ref[dests[i], q * states : (q + 1) * states, cols] = final[l].astype(BF16)


def decode_prepare_kernel(
    rows_ref, gate_ref, state_ref, step_w_ref, extra_ref, step_ref, sel_ref, gate_out_ref, h_ref,
    low_scr, scr,
):
    reqs, steps, channels = gate_ref.shape
    states = state_ref.shape[1]
    take_tiles(rows_ref, PROMPT_GROUPS, low_scr, sel_ref)
    step_ref[...] = steps_of(low_scr, step_w_ref, extra_ref[0:1, :])
    for r in range(reqs):
        put_lanes(scr, 8 * r, silu(gate_ref[r].astype(F32)))
        for l in range(channels // LANES):
            cols = slice(l * LANES, (l + 1) * LANES)
            h_ref[l, pl.ds(r, states, stride=reqs), :] = state_ref[r, :, cols]
    for l in range(channels // LANES):
        cols = slice(l * LANES, (l + 1) * LANES)
        for t in range(steps):
            gate_out_ref[t * reqs : (t + 1) * reqs, cols] = scr[l, pl.ds(t, reqs, stride=8), :]


def decode_scan_kernel(
    mig_ref, got_ref, x_ref, gate_ref, step_ref, sel_ref, decay_ref, extra_ref, h_ref, out_ref,
    final_ref, prompt_state_ref, x_scr, h_scr, y_scr, moved_scr,
):
    reqs, steps, channels = out_ref.shape
    groups = got_ref.shape[0]
    states = decay_ref.shape[1] // 8
    slots = PAIR * states
    x_scr[...] = x_ref[...].astype(F32)
    h_scr[...] = h_ref[...]
    for n in range(states):
        put_lanes(moved_scr, n * MIG, got_ref[n, slots:, :].astype(F32)[:MIG])
    _, picks = picks_of(mig_ref, reqs)
    for k in range(MIG):
        for l in range(channels // LANES):
            h_scr[l, pl.ds(picks[k], states, stride=reqs), :] = moved_scr[
                l, pl.ds(k, states, stride=MIG), :
            ]
    for s in range(groups):
        for q in range(PAIR):
            prompt_state_ref[s * PAIR + q] = got_ref[s, q * states : (q + 1) * states, :].astype(F32)

    skip = extra_ref[1:2, :]
    for t in range(steps):
        scan(t, reqs, None, x_scr, gate_ref, sel_ref, step_ref, decay_ref, skip, h_scr, y_scr, 8)

    for r in range(reqs):
        for l in range(channels // LANES):
            cols = slice(l * LANES, (l + 1) * LANES)
            out_ref[r, :, cols] = y_scr[l, 8 * r : 8 * r + steps, :].astype(BF16)
            final_ref[r, :, cols] = h_scr[l, pl.ds(r, states, stride=reqs), :]


def exchange(value, axis):
    return lax.all_to_all(value, axis, split_axis=0, concat_axis=0, tiled=True)


def on_device(
    resident_state,
    resident_conv,
    migrate_from,
    decode_inputs,
    decode_gates,
    prompt_inputs,
    prompt_gates,
    prompt_length,
    prompt_dest,
    conv_weight,
    conv_bias,
    rank_weight,
    select_weight,
    step_weight,
    step_bias,
    decay_log,
    skip_gain,
):
    groups = lax.axis_size("group")
    peers = lax.axis_size("mp")
    reqs, states, channels = resident_state.shape
    prompts, steps, _ = prompt_inputs.shape
    decode_steps = decode_inputs.shape[1]
    tiles = channels // LANES
    rank = rank_weight.shape[1]
    selects = select_weight.shape[1]
    prompt_rows = prompts * steps
    decode_rows = reqs * decode_steps
    bias_row = conv_bias.reshape(1, channels)
    step_bias_row = step_bias.reshape(1, channels)
    skip_row = skip_gain.reshape(1, channels)

    def struct(shape, dtype):
        return jax.ShapeDtypeStruct(shape, dtype)

    def scratch(shape):
        return pltpu.VMEM(shape, F32)

    def cost(flops, size):
        return pl.CostEstimate(flops=flops, bytes_accessed=size, transcendentals=0)

    dest = prompt_dest.reshape(prompts)
    conv_rows = jnp.transpose(resident_conv, (1, 0, 2))
    select_rows = jnp.transpose(select_weight)

    send_first = pl.pallas_call(
        pack_kernel,
        out_shape=struct((groups, ROWS0, channels), BF16),
        in_specs=[SMEM] * 3 + [VMEM, pl.BlockSpec(memory_space=pl.ANY), VMEM],
        out_specs=VMEM,
        scratch_shapes=[
            scratch((groups + 1, ROWS0, channels)),
            scratch((3 * reqs, channels)),
            scratch((prompts * (steps + 8), channels)),
            scratch((MIG, states, channels)),
            pltpu.SemaphoreType.DMA((MIG,)),
        ],
        compiler_params=ALL_VMEM,
        name="pack",
    )(migrate_from, dest, prompt_length, conv_rows, resident_state, prompt_inputs)
    got_first = exchange(send_first, "group")

    prompt_low, prompt_sel, prompt_x = pl.pallas_call(
        prompt_kernel,
        out_shape=(
            struct((prompt_rows, rank), F32),
            struct((prompt_rows, selects), F32),
            struct((prompt_rows, channels), BF16),
        ),
        in_specs=[VMEM] * 5,
        out_specs=(VMEM,) * 3,
        scratch_shapes=[scratch((tiles, prompt_rows, LANES)), scratch((prompt_rows, channels))],
        compiler_params=PARAMS,
        cost_estimate=cost(10**9, 2 * 10**6),
        name="prompt_features",
    )(prompt_inputs, conv_weight, bias_row, rank_weight, select_rows)

    gate_rows, decay, extra = pl.pallas_call(
        prompt_prepare_kernel,
        out_shape=(
            struct((prompt_rows, channels), F32),
            struct((tiles, 8 * states, LANES), F32),
            struct((2, channels), F32),
        ),
        in_specs=[VMEM] * 4,
        out_specs=(VMEM,) * 3,
        scratch_shapes=[scratch((tiles, prompt_rows, LANES))],
        compiler_params=PARAMS,
        cost_estimate=cost(10**9, 2 * 10**6),
        name="prompt_prepare",
    )(prompt_gates, decay_log, step_bias_row, skip_row)

    pay, decode_x, relay, final_conv, prompt_conv = pl.pallas_call(
        decode_kernel,
        out_shape=(
            struct((peers, 32, LANES), BF16),
            struct((decode_rows, channels), BF16),
            struct((groups, 8, channels), BF16),
            struct((3, reqs, channels), BF16),
            struct((3, groups * PAIR, channels), F32),
        ),
        in_specs=[SMEM] + [VMEM] * 9,
        out_specs=(VMEM,) * 5,
        scratch_shapes=[
            scratch((groups * ROWS0, channels)),
            scratch((peers, 32, LANES)),
            scratch((tiles, reqs * 8, LANES)),
            scratch((decode_rows, channels)),
        ],
        compiler_params=PARAMS,
        name="decode_features",
    )(
        migrate_from, got_first, conv_rows, decode_inputs, conv_weight, bias_row, rank_weight,
        select_rows, prompt_low, prompt_sel,
    )

    parts = exchange(pay, "mp")
    shares = pl.pallas_call(
        sum_kernel,
        out_shape=struct(parts.shape, BF16),
        in_specs=[VMEM],
        out_specs=VMEM,
        compiler_params=PARAMS,
        name="sum_parts",
    )(parts)
    rows = exchange(shares, "mp")

    prefill_out, send_final = pl.pallas_call(
        prefill_kernel,
        out_shape=(
            struct(prompt_inputs.shape, BF16),
            struct((groups, PAIR * states + 8, channels), BF16),
        ),
        in_specs=[SMEM] * 2 + [VMEM] * 7,
        out_specs=(VMEM, VMEM),
        scratch_shapes=[
            scratch((prompt_rows, rank)),
            scratch((prompt_rows, LANES)),
            scratch((prompt_rows, channels)),
            scratch((prompt_rows, channels)),
            scratch((tiles, prompts * states, LANES)),
            scratch((tiles, prompt_rows, LANES)),
        ],
        compiler_params=PARAMS,
        name="prefill_scan",
    )(
        prompt_length, dest, rows, prompt_x, gate_rows, step_weight, decay, extra, relay,
    )
    got_final = exchange(send_final, "group")

    decode_step, decode_sel, decode_gate, first_state = pl.pallas_call(
        decode_prepare_kernel,
        out_shape=(
            struct((decode_rows, channels), F32),
            struct((decode_rows, LANES), F32),
            struct((decode_rows, channels), F32),
            struct((tiles, reqs * states, LANES), F32),
        ),
        in_specs=[VMEM] * 5,
        out_specs=(VMEM,) * 4,
        scratch_shapes=[scratch((decode_rows, rank)), scratch((tiles, reqs * 8, LANES))],
        compiler_params=PARAMS,
        cost_estimate=cost(4 * 10**9, 4 * 10**6),
        name="decode_prepare",
    )(rows, decode_gates, resident_state, step_weight, extra)

    decode_out, final_state, prompt_state = pl.pallas_call(
        decode_scan_kernel,
        out_shape=(
            struct(decode_inputs.shape, BF16),
            struct(resident_state.shape, F32),
            struct((groups * PAIR, states, channels), F32),
        ),
        in_specs=[SMEM] + [VMEM] * 8,
        out_specs=(VMEM,) * 3,
        scratch_shapes=[
            scratch((decode_rows, channels)),
            scratch((tiles, reqs * states, LANES)),
            scratch((tiles, reqs * 8, LANES)),
            scratch((tiles, states * MIG, LANES)),
        ],
        compiler_params=PARAMS,
        name="decode_scan",
    )(
        migrate_from, got_final, decode_x, decode_gate, decode_step, decode_sel, decay, extra,
        first_state,
    )
    final_conv = jnp.transpose(final_conv, (1, 0, 2))
    prompt_conv = jnp.transpose(prompt_conv, (1, 0, 2)).astype(BF16)
    return (decode_out, final_state, final_conv, prefill_out, prompt_state, prompt_conv)


def solution(mesh):
    whole = P("group", None, "mp")
    return jax.shard_map(
        on_device,
        mesh=mesh,
        in_specs=(
            whole,
            whole,
            P("group"),
            whole,
            whole,
            whole,
            whole,
            P("group"),
            P("group", None),
            P(None, "mp"),
            P("mp"),
            P("mp", None),
            P("mp", None),
            P(None, "mp"),
            P("mp"),
            P(None, "mp"),
            P("mp"),
        ),
        out_specs=(whole,) * 6,
        check_vma=False,
    )
```

time: 118 us -> 104 us (0.88)
  between operations: 14.2 us -> 0.79 us
  starting transfers between devices: 27.6 us -> 20.2 us
  blocking collectives: 16.8 us -> 24 us
  local copies, waits for them, and re-layouts: 7.83 us -> 2.83 us
  waiting for transfers between devices: 38.5 us -> 42.8 us
    all_to_all x3, starting transfers between devices: 27.6 us -> 20.2 us  [exchange(): return lax.all_to_all(value, axis, split_axis=0, concat_axis=0, tiled=True)]
    all_to_all x1, blocking collectives: 16.8 us -> 24 us  [exchange(): return lax.all_to_all(value, axis, split_axis=0, concat_axis=0, tiled=True)]
    unnamed x41 -> x34, local copies, waits for them, and re-layouts: 7.83 us -> 2.83 us
    all_to_all x3, waiting for transfers between devices: 37.8 us -> 42.8 us  [exchange(): return lax.all_to_all(value, axis, split_axis=0, concat_axis=0, tiled=True)]
    pallas_call x4 -> x6, Pallas kernels: 4.17 us -> 6.37 us  [the longest x1 2.69 us: on_device(): pl.pallas_call(pack_kernel, out_shape=struct((groups, ROWS0, channels), B...]
  transfers between devices with their start and end apart: 4 -> 3, of which waited for: 3 -> 3; matrix products, arithmetic and copies ran while one was open for 1% -> 1% of each run, Pallas kernels for 7% -> 1%
where the time goes in v2:
time: 104 us; the launch traced here: 103 us
  waiting for transfers between devices  42.8 us (41%)
  blocking collectives  24 us (23%)
  starting transfers between devices  20.2 us (19%)
  Pallas kernels  12.2 us (12%)
  local copies, waits for them, and re-layouts  2.83 us (3%)
    all_to_all x3, waiting for transfers between devices, exchange(): return lax.all_to_all(value, axis, split_axis=0, concat_axis=0, tiled=True)  42.8 us
    all_to_all x1, blocking collectives, exchange(): return lax.all_to_all(value, axis, split_axis=0, concat_axis=0, tiled=True)  24 us
    all_to_all x3, starting transfers between devices, exchange(): return lax.all_to_all(value, axis, split_axis=0, concat_axis=0, tiled=True)  20.2 us
    pallas_call x1, Pallas kernels, on_device(): pl.pallas_call(prefill_kernel, out_shape=(struct(prompt_inputs.shape, BF1...  3.13 us
    unnamed x34, local copies, waits for them, and re-layouts  2.83 us
    pallas_call x1, Pallas kernels, on_device(): pl.pallas_call(pack_kernel, out_shape=struct((groups, ROWS0, channels), B...  2.69 us
    pallas_call x1, Pallas kernels, on_device(): pl.pallas_call(decode_scan_kernel, out_shape=(struct(decode_inputs.shape,...  2.66 us
  transfers between devices with their start and end apart: 3, of which 3 were waited for; matrix products, arithmetic and copies ran while one was open for 1% of the time, Pallas kernels for 1%

profile of v2, /device:TPU:1, one launch (start us, length us, event | category | flops | bytes accessed | tf_op | source)
XLA Modules:
  0.0 103.5 jit_solution(248047085330584262)
XLA Ops:
  0.6 2.7 %pack.1 = bf16[16,24,512]{2,1,0:T(8,128)(2,1)} custom-call(s32[16]{0:T(128)} %mig_ref.5, s32[8]{0:T(128)} %bitcast.15, s32[8]{0:T(128)} %len_ref.3, bf16[3,16,512]{2,1,0:T(8,128)(2,1)} %bitcast.9, f32[16,16,512]{2,1,0:T(8,128)} %state_ref.3, bf16[8,16,512]{2,1,0:T(8,128)(2,1)} %u_ref.4), custom_call_target="tpu_custom_call" | custom-call | tf_op jit(solution)/shard_map/pack/pallas_call | solution.py:470
  3.3 0.0 copy-start.1
  3.3 0.0 copy-start.4
  3.4 0.0 copy-start.6
  3.4 0.0 copy-start.7
  3.4 10.4 %all-to-all-start = ((bf16[16,24,512]{2,1,0:T(8,128)(2,1)}), bf16[16,24,512]{2,1,0:T(8,128)(2,1)S(1)}, u32[]{:S(2)}, u32[]{:S(2)}) async-start(bf16[16,24,512]{2,1,0:T(8,128)(2,1)} %pack.1), calls=%async_computation | async-start | bytes 786432 | tf_op jit(solution)/shard_map/all_to_all | solution.py:421
  13.7 0.0 copy-start.9
  13.7 0.0 copy-done.1
  13.8 0.0 copy-done.4
  13.8 0.0 copy-done.6
  13.8 0.0 copy-done.7
  13.8 0.6 copy-done.9
  14.4 0.0 copy-start.3
  14.4 0.0 copy-start.5
  14.4 0.4 prompt_features.1
  14.8 13.5 %all-to-all-done.got_ref = bf16[16,24,512]{2,1,0:T(8,128)(2,1)S(1)} async-done(((bf16[16,24,512]{2,1,0:T(8,128)(2,1)}), bf16[16,24,512]{2,1,0:T(8,128)(2,1)S(1)}, u32[]{:S(2)}, u32[]{:S(2)}) %all-to-all-start) | async-done | bytes 393248 | tf_op jit(solution)/shard_map/all_to_all | solution.py:421
  28.3 0.0 copy-start.8
  28.3 0.0 copy-done.3
  28.3 0.0 copy-done.5
  28.3 0.6 copy-done.8
  28.9 1.8 %decode_features.1 = (bf16[32,32,128]{2,1,0:T(8,128)(2,1)S(1)}, bf16[64,512]{1,0:T(8,128)(2,1)S(1)}, bf16[16,8,512]{2,1,0:T(8,128)(2,1)S(1)}, bf16[3,16,512]{2,1,0:T(8,128)(2,1)}, f32[3,32,512]{2,1,0:T(8,128)S(1)}) custom-call(s32[16]{0:T(128)S(1)} %copy-done.8, bf16[16,24,512]{2,1,0:T(8,128)(2,1)S(1)} %all-to-all-done.got_ref, ...), custom_call_target="tpu_custom_call" | custom-call | tf_op jit(solution)/shard_map/decode_features/pallas_call | solution.py:517
  30.7 24.0 %all_to_all.20.got_ref = bf16[32,32,128]{2,1,0:T(8,128)(2,1)S(1)} all-to-all(bf16[32,32,128]{2,1,0:T(8,128)(2,1)S(1)} %get-tuple-element.28), channel_id=1, replica_groups=mesh['group'=16,'mp'=32] {'mp'}, dimensions={0} | all-to-all | bytes 524288 | tf_op jit(solution)/shard_map/all_to_all | solution.py:421
  54.8 0.8 sum_parts.1
  55.5 0.0 copy-start.12
  55.5 0.0 copy-start.14
  55.5 0.0 copy-start.16
  55.5 4.0 %all-to-all-start.2 = ((bf16[32,32,128]{2,1,0:T(8,128)(2,1)}), bf16[32,32,128]{2,1,0:T(8,128)(2,1)S(1)}, u32[]{:S(2)}, u32[]{:S(2)}) async-start(bf16[32,32,128]{2,1,0:T(8,128)(2,1)} %sum_parts.1), calls=%async_computation.2 | async-start | bytes 524288 | tf_op jit(solution)/shard_map/all_to_all | solution.py:421
  59.6 0.0 copy-start.15
  59.6 0.0 copy-done.12
  59.6 0.0 copy-done.14
  59.6 0.0 copy-done.16
  59.6 0.6 copy-done.15
  60.2 0.0 copy-start.2
  60.2 0.2 prompt_prepare.1
  60.4 10.7 %all-to-all-done.2.rows_ref = bf16[32,32,128]{2,1,0:T(8,128)(2,1)S(1)} async-done(((bf16[32,32,128]{2,1,0:T(8,128)(2,1)}), bf16[32,32,128]{2,1,0:T(8,128)(2,1)S(1)}, u32[]{:S(2)}, u32[]{:S(2)}) %all-to-all-start.2) | async-done | bytes 262176 | tf_op jit(solution)/shard_map/all_to_all | solution.py:421
  71.1 0.0 copy-start.10
  71.1 0.0 copy-start.11
  71.1 0.0 copy-done.2
  71.1 0.6 copy-done.10
  71.8 0.0 copy-done.11
  71.8 3.1 %prefill_scan.1 = (bf16[8,16,512]{2,1,0:T(8,128)(2,1)}, bf16[16,40,512]{2,1,0:T(8,128)(2,1)}) custom-call(s32[8]{0:T(128)S(1)} %copy-done.10, s32[8]{0:T(128)S(1)} %bitcast.16, bf16[32,32,128]{2,1,0:T(8,128)(2,1)S(1)} %all-to-all-done.2.rows_ref, bf16[128,512]{1,0:T(8,128)(2,1)S(1)} %get-tuple-element.29.x_ref, f32[128,512]{1,0:T(8,128)S(1)} %get-tuple-element.30.gate_ref, ...), custom_call_target="tpu_custom_call" | custom-call | tf_op jit(solution)/shard_map/prefill_scan/pallas_call | solution.py:552
  74.9 5.8 %all-to-all-start.3 = ((bf16[16,40,512]{2,1,0:T(8,128)(2,1)}), bf16[16,40,512]{2,1,0:T(8,128)(2,1)S(1)}, u32[]{:S(2)}, u32[]{:S(2)}) async-start(bf16[16,40,512]{2,1,0:T(8,128)(2,1)} %get-tuple-element.34), calls=%async_computation.3 | async-start | bytes 1310720 | tf_op jit(solution)/shard_map/all_to_all | solution.py:421
  80.8 0.7 convert_bitcast_fusion
  81.4 0.0 copy-done
  81.4 0.2 copy-done.13
  81.6 0.6 decode_prepare.1
  82.2 18.6 %all-to-all-done.3.got_ref = bf16[16,40,512]{2,1,0:T(8,128)(2,1)S(1)} async-done(((bf16[16,40,512]{2,1,0:T(8,128)(2,1)}), bf16[16,40,512]{2,1,0:T(8,128)(2,1)S(1)}, u32[]{:S(2)}, u32[]{:S(2)}) %all-to-all-start.3) | async-done | bytes 655392 | tf_op jit(solution)/shard_map/all_to_all | solution.py:421
  100.8 2.7 %decode_scan.1 = (bf16[16,4,512]{2,1,0:T(4,128)(2,1)}, f32[16,16,512]{2,1,0:T(8,128)}, f32[32,16,512]{2,1,0:T(8,128)}) custom-call(s32[16]{0:T(128)S(1)} %copy-done.8, bf16[16,40,512]{2,1,0:T(8,128)(2,1)S(1)} %all-to-all-done.3.got_ref, bf16[64,512]{1,0:T(8,128)(2,1)S(1)} %get-tuple-element.35.x_ref, f32[64,512]{1,0:T(8,128)S(1)} %get-tuple-element.36.gate_ref, ...), custom_call_target="tpu_custom_call" | custom-call | tf_op jit(solution)/shard_map/decode_scan/pallas_call | solution.py:591
  (2 shorter events, 0.0 us)
Async XLA Ops:
  3.3 10.4 %copy-start.1 = (bf16[512,512]{1,0:T(8,128)(2,1)S(1)}, bf16[512,512]{1,0:T(8,128)(2,1)}, u32[]{:S(2)}) copy-start(bf16[512,512]{1,0:T(8,128)(2,1)} %rank_ref.3) | copy-start | bytes 1572868
  3.3 10.4 %copy-start.4 = (bf16[8,16,512]{2,1,0:T(8,128)(2,1)S(1)}, bf16[8,16,512]{2,1,0:T(8,128)(2,1)}, u32[]{:S(2)}) copy-start(bf16[8,16,512]{2,1,0:T(8,128)(2,1)} %u_ref.4) | copy-start | bytes 393220
  3.4 10.4 %copy-start.6 = (bf16[512,32]{0,1:T(8,128)(2,1)S(1)}, bf16[512,32]{0,1:T(8,128)(2,1)}, u32[]{:S(2)}) copy-start(bf16[512,32]{0,1:T(8,128)(2,1)} %param.29) | copy-start | bytes 98308
  3.4 10.4 %copy-start.7 = (f32[4,512]{1,0:T(4,128)S(1)}, f32[4,512]{1,0:T(4,128)}, u32[]{:S(2)}) copy-start(f32[4,512]{1,0:T(4,128)} %cw_ref.3) | copy-start | bytes 24580
  3.4 24.9 %all-to-all-start = ((bf16[16,24,512]{2,1,0:T(8,128)(2,1)}), bf16[16,24,512]{2,1,0:T(8,128)(2,1)S(1)}, u32[]{:S(2)}, u32[]{:S(2)}) async-start(bf16[16,24,512]{2,1,0:T(8,128)(2,1)} %pack.1), calls=%async_computation | async-start | bytes 786432 | tf_op jit(solution)/shard_map/all_to_all | solution.py:421
  13.7 0.7 copy-start.9
  14.4 13.9 %copy-start.3 = (bf16[16,3,512]{2,0,1:T(8,128)(2,1)S(1)}, bf16[16,3,512]{2,0,1:T(8,128)(2,1)}, u32[]{:S(2)}) copy-start(bf16[16,3,512]{2,0,1:T(8,128)(2,1)} %param.18) | copy-start | bytes 147460
  14.4 13.9 %copy-start.5 = (bf16[16,4,512]{2,1,0:T(4,128)(2,1)S(1)}, bf16[16,4,512]{2,1,0:T(4,128)(2,1)}, u32[]{:S(2)}) copy-start(bf16[16,4,512]{2,1,0:T(4,128)(2,1)} %u_ref.5) | copy-start | bytes 196612
  28.3 0.7 copy-start.8
  55.5 4.0 %copy-start.12 = (bf16[8,16,512]{2,1,0:T(8,128)(2,1)S(1)}, bf16[8,16,512]{2,1,0:T(8,128)(2,1)}, u32[]{:S(2)}) copy-start(bf16[8,16,512]{2,1,0:T(8,128)(2,1)} %gate_ref.2) | copy-start | bytes 393220
  55.5 4.1 %copy-start.14 = (f32[16,512]{1,0:T(8,128)S(1)}, f32[16,512]{1,0:T(8,128)}, u32[]{:S(2)}) copy-start(f32[16,512]{1,0:T(8,128)} %decay_ref.1) | copy-start | bytes 98308
  55.5 4.1 %copy-start.16 = (f32[512]{0:T(512)S(1)}, f32[512]{0:T(512)}, u32[]{:S(2)}) copy-start(f32[512]{0:T(512)} %param.33) | copy-start | bytes 6148
  55.5 15.6 %all-to-all-start.2 = ((bf16[32,32,128]{2,1,0:T(8,128)(2,1)}), bf16[32,32,128]{2,1,0:T(8,128)(2,1)S(1)}, u32[]{:S(2)}, u32[]{:S(2)}) async-start(bf16[32,32,128]{2,1,0:T(8,128)(2,1)} %sum_parts.1), calls=%async_computation.2 | async-start | bytes 524288 | tf_op jit(solution)/shard_map/all_to_all | solution.py:421
  59.6 0.7 copy-start.15
  60.2 10.9 %copy-start.2 = (bf16[512,512]{1,0:T(8,128)(2,1)S(1)}, bf16[512,512]{1,0:T(8,128)(2,1)}, u32[]{:S(2)}) copy-start(bf16[512,512]{1,0:T(8,128)(2,1)} %step_w_ref.3) | copy-start | bytes 1572868
  71.1 0.7 copy-start.10
  71.1 0.7 copy-start.11
  74.9 6.5 %copy-start = (f32[16,16,512]{2,1,0:T(8,128)S(1)}, f32[16,16,512]{2,1,0:T(8,128)}, u32[]{:S(2)}) copy-start(f32[16,16,512]{2,1,0:T(8,128)} %state_ref.3) | copy-start | bytes 1572868
  74.9 25.9 %all-to-all-start.3 = ((bf16[16,40,512]{2,1,0:T(8,128)(2,1)}), bf16[16,40,512]{2,1,0:T(8,128)(2,1)S(1)}, u32[]{:S(2)}, u32[]{:S(2)}) async-start(bf16[16,40,512]{2,1,0:T(8,128)(2,1)} %get-tuple-element.34), calls=%async_computation.3 | async-start | bytes 1310720 | tf_op jit(solution)/shard_map/all_to_all | solution.py:421
  80.8 0.8 copy-start.13

commit v3 on v2

v3 whole, which is shorter than its diff:
```python
import jax
import jax.numpy as jnp
from jax import lax
from jax.experimental import pallas as pl
from jax.experimental.pallas import tpu as pltpu
from jax.sharding import PartitionSpec as P

MIG = 4
PAIR = 2
EPS = 1e-06
LANES = 128
ROWS0 = 24
PROMPT_GROUPS = 16
STATE_ROW = 14
TAIL_ROW = 18
LOG2E = 1.4426950408889634

F32 = jnp.float32
BF16 = jnp.bfloat16
VMEM = pl.BlockSpec(memory_space=pltpu.VMEM)
SMEM = pl.BlockSpec(memory_space=pltpu.SMEM)
PARAMS = pltpu.CompilerParams(vmem_limit_bytes=40 * 1024 * 1024)
ALL_VMEM = pltpu.CompilerParams(vmem_limit_bytes=60 * 1024 * 1024)


def silu(x):
    return x / (1.0 + jnp.exp(-x))


def softplus(x):
    return jnp.maximum(x, 0.0) + jnp.log1p(jnp.exp(-jnp.abs(x)))


def iota(shape, dim):
    return lax.broadcasted_iota(jnp.int32, shape, dim)


def from_scalars(ref, count, shape, first=0):
    rows = iota(shape, 0)
    out = jnp.zeros(shape, jnp.int32)
    for i in range(count):
        out = jnp.where(rows == i, ref[first + i], out)
    return out


def slots_of(dest_ref, count, first=0):
    dests = [dest_ref[first + i] for i in range(count)]
    ranks = []
    for i in range(count):
        rank = jnp.int32(0)
        for j in range(i):
            rank = rank + (dests[j] == dests[i]).astype(jnp.int32)
        ranks.append(rank)
    return dests, ranks


def picks_of(mig_ref, reqs):
    own = lax.axis_index("group")
    count = jnp.int32(0)
    picks = [jnp.int32(0) for _ in range(MIG)]
    for r in range(reqs):
        moved = mig_ref[r] != own * reqs + r
        for k in range(MIG):
            picks[k] = jnp.where(moved & (count == k), r, picks[k])
        count = count + moved.astype(jnp.int32)
    return own, picks


def pack_kernel(
    mig_ref, dest_ref, len_ref, conv_ref, state_ref, u_ref, pay_ref, scr, conv_scr, u_scr
):
    groups = pay_ref.shape[0]
    _, reqs, channels = conv_ref.shape
    prompts, steps, _ = u_ref.shape
    states = state_ref.shape[1]
    own, picks = picks_of(mig_ref, reqs)
    base = scr.at[groups]
    base[...] = jnp.zeros(base.shape, F32)
    lane = iota((1, channels), 1)
    ids = jnp.zeros((1, channels), jnp.int32)
    wanted = jnp.zeros((1, channels), jnp.int32)
    for j in range(3):
        conv_scr[j * reqs : (j + 1) * reqs, :] = conv_ref[j].astype(F32)
    for k in range(MIG):
        for at in (k, 4 + k, 8 + k, STATE_ROW + k):
            ids = jnp.where(lane == own * ROWS0 + at, own * reqs + picks[k], ids)
        wanted = jnp.where(lane == own * MIG + k, mig_ref[picks[k]], wanted)
        for j in range(3):
            at = 4 * j + k
            base[at : at + 1, :] = conv_scr[pl.ds(j * reqs + picks[k], 1), :]
    base[12:13, :] = ids.astype(F32)
    base[13:14, :] = wanted.astype(F32)
    for d in range(groups):
        scr[d] = base[...]
    dests, ranks = slots_of(dest_ref, prompts)
    pad = u_scr.shape[0] // prompts
    for i in range(prompts):
        u_scr[i * pad : i * pad + 8, :] = jnp.zeros((8, channels), F32)
        u_scr[i * pad + 8 : i * pad + 8 + steps, :] = u_ref[i].astype(F32)
    for i in range(prompts):
        tails = [u_scr[pl.ds(i * pad + 5 + j + len_ref[i], 1), :] for j in range(3)]
        for q in range(PAIR):

            @pl.when(ranks[i] == q)
            def _():
                for j in range(3):
                    at = TAIL_ROW + 3 * q + j
                    scr[dests[i], at : at + 1, :] = tails[j]

    for k in range(MIG):
        state = state_ref[picks[k]]
        for n in range(states):
            scr[n, STATE_ROW + k : STATE_ROW + k + 1, :] = state[n : n + 1, :]
    for d in range(groups):
        pay_ref[d] = scr[d].astype(BF16)


def put_lanes(ref, start, value):
    for l in range(ref.shape[0]):
        ref[l, start : start + value.shape[0], :] = value[:, l * LANES : (l + 1) * LANES]


def project(x, rank_ref, select_ref):
    low = jnp.dot(x, rank_ref[...], preferred_element_type=F32)
    sel = lax.dot_general(
        x, select_ref[...], (((1,), (1,)), ((), ())), preferred_element_type=F32
    )
    return low, sel


def put_tiles(scr, first, low, sel):
    tiles = low.shape[1] // LANES
    width = sel.shape[1]
    share = LANES // width
    for g in range(low.shape[0] // 8):
        rows = slice(8 * g, 8 * g + 8)
        for l in range(tiles):
            owner, place = divmod((first + g) * tiles + l, 3)
            scr[owner, 8 * place : 8 * place + 8, :] = low[rows, l * LANES : (l + 1) * LANES]
        pair, place = divmod(first + g, share)
        cols = slice(place * width, (place + 1) * width)
        scr[2 * pair, 24:28, cols] = sel[8 * g : 8 * g + 4]
        scr[2 * pair + 1, 24:28, cols] = sel[8 * g + 4 : 8 * g + 8]


def take_tiles(rows_ref, first, low_scr, sel_scr):
    count, channels = low_scr.shape
    tiles = channels // LANES
    for g in range(count // 8):
        upper, lower = slice(8 * g, 8 * g + 4), slice(8 * g + 4, 8 * g + 8)
        for l in range(tiles):
            cols = slice(l * LANES, (l + 1) * LANES)
            owner, place = divmod((first + g) * tiles + l, 3)
            low_scr[upper, cols] = rows_ref[owner, 2 * place].astype(F32)
            low_scr[lower, cols] = rows_ref[owner, 2 * place + 1].astype(F32)
        pair, place = divmod(first + g, 4)
        sel_scr[upper, :] = rows_ref[2 * pair, 6].astype(F32)
        sel_scr[lower, :] = rows_ref[2 * pair + 1, 6].astype(F32)
    for g in range(count // 8):
        place = (first + g) % 4
        if place:
            rows = slice(8 * g, 8 * g + 8)
            sel_scr[rows, :] = pltpu.roll(sel_scr[rows, :], LANES - 32 * place, 1)


def prompt_kernel(
    mig_ref, dest_ref, len_ref, u_ref, gate_ref, cw_ref, cb_ref, rank_ref, select_ref, decay_ref,
    step_b_ref, skip_ref, low_ref, sel_ref, x_ref, gate_out_ref, decay_out_ref, extra_ref,
    plan_ref, scr, x_scr,
):
    prompts, steps, channels = u_ref.shape
    reqs = mig_ref.shape[0]
    for i in range(reqs):
        plan_ref[i] = mig_ref[i]
    for i in range(prompts):
        plan_ref[reqs + i] = dest_ref[i]
        plan_ref[reqs + prompts + i] = len_ref[i]
    extra_ref[0:1, :] = step_b_ref[...]
    extra_ref[1:2, :] = skip_ref[...]
    extra_ref[2:3, :] = cb_ref[...]
    extra_ref[3:8, :] = jnp.zeros((5, channels), F32)
    decay = jnp.exp(decay_ref[...]) * -LOG2E
    for n in range(decay.shape[0]):
        put_lanes(decay_out_ref, 8 * n, jnp.broadcast_to(decay[n : n + 1], (8, channels)))
    for i in range(prompts):
        put_lanes(scr, i * steps, silu(gate_ref[i].astype(F32)))
    for l in range(channels // LANES):
        cols = slice(l * LANES, (l + 1) * LANES)
        for t in range(steps):
            gate_out_ref[t * prompts : (t + 1) * prompts, cols] = scr[
                l, pl.ds(t, prompts, stride=steps), :
            ]
    for i in range(prompts):
        put_lanes(scr, i * steps, u_ref[i].astype(F32))
    for l in range(channels // LANES):
        cols = slice(l * LANES, (l + 1) * LANES)
        taps = [cw_ref[k : k + 1, cols] for k in range(4)]
        bias = cb_ref[:, cols]
        window = [jnp.zeros((prompts, LANES), F32) for _ in range(3)]
        for t in range(steps):
            window.append(scr[l, pl.ds(t, prompts, stride=steps), :])
            acc = bias
            for k in range(4):
                acc = acc + taps[k] * window[t + k]
            x_scr[t * prompts : (t + 1) * prompts, cols] = silu(acc)
    x = x_scr[...].astype(BF16)
    x_ref[...] = x
    low, sel = project(x, rank_ref, select_ref)
    low_ref[...] = low
    sel_ref[...] = sel


def decode_kernel(
    plan_ref, got_ref, conv_ref, u_ref, cw_ref, extra_ref, rank_ref, select_ref, prompt_low_ref,
    prompt_sel_ref, pay_ref, x_ref, pass_ref, pool_scr, pay_scr, scr, x_scr,
):
    groups = got_ref.shape[0]
    reqs, steps, channels = u_ref.shape
    table = groups * ROWS0
    own = lax.axis_index("group")
    marks = jnp.zeros((8, channels), F32)
    for s in range(groups):
        block = got_ref[s].astype(F32)
        pool_scr[s * ROWS0 : (s + 1) * ROWS0, :] = block
        marks = marks + block[8:16]
    for r in range(reqs):
        put_lanes(scr, 8 * r, u_ref[r].astype(F32))
    pool = pool_scr[...].astype(BF16)
    ids = marks[4:5, :table]
    place = lax.rem(iota((1, table), 1), ROWS0)
    moves = groups * MIG
    square = (moves, LANES)
    wanted = jnp.sum(
        jnp.where(
            iota(square, 0) == iota(square, 1), jnp.broadcast_to(marks[5:6, :LANES], square), 0.0
        ),
        axis=1,
        keepdims=True,
    )
    passed = (wanted == ids) & (place >= STATE_ROW) & (place < STATE_ROW + MIG)
    relay = jnp.dot(jnp.where(passed, 1.0, 0.0).astype(BF16), pool, preferred_element_type=F32)
    for d in range(groups):
        pass_ref[d] = relay[d * MIG : (d + 1) * MIG].astype(BF16)
    wide = (reqs, channels)
    moved_wide = from_scalars(plan_ref, reqs, wide) != own * reqs + iota(wide, 0)
    shape = (reqs, table)
    needs = from_scalars(plan_ref, reqs, shape)
    found = (needs != own * reqs + iota(shape, 0)) & (
        jnp.broadcast_to(ids, shape) == needs.astype(F32)
    )
    hist = []
    for j in range(3):
        hit = jnp.where(found & (place >= 4 * j) & (place < 4 * j + 4), 1.0, 0.0).astype(BF16)
        taken = jnp.dot(hit, pool, preferred_element_type=F32)
        hist.append(jnp.where(moved_wide, taken, conv_ref[j].astype(F32)))
    for l in range(channels // LANES):
        cols = slice(l * LANES, (l + 1) * LANES)
        taps = [cw_ref[k : k + 1, cols] for k in range(4)]
        bias = extra_ref[2:3, cols]
        window = [hist[j][:, cols] for j in range(3)]
        for t in range(steps):
            window.append(scr[l, pl.ds(t, reqs, stride=8), :])
            acc = bias
            for k in range(4):
                acc = acc + taps[k] * window[t + k]
            x_scr[t * reqs : (t + 1) * reqs, cols] = silu(acc)
    x = x_scr[...].astype(BF16)
    x_ref[...] = x
    low, sel = project(x, rank_ref, select_ref)
    prompt_groups = prompt_low_ref.shape[0] // 8
    pay_scr[...] = jnp.zeros(pay_scr.shape, F32)
    put_tiles(pay_scr, 0, prompt_low_ref[...], prompt_sel_ref[...])
    put_tiles(pay_scr, prompt_groups, low, sel)
    peers, blocks, four, _ = pay_ref.shape
    for j in range(peers):
        for a in range(blocks):
            pay_ref[j, a] = pay_scr[j, four * a : four * (a + 1), :].astype(BF16)


def sum_kernel(got_ref, out_ref):
    total = got_ref[0].astype(F32)
    for j in range(1, got_ref.shape[0]):
        total = total + got_ref[j].astype(F32)
    own_rows = total.astype(BF16)
    for j in range(out_ref.shape[0]):
        out_ref[j] = own_rows


def steps_of(low_scr, step_w_ref, step_b):
    low = low_scr[...]
    scale = lax.rsqrt(jnp.mean(low * low, axis=-1, keepdims=True) + EPS)
    raw = jnp.dot(low.astype(BF16), step_w_ref[...], preferred_element_type=F32)
    return softplus(raw * scale + step_b)


def scan(t, items, live, x, gate, sel, step, decay, skip, h_scr, y_scr, y_stride):
    states = decay.shape[1] // 8
    for g in range(items // 8):
        rows = slice(t * items + 8 * g, t * items + 8 * g + 8)
        alive = None if live is None else live[8 * g : 8 * g + 8]
        pair = sel[rows, :]
        lanes = range(h_scr.shape[0])
        steps, drive, y = [], [], []
        for l in lanes:
            cols = slice(l * LANES, (l + 1) * LANES)
            step_l = step[rows, cols]
            if alive is not None:
                step_l = jnp.where(alive, step_l, 0.0)
            x_l = x[rows, cols]
            steps.append(step_l)
            drive.append(step_l * x_l)
            y.append(skip[:, cols] * x_l)
        for n in range(states):
            b = jnp.broadcast_to(pair[:, n : n + 1], (8, LANES))
            c = jnp.broadcast_to(pair[:, states + n : states + n + 1], (8, LANES))
            at = slice(n * items + 8 * g, n * items + 8 * g + 8)
            for l in lanes:
                keep = jnp.exp2(steps[l] * decay[l, 8 * n : 8 * n + 8, :])
                h = keep * h_scr[l, at, :] + drive[l] * b
                h_scr[l, at, :] = h
                y[l] = y[l] + c * h
        for l in lanes:
            cols = slice(l * LANES, (l + 1) * LANES)
            out = y[l] * gate[rows, cols]
            if alive is not None:
                out = jnp.where(alive, out, 0.0)
            y_scr[l, pl.ds(8 * g * y_stride + t, 8, stride=y_stride), :] = out


def prefill_kernel(
    plan_ref, rows_ref, x_ref, gate_ref, step_w_ref, decay_ref, extra_ref, relay_ref,
    out_ref, pay_ref, low_scr, sel_scr, step_scr, x_scr, h_scr, y_scr,
):
    prompts, steps, channels = out_ref.shape
    states = decay_ref.shape[1] // 8
    reqs = plan_ref.shape[0] - 2 * prompts
    take_tiles(rows_ref, 0, low_scr, sel_scr)
    step_scr[...] = steps_of(low_scr, step_w_ref, extra_ref[0:1, :])
    x_scr[...] = x_ref[...].astype(F32)
    h_scr[...] = jnp.zeros(h_scr.shape, F32)
    lengths = from_scalars(plan_ref, prompts, (prompts, LANES), reqs + prompts)
    skip = extra_ref[1:2, :]
    for t in range(steps):
        scan(
            t, prompts, t < lengths, x_scr, gate_ref, sel_scr, step_scr, decay_ref, skip, h_scr,
            y_scr, steps,
        )
    dests, ranks = slots_of(plan_ref, prompts, reqs)
    groups, blocks, four, _ = pay_ref.shape
    parts = states // four
    for d in range(groups):
        pay_ref[d, : blocks - 1] = jnp.zeros((blocks - 1, four, channels), BF16)
        pay_ref[d, blocks - 1] = relay_ref[d]
    for i in range(prompts):
        at = ranks[i] * parts
        for l in range(channels // LANES):
            cols = slice(l * LANES, (l + 1) * LANES)
            out_ref[i, :, cols] = y_scr[l, i * steps : (i + 1) * steps, :].astype(BF16)
            final = h_scr[l, pl.ds(i, states, stride=prompts), :]
            for p in range(parts):
                pay_ref[dests[i], at + p, :, cols] = final[p * four : (p + 1) * four].astype(BF16)


def decode_scan_kernel(
    plan_ref, rows_ref, x_ref, u_ref, gate_ref, state_ref, step_w_ref, decay_ref, extra_ref,
    got_ref, out_ref, final_ref, base_ref, held_ref, weight_ref, keep_ref, pick_ref,
    final_conv_ref, prompt_conv_ref, low_scr, sel_scr, step_scr, x_scr, gate_scr, scr, h_scr, y_scr,
    conv_scr,
):
    reqs, steps, channels = gate_ref.shape
    states = state_ref.shape[1]
    lanes = channels // LANES
    own, picks = picks_of(plan_ref, reqs)
    take_tiles(rows_ref, PROMPT_GROUPS, low_scr, sel_scr)
    step_scr[...] = steps_of(low_scr, step_w_ref, extra_ref[0:1, :])
    x_scr[...] = x_ref[...].astype(F32)
    for r in range(reqs):
        put_lanes(scr, 8 * r, silu(gate_ref[r].astype(F32)))
        kept = plan_ref[r] == own * reqs + r
        for l in range(lanes):
            cols = slice(l * LANES, (l + 1) * LANES)
            h_scr[l, pl.ds(r, states, stride=reqs), :] = jnp.where(
                kept, state_ref[r, :, cols], 0.0
            )
    for l in range(lanes):
        cols = slice(l * LANES, (l + 1) * LANES)
        for t in range(steps):
            gate_scr[t * reqs : (t + 1) * reqs, cols] = scr[l, pl.ds(t, reqs, stride=8), :]
    skip = extra_ref[1:2, :]
    for t in range(steps):
        scan(t, reqs, None, x_scr, gate_scr, sel_scr, step_scr, decay_ref, skip, h_scr, y_scr, 8)
    for r in range(reqs):
        final_conv_ref[:, r : r + 1, :] = u_ref[r].astype(F32)[1:4].reshape(3, 1, channels)
        for l in range(lanes):
            cols = slice(l * LANES, (l + 1) * LANES)
            final_ref[r, :, cols] = h_scr[l, pl.ds(r, states, stride=reqs), :]
            out_ref[r, :, cols] = y_scr[l, 8 * r : 8 * r + steps, :].astype(BF16)
    outward = jnp.transpose(sel_scr[...])[states : 2 * states]
    column = iota(outward.shape, 1)
    for k in range(MIG):
        pick_ref[k : k + 1, :] = jnp.broadcast_to(picks[k], (1, LANES)).astype(F32)
        held_ref[k] = final_ref[picks[k]]
        total = jnp.zeros((1, channels), F32)
        for t in range(steps):
            row = t * reqs + picks[k]
            total = total + step_scr[pl.ds(row, 1), :]
            gate = gate_scr[pl.ds(row, 1), :]
            c = jnp.sum(jnp.where(column == row, outward, 0.0), axis=1, keepdims=True)
            for l in range(lanes):
                cols = slice(l * LANES, (l + 1) * LANES)
                keep = jnp.exp2(total[:, cols] * decay_ref[l, pl.ds(0, states, stride=8), :])
                weight_ref[k * steps + t, :, cols] = keep * c * gate[:, cols]
                base_ref[k * steps + t : k * steps + t + 1, cols] = y_scr[
                    l, pl.ds(8 * picks[k] + t, 1), :
                ]
                if t == steps - 1:
                    keep_ref[k, :, cols] = keep
    pick_ref[MIG:, :] = jnp.zeros((pick_ref.shape[0] - MIG, LANES), F32)
    for s in range(got_ref.shape[0]):
        block = got_ref[s].astype(F32)
        for q in range(PAIR):
            for j in range(3):
                at = TAIL_ROW + 3 * q + j
                conv_scr[j, s * PAIR + q : s * PAIR + q + 1, :] = block[at : at + 1]
    prompt_conv_ref[...] = conv_scr[...].astype(BF16)


def finish_kernel(
    got_ref, base_ref, held_ref, weight_ref, keep_ref, pick_ref, _out, _final, out_ref, final_ref,
    prompt_state_ref, state_scr, moved_scr, out_scr, final_scr, sems,
):
    groups, blocks, four, channels = got_ref.shape
    slots, states, _ = state_scr.shape
    steps = base_ref.shape[0] // MIG
    lanes = channels // LANES
    parts = states // four
    copies = []
    for n in range(states):
        put_lanes(moved_scr, n * MIG, got_ref[n, blocks - 1].astype(F32))
    for k in range(MIG):
        pick = jnp.max(pick_ref[k : k + 1, :]).astype(jnp.int32)
        for l in range(lanes):
            cols = slice(l * LANES, (l + 1) * LANES)
            start = moved_scr[l, pl.ds(k, states, stride=MIG), :]
            final_scr[k, :, cols] = held_ref[k, :, cols] + keep_ref[k, :, cols] * start
            rows = []
            for t in range(steps):
                at = k * steps + t
                more = jnp.sum(weight_ref[at, :, cols] * start, axis=0, keepdims=True)
                rows.append(base_ref[at : at + 1, cols] + more)
            out_scr[k, :, cols] = jnp.concatenate(rows, axis=0).astype(BF16)
        copies.append(
            pltpu.make_async_copy(final_scr.at[k], final_ref.at[pick], sems.at[groups + k])
        )
        copies.append(
            pltpu.make_async_copy(out_scr.at[k], out_ref.at[pick], sems.at[groups + MIG + k])
        )
        copies[-2].start()
        copies[-1].start()
    for s in range(groups):
        for q in range(PAIR):
            for p in range(parts):
                state_scr[s * PAIR + q, p * four : (p + 1) * four, :] = got_ref[
                    s, q * parts + p
                ].astype(F32)
        here = pl.ds(s * PAIR, PAIR)
        copies.append(
            pltpu.make_async_copy(state_scr.at[here], prompt_state_ref.at[here], sems.at[s])
        )
        copies[-1].start()
    for copy in copies:
        copy.wait()


def exchange(value, axis):
    return lax.all_to_all(value, axis, split_axis=0, concat_axis=0, tiled=True)


def on_device(
    resident_state,
    resident_conv,
    migrate_from,
    decode_inputs,
    decode_gates,
    prompt_inputs,
    prompt_gates,
    prompt_length,
    prompt_dest,
    conv_weight,
    conv_bias,
    rank_weight,
    select_weight,
    step_weight,
    step_bias,
    decay_log,
    skip_gain,
):
    groups = lax.axis_size("group")
    peers = lax.axis_size("mp")
    reqs, states, channels = resident_state.shape
    prompts, steps, _ = prompt_inputs.shape
    decode_steps = decode_inputs.shape[1]
    tiles = channels // LANES
    rank = rank_weight.shape[1]
    selects = select_weight.shape[1]
    prompt_rows = prompts * steps
    decode_rows = reqs * decode_steps
    bias_row = conv_bias.reshape(1, channels)
    step_bias_row = step_bias.reshape(1, channels)
    skip_row = skip_gain.reshape(1, channels)

    def struct(shape, dtype):
        return jax.ShapeDtypeStruct(shape, dtype)

    def scratch(shape):
        return pltpu.VMEM(shape, F32)

    def cost(flops, size):
        return pl.CostEstimate(flops=flops, bytes_accessed=size, transcendentals=0)

    dest = prompt_dest.reshape(prompts)
    conv_rows = jnp.transpose(resident_conv, (1, 0, 2))
    select_rows = jnp.transpose(select_weight)

    send_first = pl.pallas_call(
        pack_kernel,
        out_shape=struct((groups, ROWS0, channels), BF16),
        in_specs=[SMEM] * 3 + [VMEM] * 3,
        out_specs=VMEM,
        scratch_shapes=[
            scratch((groups + 1, ROWS0, channels)),
            scratch((3 * reqs, channels)),
            scratch((prompts * (steps + 8), channels)),
        ],
        compiler_params=ALL_VMEM,
        name="pack",
    )(migrate_from, dest, prompt_length, conv_rows, resident_state, prompt_inputs)
    got_first = exchange(send_first, "group")

    prompt_low, prompt_sel, prompt_x, gate_rows, decay, extra, plan = pl.pallas_call(
        prompt_kernel,
        out_shape=(
            struct((prompt_rows, rank), F32),
            struct((prompt_rows, selects), F32),
            struct((prompt_rows, channels), BF16),
            struct((prompt_rows, channels), F32),
            struct((tiles, 8 * states, LANES), F32),
            struct((8, channels), F32),
            struct((reqs + 2 * prompts,), jnp.int32),
        ),
        in_specs=[SMEM] * 3 + [VMEM] * 9,
        out_specs=(VMEM,) * 6 + (SMEM,),
        scratch_shapes=[scratch((tiles, prompt_rows, LANES)), scratch((prompt_rows, channels))],
        compiler_params=PARAMS,
        cost_estimate=cost(10**9, 2 * 10**6),
        name="prompt_features",
    )(
        migrate_from, dest, prompt_length, prompt_inputs, prompt_gates, conv_weight, bias_row,
        rank_weight, select_rows, decay_log, step_bias_row, skip_row,
    )

    pay, decode_x, relay = pl.pallas_call(
        decode_kernel,
        out_shape=(
            struct((peers, 7, 4, LANES), BF16),
            struct((decode_rows, channels), BF16),
            struct((groups, MIG, channels), BF16),
        ),
        in_specs=[SMEM] + [VMEM] * 9,
        out_specs=(VMEM,) * 3,
        scratch_shapes=[
            scratch((groups * ROWS0, channels)),
            scratch((peers, 32, LANES)),
            scratch((tiles, reqs * 8, LANES)),
            scratch((decode_rows, channels)),
        ],
        compiler_params=PARAMS,
        name="decode_features",
    )(
        plan, got_first, conv_rows, decode_inputs, conv_weight, extra, rank_weight, select_rows,
        prompt_low, prompt_sel,
    )

    parts = exchange(pay, "mp")
    shares = pl.pallas_call(
        sum_kernel,
        out_shape=struct(parts.shape, BF16),
        in_specs=[VMEM],
        out_specs=VMEM,
        compiler_params=PARAMS,
        name="sum_parts",
    )(parts)
    rows = exchange(shares, "mp")

    prefill_out, send_final = pl.pallas_call(
        prefill_kernel,
        out_shape=(
            struct(prompt_inputs.shape, BF16),
            struct((groups, PAIR * states // MIG + 1, MIG, channels), BF16),
        ),
        in_specs=[SMEM] + [VMEM] * 7,
        out_specs=(VMEM, VMEM),
        scratch_shapes=[
            scratch((prompt_rows, rank)),
            scratch((prompt_rows, LANES)),
            scratch((prompt_rows, channels)),
            scratch((prompt_rows, channels)),
            scratch((tiles, prompts * states, LANES)),
            scratch((tiles, prompt_rows, LANES)),
        ],
        compiler_params=PARAMS,
        name="prefill_scan",
    )(plan, rows, prompt_x, gate_rows, step_weight, decay, extra, relay)
    got_final = exchange(send_final, "group")

    early_out, early_final, base, held, weight, keep, pick, final_conv, prompt_conv = pl.pallas_call(
        decode_scan_kernel,
        out_shape=(
            struct(decode_inputs.shape, BF16),
            struct(resident_state.shape, F32),
            struct((MIG * decode_steps, channels), F32),
            struct((MIG, states, channels), F32),
            struct((MIG * decode_steps, states, channels), F32),
            struct((MIG, states, channels), F32),
            struct((8, LANES), F32),
            struct((3, reqs, channels), F32),
            struct((3, groups * PAIR, channels), BF16),
        ),
        in_specs=[SMEM] + [VMEM] * 9,
        out_specs=(VMEM,) * 9,
        scratch_shapes=[
            scratch((decode_rows, rank)),
            scratch((decode_rows, LANES)),
            scratch((decode_rows, channels)),
            scratch((decode_rows, channels)),
            scratch((decode_rows, channels)),
            scratch((tiles, reqs * 8, LANES)),
            scratch((tiles, reqs * states, LANES)),
            scratch((tiles, reqs * 8, LANES)),
            scratch((3, groups * PAIR, channels)),
        ],
        compiler_params=PARAMS,
        cost_estimate=cost(6 * 10**9, 8 * 10**6),
        name="decode_scan",
    )(
        plan, rows, decode_x, decode_inputs, decode_gates, resident_state, step_weight, decay,
        extra, got_first,
    )

    anywhere = pl.BlockSpec(memory_space=pl.ANY)
    decode_out, final_state, prompt_state = pl.pallas_call(
        finish_kernel,
        out_shape=(
            struct(decode_inputs.shape, BF16),
            struct(resident_state.shape, F32),
            struct((groups * PAIR, states, channels), F32),
        ),
        in_specs=[VMEM] * 6 + [anywhere] * 2,
        out_specs=(anywhere,) * 3,
        scratch_shapes=[
            scratch((groups * PAIR, states, channels)),
            scratch((tiles, states * MIG, LANES)),
            pltpu.VMEM((MIG, decode_steps, channels), BF16),
            scratch((MIG, states, channels)),
            pltpu.SemaphoreType.DMA((groups + 2 * MIG,)),
        ],
        input_output_aliases={6: 0, 7: 1},
        compiler_params=PARAMS,
        name="finish",
    )(got_final, base, held, weight, keep, pick, early_out, early_final)
    final_conv = jnp.transpose(final_conv, (1, 0, 2)).astype(BF16)
    prompt_conv = jnp.transpose(prompt_conv, (1, 0, 2))
    return (decode_out, final_state, final_conv, prefill_out, prompt_state, prompt_conv)


def solution(mesh):
    whole = P("group", None, "mp")
    return jax.shard_map(
        on_device,
        mesh=mesh,
        in_specs=(
            whole,
            whole,
            P("group"),
            whole,
            whole,
            whole,
            whole,
            P("group"),
            P("group", None),
            P(None, "mp"),
            P("mp"),
            P("mp", None),
            P("mp", None),
            P(None, "mp"),
            P("mp"),
            P(None, "mp"),
            P("mp"),
        ),
        out_specs=(whole,) * 6,
        check_vma=False,
    )
```

time: 104 us -> 96.6 us (0.929)
  waiting for transfers between devices: 42.8 us -> 26.6 us
  blocking collectives: 24 us -> 38.2 us
  starting transfers between devices: 20.2 us -> 16 us
  local copies, waits for them, and re-layouts: 2.83 us -> 1.49 us
    all_to_all x3 -> x2, waiting for transfers between devices: 42.8 us -> 26.6 us  [exchange(): return lax.all_to_all(value, axis, split_axis=0, concat_axis=0, tiled=True)]
    all_to_all x1 -> x2, blocking collectives: 24 us -> 38.2 us  [exchange(): return lax.all_to_all(value, axis, split_axis=0, concat_axis=0, tiled=True)]
    all_to_all x3 -> x2, starting transfers between devices: 20.2 us -> 16 us  [exchange(): return lax.all_to_all(value, axis, split_axis=0, concat_axis=0, tiled=True)]
    unnamed x34 -> x38, local copies, waits for them, and re-layouts: 2.83 us -> 1.49 us
    pallas_call x1, Pallas kernels: 0.39 us -> 1.57 us  [on_device(): pl.pallas_call(prompt_kernel, out_shape=(struct((prompt_rows, rank), F32)...]
    pallas_call x3 -> x2, Pallas kernels: 2.53 us -> 2.61 us  [the longest x1 1.33 us: on_device(): pl.pallas_call(finish_kernel, out_shape=(struct(decode_inputs.shape, BF16...]
  transfers between devices with their start and end apart: 3 -> 2, of which waited for: 3 -> 2; matrix products, arithmetic and copies ran while one was open for 1% -> 1% of each run, Pallas kernels for 1% -> 5%
where the time goes in v3:
time: 96.6 us; the launch traced here: 96.1 us
  blocking collectives  38.2 us (40%)
  waiting for transfers between devices  26.6 us (28%)
  starting transfers between devices  16 us (17%)
  Pallas kernels  12.4 us (13%)
  local copies, waits for them, and re-layouts  1.49 us (2%)
    all_to_all x2, blocking collectives, exchange(): return lax.all_to_all(value, axis, split_axis=0, concat_axis=0, tiled=True)  38.2 us
    all_to_all x2, waiting for transfers between devices, exchange(): return lax.all_to_all(value, axis, split_axis=0, concat_axis=0, tiled=True)  26.6 us
    all_to_all x2, starting transfers between devices, exchange(): return lax.all_to_all(value, axis, split_axis=0, concat_axis=0, tiled=True)  16 us
    pallas_call x1, Pallas kernels, on_device(): pl.pallas_call(prefill_kernel, out_shape=(struct(prompt_inputs.shape, BF1...  3.08 us
    pallas_call x1, Pallas kernels, on_device(): pl.pallas_call(decode_scan_kernel, out_shape=(struct(decode_inputs.shape,...  2.82 us
    pallas_call x1, Pallas kernels, on_device(): pl.pallas_call(pack_kernel, out_shape=struct((groups, ROWS0, channels), B...  2.21 us
  transfers between devices with their start and end apart: 2, of which 2 were waited for; matrix products, arithmetic and copies ran while one was open for 1% of the time, Pallas kernels for 5%

profile of v3, /device:TPU:1, one launch (start us, length us, event | category | flops | bytes accessed | tf_op | source)
XLA Modules:
  0.0 96.1 jit_solution(12972711944295008152)
XLA Ops:
  0.6 0.0 copy-start.11
  0.6 2.2 %pack.1 = bf16[16,24,512]{2,1,0:T(8,128)(2,1)} custom-call(s32[16]{0:T(128)} %mig_ref.3, s32[8]{0:T(128)} %bitcast.13, s32[8]{0:T(128)} %len_ref.3, bf16[3,16,512]{2,1,0:T(8,128)(2,1)} %bitcast.9, f32[16,16,512]{2,1,0:T(8,128)} %state_ref.3, bf16[8,16,512]{2,1,0:T(8,128)(2,1)} %u_ref.5), custom_call_target="tpu_custom_call" | custom-call | tf_op jit(solution)/shard_map/pack/pallas_call | solution.py:525
  2.8 0.0 copy-start
  2.9 0.0 copy-start.6
  2.9 0.0 copy-start.7
  2.9 0.0 copy-start.15
  2.9 0.0 copy-start.17
  2.9 0.0 copy-start.18
  2.9 10.4 %all-to-all-start = ((bf16[16,24,512]{2,1,0:T(8,128)(2,1)}), bf16[16,24,512]{2,1,0:T(8,128)(2,1)S(1)}, u32[]{:S(2)}, u32[]{:S(2)}) async-start(bf16[16,24,512]{2,1,0:T(8,128)(2,1)} %pack.1), calls=%async_computation | async-start | bytes 786432 | tf_op jit(solution)/shard_map/all_to_all | solution.py:476
  13.3 0.0 copy-start.16
  13.3 0.0 copy-start.8
  13.3 0.0 copy-start.9
  13.3 0.0 copy-start.10
  13.3 0.0 copy-done.11
  13.3 0.0 copy-done
  13.3 0.0 copy-done.4
  13.3 0.0 copy-done.6
  13.4 0.0 copy-done.7
  13.4 0.0 copy-done.15
  13.4 0.0 copy-done.17
  13.4 0.0 copy-done.18
  13.4 0.6 copy-done.16
  13.9 0.0 copy-done.8
  14.0 0.0 copy-done.9
  14.0 0.0 copy-done.10
  14.0 0.0 copy-start.3
  14.0 0.0 copy-start.5
  14.0 1.6 %prompt_features.1 = (f32[128,512]{1,0:T(8,128)S(1)}, f32[128,32]{1,0:T(8,128)S(1)}, bf16[128,512]{1,0:T(8,128)(2,1)S(1)}, f32[128,512]{1,0:T(8,128)S(1)}, f32[4...) custom-call(s32[16]{0:T(128)S(1)} %copy-done.8, s32[8]{0:T(128)S(1)} %bitcast.14, s32[8]{0:T(128)S(1)} %copy-done.10, ...), custom_call_target="tpu_custom_call" | custom-call | flops 1000000000 | bytes 2000000 | tf_op jit(solution)/shard_map/prompt_features/pallas_call | solution.py:540
  15.6 12.3 %all-to-all-done.got_ref = bf16[16,24,512]{2,1,0:T(8,128)(2,1)S(1)} async-done(((bf16[16,24,512]{2,1,0:T(8,128)(2,1)}), bf16[16,24,512]{2,1,0:T(8,128)(2,1)S(1)}, u32[]{:S(2)}, u32[]{:S(2)}) %all-to-all-start) | async-done | bytes 393248 | tf_op jit(solution)/shard_map/all_to_all | solution.py:476
  27.8 0.0 copy-done.3
  27.8 0.0 copy-done.5
  27.8 1.3 %decode_features.1 = (bf16[32,7,4,128]{3,2,1,0:T(4,128)(2,1)S(1)}, bf16[64,512]{1,0:T(8,128)(2,1)S(1)}, bf16[16,4,512]{2,1,0:T(4,128)(2,1)S(1)}) custom-call(s32[32]{0:T(128)S(1)} %get-tuple-element.30.plan_ref, bf16[16,24,512]{2,1,0:T(8,128)(2,1)S(1)} %all-to-all-done.got_ref, bf16[3,16,512]{2,1,0:T(8,128)(2,1)S(1)} %bitcast.10, ...), custom_call_target="tpu_custom_call" | custom-call | tf_op jit(solution)/shard_map/decode_features/pallas_call | solution.py:562
  29.1 0.0 copy-start.13
  29.1 23.5 %all_to_all.20.got_ref = bf16[32,7,4,128]{3,2,1,0:T(4,128)(2,1)S(1)} all-to-all(bf16[32,7,4,128]{3,2,1,0:T(4,128)(2,1)S(1)} %get-tuple-element.34), channel_id=1, replica_groups=mesh['group'=16,'mp'=32] {'mp'}, dimensions={0} | all-to-all | bytes 458752 | tf_op jit(solution)/shard_map/all_to_all | solution.py:476
  52.6 0.0 copy-done.13
  52.6 0.1 sum_parts.1
  52.7 14.7 %all_to_all.21.rows_ref = bf16[32,7,4,128]{3,2,1,0:T(4,128)(2,1)S(1)} all-to-all(bf16[32,7,4,128]{3,2,1,0:T(4,128)(2,1)S(1)} %sum_parts.1), channel_id=1, replica_groups=mesh['group'=16,'mp'=32] {'mp'}, dimensions={0} | all-to-all | bytes 458752 | tf_op jit(solution)/shard_map/all_to_all | solution.py:476
  67.4 0.0 copy-done.2
  67.4 3.1 %prefill_scan.1 = (bf16[8,16,512]{2,1,0:T(8,128)(2,1)}, bf16[16,9,4,512]{3,2,1,0:T(4,128)(2,1)}) custom-call(s32[32]{0:T(128)S(1)} %get-tuple-element.30.plan_ref, bf16[32,7,4,128]{3,2,1,0:T(4,128)(2,1)S(1)} %all_to_all.21.rows_ref, bf16[128,512]{1,0:T(8,128)(2,1)S(1)} %get-tuple-element.35.x_ref, f32[128,512]{1,0:T(8,128)S(1)} %get-tuple-element.36.gate_ref, ...), custom_call_target="tpu_custom_call" | custom-call | tf_op jit(solution)/shard_map/prefill_scan/pallas_call | solution.py:595
  70.5 5.6 %all-to-all-start.3 = ((bf16[16,9,4,512]{3,2,1,0:T(4,128)(2,1)}), bf16[16,9,4,512]{3,2,1,0:T(4,128)(2,1)S(1)}, u32[]{:S(2)}, u32[]{:S(2)}) async-start(bf16[16,9,4,512]{3,2,1,0:T(4,128)(2,1)} %get-tuple-element.39), calls=%async_computation.3 | async-start | bytes 1179648 | tf_op jit(solution)/shard_map/all_to_all | solution.py:476
  76.2 0.0 copy-done.1
  76.2 0.0 copy-done.12
  76.2 0.0 copy-start.14
  76.2 0.8 copy-done.14
  77.0 2.8 %decode_scan.1 = (bf16[16,4,512]{2,1,0:T(4,128)(2,1)}, f32[16,16,512]{2,1,0:T(8,128)}, f32[16,512]{1,0:T(8,128)S(1)}, f32[4,16,512]{2,1,0:T(8,128)S(1)}, f32[16,...) custom-call(s32[32]{0:T(128)S(1)} %get-tuple-element.30.plan_ref, ...), custom_call_target="tpu_custom_call" | custom-call | flops 6000000000 | bytes 8000000 | tf_op jit(solution)/shard_map/decode_scan/pallas_call | solution.py:616
  79.8 0.6 convert_bitcast_fusion
  80.5 14.3 %all-to-all-done.3.got_ref = bf16[16,9,4,512]{3,2,1,0:T(4,128)(2,1)S(1)} async-done(((bf16[16,9,4,512]{3,2,1,0:T(4,128)(2,1)}), bf16[16,9,4,512]{3,2,1,0:T(4,128)(2,1)S(1)}, u32[]{:S(2)}, u32[]{:S(2)}) %all-to-all-start.3) | async-done | bytes 589856 | tf_op jit(solution)/shard_map/all_to_all | solution.py:476
  94.8 1.3 %finish.1 = (bf16[16,4,512]{2,1,0:T(4,128)(2,1)}, f32[16,16,512]{2,1,0:T(8,128)}, f32[32,16,512]{2,1,0:T(8,128)}) custom-call(bf16[16,9,4,512]{3,2,1,0:T(4,128)(2,1)S(1)} %all-to-all-done.3.got_ref, f32[16,512]{1,0:T(8,128)S(1)} %get-tuple-element.41.base_ref, ...), custom_call_target="tpu_custom_call", output_to_operand_aliasing={{0}: (6, {}), {1}: (7, {})} | custom-call | tf_op jit(solution)/shard_map/finish/pallas_call | solution.py:651
  (4 shorter events, 0.0 us)
Async XLA Ops:
  0.6 12.7 %copy-start.11 = (bf16[8,16,512]{2,1,0:T(8,128)(2,1)S(1)}, bf16[8,16,512]{2,1,0:T(8,128)(2,1)}, u32[]{:S(2)}) copy-start(bf16[8,16,512]{2,1,0:T(8,128)(2,1)} %gate_ref.2) | copy-start | bytes 393220
  2.8 10.5 %copy-start = (bf16[512,512]{1,0:T(8,128)(2,1)S(1)}, bf16[512,512]{1,0:T(8,128)(2,1)}, u32[]{:S(2)}) copy-start(bf16[512,512]{1,0:T(8,128)(2,1)} %rank_ref.3) | copy-start | bytes 1572868
  2.8 10.5 %copy-start.4 = (bf16[8,16,512]{2,1,0:T(8,128)(2,1)S(1)}, bf16[8,16,512]{2,1,0:T(8,128)(2,1)}, u32[]{:S(2)}) copy-start(bf16[8,16,512]{2,1,0:T(8,128)(2,1)} %u_ref.5) | copy-start | bytes 393220
  2.9 10.5 %copy-start.6 = (bf16[512,32]{0,1:T(8,128)(2,1)S(1)}, bf16[512,32]{0,1:T(8,128)(2,1)}, u32[]{:S(2)}) copy-start(bf16[512,32]{0,1:T(8,128)(2,1)} %param.29) | copy-start | bytes 98308
  2.9 10.5 %copy-start.7 = (f32[4,512]{1,0:T(4,128)S(1)}, f32[4,512]{1,0:T(4,128)}, u32[]{:S(2)}) copy-start(f32[4,512]{1,0:T(4,128)} %cw_ref.3) | copy-start | bytes 24580
  2.9 10.5 %copy-start.15 = (f32[16,512]{1,0:T(8,128)S(1)}, f32[16,512]{1,0:T(8,128)}, u32[]{:S(2)}) copy-start(f32[16,512]{1,0:T(8,128)} %decay_ref.1) | copy-start | bytes 98308
  2.9 10.5 %copy-start.17 = (f32[512]{0:T(512)S(1)}, f32[512]{0:T(512)}, u32[]{:S(2)}) copy-start(f32[512]{0:T(512)} %param.31) | copy-start | bytes 6148
  2.9 10.5 %copy-start.18 = (f32[512]{0:T(512)S(1)}, f32[512]{0:T(512)}, u32[]{:S(2)}) copy-start(f32[512]{0:T(512)} %param.33) | copy-start | bytes 6148
  2.9 24.9 %all-to-all-start = ((bf16[16,24,512]{2,1,0:T(8,128)(2,1)}), bf16[16,24,512]{2,1,0:T(8,128)(2,1)S(1)}, u32[]{:S(2)}, u32[]{:S(2)}) async-start(bf16[16,24,512]{2,1,0:T(8,128)(2,1)} %pack.1), calls=%async_computation | async-start | bytes 786432 | tf_op jit(solution)/shard_map/all_to_all | solution.py:476
  13.3 0.7 copy-start.16
  13.3 0.7 copy-start.8
  13.3 0.7 copy-start.9
  13.3 0.7 copy-start.10
  14.0 13.8 %copy-start.3 = (bf16[16,3,512]{2,0,1:T(8,128)(2,1)S(1)}, bf16[16,3,512]{2,0,1:T(8,128)(2,1)}, u32[]{:S(2)}) copy-start(bf16[16,3,512]{2,0,1:T(8,128)(2,1)} %param.18) | copy-start | bytes 147460
  14.0 13.8 %copy-start.5 = (bf16[16,4,512]{2,1,0:T(4,128)(2,1)S(1)}, bf16[16,4,512]{2,1,0:T(4,128)(2,1)}, u32[]{:S(2)}) copy-start(bf16[16,4,512]{2,1,0:T(4,128)(2,1)} %u_ref.7) | copy-start | bytes 196612
  29.1 23.5 %copy-start.13 = (bf16[64,512]{1,0:T(8,128)(2,1)}, bf16[64,512]{1,0:T(8,128)(2,1)S(1)}, u32[]{:S(2)}) copy-start(bf16[64,512]{1,0:T(8,128)(2,1)S(1)} %get-tuple-element.40.x_ref) | copy-start | bytes 196612
  52.6 14.8 %copy-start.2 = (bf16[512,512]{1,0:T(8,128)(2,1)S(1)}, bf16[512,512]{1,0:T(8,128)(2,1)}, u32[]{:S(2)}) copy-start(bf16[512,512]{1,0:T(8,128)(2,1)} %step_w_ref.3) | copy-start | bytes 1572868
  70.5 5.6 %copy-start.1 = (f32[16,16,512]{2,1,0:T(8,128)S(1)}, f32[16,16,512]{2,1,0:T(8,128)}, u32[]{:S(2)}) copy-start(f32[16,16,512]{2,1,0:T(8,128)} %state_ref.3) | copy-start | bytes 1572868
  70.5 5.7 %copy-start.12 = (bf16[16,4,512]{2,1,0:T(4,128)(2,1)S(1)}, bf16[16,4,512]{2,1,0:T(4,128)(2,1)}, u32[]{:S(2)}) copy-start(bf16[16,4,512]{2,1,0:T(4,128)(2,1)} %gate_ref.3) | copy-start | bytes 196612
  70.5 24.3 %all-to-all-start.3 = ((bf16[16,9,4,512]{3,2,1,0:T(4,128)(2,1)}), bf16[16,9,4,512]{3,2,1,0:T(4,128)(2,1)S(1)}, u32[]{:S(2)}, u32[]{:S(2)}) async-start(bf16[16,9,4,512]{3,2,1,0:T(4,128)(2,1)} %get-tuple-element.39), calls=%async_computation.3 | async-start | bytes 1179648 | tf_op jit(solution)/shard_map/all_to_all | solution.py:476
  76.2 0.8 copy-start.14

commit v4 on v3

--- a/solution.py
+++ b/solution.py
@@ -166,15 +166,24 @@
 def prompt_kernel(
     mig_ref, dest_ref, len_ref, u_ref, gate_ref, cw_ref, cb_ref, rank_ref, select_ref, decay_ref,
     step_b_ref, skip_ref, low_ref, sel_ref, x_ref, gate_out_ref, decay_out_ref, extra_ref,
-    plan_ref, scr, x_scr,
+    plan_ref, items_ref, empty_ref, scr, x_scr, empty_scr, sem,
 ):
     prompts, steps, channels = u_ref.shape
     reqs = mig_ref.shape[0]
+    empty_scr[...] = jnp.zeros(empty_scr.shape, BF16)
+    empty = pltpu.make_async_copy(empty_scr, empty_ref, sem)
+    empty.start()
     for i in range(reqs):
         plan_ref[i] = mig_ref[i]
     for i in range(prompts):
         plan_ref[reqs + i] = dest_ref[i]
         plan_ref[reqs + prompts + i] = len_ref[i]
+    own = lax.axis_index("group")
+    wanted = from_scalars(mig_ref, reqs, (reqs, LANES))
+    moved = wanted != own * reqs + iota(wanted.shape, 0)
+    items_ref[:reqs, :] = wanted.astype(F32)
+    items_ref[reqs : 2 * reqs, :] = jnp.where(moved, 1.0, 0.0)
+    items_ref[2 * reqs :, :] = from_scalars(len_ref, prompts, (prompts, LANES)).astype(F32)
     extra_ref[0:1, :] = step_b_ref[...]
     extra_ref[1:2, :] = skip_ref[...]
     extra_ref[2:3, :] = cb_ref[...]
@@ -208,16 +217,16 @@
     low, sel = project(x, rank_ref, select_ref)
     low_ref[...] = low
     sel_ref[...] = sel
+    empty.wait()
 
 
 def decode_kernel(
-    plan_ref, got_ref, conv_ref, u_ref, cw_ref, extra_ref, rank_ref, select_ref, prompt_low_ref,
+    items_ref, got_ref, conv_ref, u_ref, cw_ref, extra_ref, rank_ref, select_ref, prompt_low_ref,
     prompt_sel_ref, pay_ref, x_ref, pass_ref, pool_scr, pay_scr, scr, x_scr,
 ):
     groups = got_ref.shape[0]
     reqs, steps, channels = u_ref.shape
     table = groups * ROWS0
-    own = lax.axis_index("group")
     marks = jnp.zeros((8, channels), F32)
     for s in range(groups):
         block = got_ref[s].astype(F32)
@@ -241,16 +250,19 @@
     relay = jnp.dot(jnp.where(passed, 1.0, 0.0).astype(BF16), pool, preferred_element_type=F32)
     for d in range(groups):
         pass_ref[d] = relay[d * MIG : (d + 1) * MIG].astype(BF16)
-    wide = (reqs, channels)
-    moved_wide = from_scalars(plan_ref, reqs, wide) != own * reqs + iota(wide, 0)
-    shape = (reqs, table)
-    needs = from_scalars(plan_ref, reqs, shape)
-    found = (needs != own * reqs + iota(shape, 0)) & (
-        jnp.broadcast_to(ids, shape) == needs.astype(F32)
+    moved = items_ref[reqs : 2 * reqs, :] > 0.0
+    moved_wide = jnp.concatenate([items_ref[reqs : 2 * reqs, :]] * (channels // LANES), axis=1) > 0.0
+    needs = items_ref[:reqs, :]
+    found = jnp.concatenate(
+        [
+            jnp.where(moved & (ids[:, at : at + LANES] == needs), 1.0, 0.0)
+            for at in range(0, table, LANES)
+        ],
+        axis=1,
     )
     hist = []
     for j in range(3):
-        hit = jnp.where(found & (place >= 4 * j) & (place < 4 * j + 4), 1.0, 0.0).astype(BF16)
+        hit = jnp.where((place >= 4 * j) & (place < 4 * j + 4), found, 0.0).astype(BF16)
         taken = jnp.dot(hit, pool, preferred_element_type=F32)
         hist.append(jnp.where(moved_wide, taken, conv_ref[j].astype(F32)))
     for l in range(channels // LANES):
@@ -329,36 +341,51 @@
 
 def prefill_kernel(
     plan_ref, rows_ref, x_ref, gate_ref, step_w_ref, decay_ref, extra_ref, relay_ref,
-    out_ref, pay_ref, low_scr, sel_scr, step_scr, x_scr, h_scr, y_scr,
+    items_ref, _empty, out_ref, pay_ref, low_scr, sel_scr, step_scr, x_scr, h_scr, y_scr,
+    final_scr, out_scr, plan_scr, sems,
 ):
     prompts, steps, channels = out_ref.shape
     states = decay_ref.shape[1] // 8
     reqs = plan_ref.shape[0] - 2 * prompts
+    groups, blocks, four, _ = pay_ref.shape
+    parts = states // four
+    plan_copy = pltpu.make_async_copy(plan_ref, plan_scr, sems.at[0])
+    plan_copy.start()
+    passed = pltpu.make_async_copy(relay_ref, pay_ref.at[:, blocks - 1], sems.at[1])
+    passed.start()
     take_tiles(rows_ref, 0, low_scr, sel_scr)
     step_scr[...] = steps_of(low_scr, step_w_ref, extra_ref[0:1, :])
     x_scr[...] = x_ref[...].astype(F32)
     h_scr[...] = jnp.zeros(h_scr.shape, F32)
-    lengths = from_scalars(plan_ref, prompts, (prompts, LANES), reqs + prompts)
+    lengths = items_ref[2 * reqs :, :]
     skip = extra_ref[1:2, :]
     for t in range(steps):
         scan(
             t, prompts, t < lengths, x_scr, gate_ref, sel_scr, step_scr, decay_ref, skip, h_scr,
             y_scr, steps,
         )
-    dests, ranks = slots_of(plan_ref, prompts, reqs)
-    groups, blocks, four, _ = pay_ref.shape
-    parts = states // four
-    for d in range(groups):
-        pay_ref[d, : blocks - 1] = jnp.zeros((blocks - 1, four, channels), BF16)
-        pay_ref[d, blocks - 1] = relay_ref[d]
+    plan_copy.wait()
+    dests, ranks = slots_of(plan_scr, prompts, reqs)
+    passed.wait()
+    copies = []
     for i in range(prompts):
-        at = ranks[i] * parts
         for l in range(channels // LANES):
             cols = slice(l * LANES, (l + 1) * LANES)
-            out_ref[i, :, cols] = y_scr[l, i * steps : (i + 1) * steps, :].astype(BF16)
-            final = h_scr[l, pl.ds(i, states, stride=prompts), :]
             for p in range(parts):
-                pay_ref[dests[i], at + p, :, cols] = final[p * four : (p + 1) * four].astype(BF16)
+                final_scr[i, p, :, cols] = h_scr[
+                    l, pl.ds(i + p * four * prompts, four, stride=prompts), :
+                ].astype(BF16)
+        place = pay_ref.at[dests[i], pl.ds(ranks[i] * parts, parts)]
+        copies.append(pltpu.make_async_copy(final_scr.at[i], place, sems.at[2 + i]))
+        copies[-1].start()
+    for i in range(prompts):
+        for l in range(channels // LANES):
+            cols = slice(l * LANES, (l + 1) * LANES)
+            out_scr[i, :, cols] = y_scr[l, i * steps : (i + 1) * steps, :].astype(BF16)
+    copies.append(pltpu.make_async_copy(out_scr, out_ref, sems.at[2 + prompts]))
+    copies[-1].start()
+    for copy in copies:
+        copy.wait()
 
 
 def decode_scan_kernel(
@@ -435,6 +462,18 @@
     lanes = channels // LANES
     parts = states // four
     copies = []
+    for s in range(groups):
+        for q in range(PAIR):
+            for p in range(parts):
+                state_scr[s * PAIR + q, p * four : (p + 1) * four, :] = got_ref[
+                    s, q * parts + p
+                ].astype(F32)
+        if s % 4 == 3:
+            here = pl.ds((s - 3) * PAIR, 4 * PAIR)
+            copies.append(
+                pltpu.make_async_copy(state_scr.at[here], prompt_state_ref.at[here], sems.at[s])
+            )
+            copies[-1].start()
     for n in range(states):
         put_lanes(moved_scr, n * MIG, got_ref[n, blocks - 1].astype(F32))
     for k in range(MIG):
@@ -456,17 +495,6 @@
             pltpu.make_async_copy(out_scr.at[k], out_ref.at[pick], sems.at[groups + MIG + k])
         )
         copies[-2].start()
-        copies[-1].start()
-    for s in range(groups):
-        for q in range(PAIR):
-            for p in range(parts):
-                state_scr[s * PAIR + q, p * four : (p + 1) * four, :] = got_ref[
-                    s, q * parts + p
-                ].astype(F32)
-        here = pl.ds(s * PAIR, PAIR)
-        copies.append(
-            pltpu.make_async_copy(state_scr.at[here], prompt_state_ref.at[here], sems.at[s])
-        )
         copies[-1].start()
     for copy in copies:
         copy.wait()
@@ -518,6 +546,8 @@
     def cost(flops, size):
         return pl.CostEstimate(flops=flops, bytes_accessed=size, transcendentals=0)
 
+    anywhere = pl.BlockSpec(memory_space=pl.ANY)
+    send_shape = (groups, PAIR * states // MIG + 1, MIG, channels)
     dest = prompt_dest.reshape(prompts)
     conv_rows = jnp.transpose(resident_conv, (1, 0, 2))
     select_rows = jnp.transpose(select_weight)
@@ -537,7 +567,7 @@
     )(migrate_from, dest, prompt_length, conv_rows, resident_state, prompt_inputs)
     got_first = exchange(send_first, "group")
 
-    prompt_low, prompt_sel, prompt_x, gate_rows, decay, extra, plan = pl.pallas_call(
+    prompt_low, prompt_sel, prompt_x, gate_rows, decay, extra, plan, items, empty = pl.pallas_call(
         prompt_kernel,
         out_shape=(
             struct((prompt_rows, rank), F32),
@@ -547,10 +577,17 @@
             struct((tiles, 8 * states, LANES), F32),
             struct((8, channels), F32),
             struct((reqs + 2 * prompts,), jnp.int32),
+            struct((2 * reqs + prompts, LANES), F32),
+            struct(send_shape, BF16),
         ),
         in_specs=[SMEM] * 3 + [VMEM] * 9,
-        out_specs=(VMEM,) * 6 + (SMEM,),
-        scratch_shapes=[scratch((tiles, prompt_rows, LANES)), scratch((prompt_rows, channels))],
+        out_specs=(VMEM,) * 6 + (SMEM, VMEM, anywhere),
+        scratch_shapes=[
+            scratch((tiles, prompt_rows, LANES)),
+            scratch((prompt_rows, channels)),
+            pltpu.VMEM(send_shape, BF16),
+            pltpu.SemaphoreType.DMA,
+        ],
         compiler_params=PARAMS,
         cost_estimate=cost(10**9, 2 * 10**6),
         name="prompt_features",
@@ -566,7 +603,7 @@
             struct((decode_rows, channels), BF16),
             struct((groups, MIG, channels), BF16),
         ),
-        in_specs=[SMEM] + [VMEM] * 9,
+        in_specs=[VMEM] * 10,
         out_specs=(VMEM,) * 3,
         scratch_shapes=[
             scratch((groups * ROWS0, channels)),
@@ -577,7 +614,7 @@
         compiler_params=PARAMS,
         name="decode_features",
     )(
-        plan, got_first, conv_rows, decode_inputs, conv_weight, extra, rank_weight, select_rows,
+        items, got_first, conv_rows, decode_inputs, conv_weight, extra, rank_weight, select_rows,
         prompt_low, prompt_sel,
     )
 
@@ -596,10 +633,10 @@
         prefill_kernel,
         out_shape=(
             struct(prompt_inputs.shape, BF16),
-            struct((groups, PAIR * states // MIG + 1, MIG, channels), BF16),
+            struct(send_shape, BF16),
         ),
-        in_specs=[SMEM] + [VMEM] * 7,
-        out_specs=(VMEM, VMEM),
+        in_specs=[anywhere] + [VMEM] * 8 + [anywhere],
+        out_specs=(anywhere,) * 2,
         scratch_shapes=[
             scratch((prompt_rows, rank)),
             scratch((prompt_rows, LANES)),
@@ -607,10 +644,15 @@
             scratch((prompt_rows, channels)),
             scratch((tiles, prompts * states, LANES)),
             scratch((tiles, prompt_rows, LANES)),
+            pltpu.VMEM((prompts, states // MIG, MIG, channels), BF16),
+            pltpu.VMEM(prompt_inputs.shape, BF16),
+            pltpu.SMEM((reqs + 2 * prompts,), jnp.int32),
+            pltpu.SemaphoreType.DMA((prompts + 3,)),
         ],
+        input_output_aliases={9: 1},
         compiler_params=PARAMS,
         name="prefill_scan",
-    )(plan, rows, prompt_x, gate_rows, step_weight, decay, extra, relay)
+    )(plan, rows, prompt_x, gate_rows, step_weight, decay, extra, relay, items, empty)
     got_final = exchange(send_final, "group")
 
     early_out, early_final, base, held, weight, keep, pick, final_conv, prompt_conv = pl.pallas_call(
@@ -647,7 +689,6 @@
         extra, got_first,
     )
 
-    anywhere = pl.BlockSpec(memory_space=pl.ANY)
     decode_out, final_state, prompt_state = pl.pallas_call(
         finish_kernel,
         out_shape=(

time: 96.6 us -> 95.4 us (0.988)
  transfers between devices with their start and end apart: 2 -> 2, of which waited for: 2 -> 2; matrix products, arithmetic and copies ran while one was open for 1% -> 1% of each run, Pallas kernels for 5% -> 6%
where the time goes in v4:
time: 95.4 us; the launch traced here: 94.9 us
  blocking collectives  38.2 us (40%)
  waiting for transfers between devices  25.7 us (27%)
  starting transfers between devices  16 us (17%)
  Pallas kernels  12 us (13%)
  local copies, waits for them, and re-layouts  1.5 us (2%)
    all_to_all x2, blocking collectives, exchange(): return lax.all_to_all(value, axis, split_axis=0, concat_axis=0, tiled=True)  38.2 us
    all_to_all x2, waiting for transfers between devices, exchange(): return lax.all_to_all(value, axis, split_axis=0, concat_axis=0, tiled=True)  25.7 us
    all_to_all x2, starting transfers between devices, exchange(): return lax.all_to_all(value, axis, split_axis=0, concat_axis=0, tiled=True)  16 us
    pallas_call x1, Pallas kernels, on_device(): pl.pallas_call(decode_scan_kernel, out_shape=(struct(decode_inputs.shape,...  2.83 us
    pallas_call x1, Pallas kernels, on_device(): pl.pallas_call(prefill_kernel, out_shape=(struct(prompt_inputs.shape, BF1...  2.46 us
    pallas_call x1, Pallas kernels, on_device(): pl.pallas_call(prompt_kernel, out_shape=(struct((prompt_rows, rank), F32)...  2.45 us
    pallas_call x1, Pallas kernels, on_device(): pl.pallas_call(pack_kernel, out_shape=struct((groups, ROWS0, channels), B...  2.21 us
  transfers between devices with their start and end apart: 2, of which 2 were waited for; matrix products, arithmetic and copies ran while one was open for 1% of the time, Pallas kernels for 6%

profile of v4, /device:TPU:1, one launch (start us, length us, event | category | flops | bytes accessed | tf_op | source)
XLA Modules:
  0.0 94.9 jit_solution(7118644152930391804)
XLA Ops:
  0.6 0.0 copy-start.11
  0.6 2.2 %pack.1 = bf16[16,24,512]{2,1,0:T(8,128)(2,1)} custom-call(s32[16]{0:T(128)} %mig_ref.3, s32[8]{0:T(128)} %bitcast.13, s32[8]{0:T(128)} %len_ref.3, bf16[3,16,512]{2,1,0:T(8,128)(2,1)} %bitcast.9, f32[16,16,512]{2,1,0:T(8,128)} %state_ref.3, bf16[8,16,512]{2,1,0:T(8,128)(2,1)} %u_ref.5), custom_call_target="tpu_custom_call" | custom-call | tf_op jit(solution)/shard_map/pack/pallas_call | solution.py:555
  2.8 0.0 copy-start.2
  2.9 0.0 copy-start.4
  2.9 0.0 copy-start.7
  2.9 0.0 copy-start.15
  2.9 0.0 copy-start.17
  2.9 0.0 copy-start.18
  2.9 10.4 %all-to-all-start = ((bf16[16,24,512]{2,1,0:T(8,128)(2,1)}), bf16[16,24,512]{2,1,0:T(8,128)(2,1)S(1)}, u32[]{:S(2)}, u32[]{:S(2)}) async-start(bf16[16,24,512]{2,1,0:T(8,128)(2,1)} %pack.1), calls=%async_computation | async-start | bytes 786432 | tf_op jit(solution)/shard_map/all_to_all | solution.py:504
  13.3 0.0 copy-start.16
  13.3 0.0 copy-start.8
  13.3 0.0 copy-start.9
  13.3 0.0 copy-start.10
  13.3 0.0 copy-done.11
  13.3 0.0 copy-done.2
  13.3 0.0 copy-done.4
  13.3 0.0 copy-done.6
  13.4 0.0 copy-done.7
  13.4 0.0 copy-done.15
  13.4 0.0 copy-done.17
  13.4 0.0 copy-done.18
  13.4 0.6 copy-done.16
  14.0 0.0 copy-done.8
  14.0 0.0 copy-done.9
  14.0 0.0 copy-done.10
  14.0 2.4 %prompt_features.1 = (f32[128,512]{1,0:T(8,128)S(1)}, f32[128,32]{1,0:T(8,128)S(1)}, bf16[128,512]{1,0:T(8,128)(2,1)S(1)}, f32[128,512]{1,0:T(8,128)S(1)}, f32[4...) custom-call(s32[16]{0:T(128)S(1)} %copy-done.8, ...), custom_call_target="tpu_custom_call" | custom-call | flops 1000000000 | bytes 2000000 | tf_op jit(solution)/shard_map/prompt_features/pallas_call | solution.py:570
  16.4 11.4 %all-to-all-done.got_ref = bf16[16,24,512]{2,1,0:T(8,128)(2,1)S(1)} async-done(((bf16[16,24,512]{2,1,0:T(8,128)(2,1)}), bf16[16,24,512]{2,1,0:T(8,128)(2,1)S(1)}, u32[]{:S(2)}, u32[]{:S(2)}) %all-to-all-start) | async-done | bytes 393248 | tf_op jit(solution)/shard_map/all_to_all | solution.py:504
  27.8 0.0 copy-done.3
  27.8 0.0 copy-done.5
  27.8 0.7 decode_features.1
  28.6 0.0 copy-start.13
  28.6 23.5 %all_to_all.20.got_ref = bf16[32,7,4,128]{3,2,1,0:T(4,128)(2,1)S(1)} all-to-all(bf16[32,7,4,128]{3,2,1,0:T(4,128)(2,1)S(1)} %get-tuple-element.37), channel_id=1, replica_groups=mesh['group'=16,'mp'=32] {'mp'}, dimensions={0} | all-to-all | bytes 458752 | tf_op jit(solution)/shard_map/all_to_all | solution.py:504
  52.0 0.0 copy-done.13
  52.1 0.1 sum_parts.1
  52.2 14.7 %all_to_all.21.rows_ref = bf16[32,7,4,128]{3,2,1,0:T(4,128)(2,1)S(1)} all-to-all(bf16[32,7,4,128]{3,2,1,0:T(4,128)(2,1)S(1)} %sum_parts.1), channel_id=1, replica_groups=mesh['group'=16,'mp'=32] {'mp'}, dimensions={0} | all-to-all | bytes 458752 | tf_op jit(solution)/shard_map/all_to_all | solution.py:504
  66.9 0.0 copy-done
  66.9 2.5 %prefill_scan.1 = (bf16[8,16,512]{2,1,0:T(8,128)(2,1)}, bf16[16,9,4,512]{3,2,1,0:T(4,128)(2,1)}) custom-call(s32[32]{0:T(128)S(1)} %get-tuple-element.32.plan_ref, bf16[32,7,4,128]{3,2,1,0:T(4,128)(2,1)S(1)} %all_to_all.21.rows_ref, bf16[128,512]{1,0:T(8,128)(2,1)S(1)} %get-tuple-element.38.x_ref, ...), custom_call_target="tpu_custom_call", output_to_operand_aliasing={{1}: (9, {})} | custom-call | tf_op jit(solution)/shard_map/prefill_scan/pallas_call | solution.py:632
  69.4 0.0 copy-start.1
  69.4 0.0 copy-start.12
  69.4 5.7 %all-to-all-start.3 = ((bf16[16,9,4,512]{3,2,1,0:T(4,128)(2,1)}), bf16[16,9,4,512]{3,2,1,0:T(4,128)(2,1)S(1)}, u32[]{:S(2)}, u32[]{:S(2)}) async-start(bf16[16,9,4,512]{3,2,1,0:T(4,128)(2,1)} %get-tuple-element.43), calls=%async_computation.3 | async-start | bytes 1179648 | tf_op jit(solution)/shard_map/all_to_all | solution.py:504
  75.0 0.0 copy-done.1
  75.0 0.0 copy-done.12
  75.1 0.0 copy-start.14
  75.1 0.8 copy-done.14
  75.9 2.8 %decode_scan.1 = (bf16[16,4,512]{2,1,0:T(4,128)(2,1)}, f32[16,16,512]{2,1,0:T(8,128)}, f32[16,512]{1,0:T(8,128)S(1)}, f32[4,16,512]{2,1,0:T(8,128)S(1)}, f32[16,...) custom-call(s32[32]{0:T(128)S(1)} %get-tuple-element.32.plan_ref, ...), custom_call_target="tpu_custom_call" | custom-call | flops 6000000000 | bytes 8000000 | tf_op jit(solution)/shard_map/decode_scan/pallas_call | solution.py:658
  78.7 0.6 convert_bitcast_fusion
  79.4 14.3 %all-to-all-done.3.got_ref = bf16[16,9,4,512]{3,2,1,0:T(4,128)(2,1)S(1)} async-done(((bf16[16,9,4,512]{3,2,1,0:T(4,128)(2,1)}), bf16[16,9,4,512]{3,2,1,0:T(4,128)(2,1)S(1)}, u32[]{:S(2)}, u32[]{:S(2)}) %all-to-all-start.3) | async-done | bytes 589856 | tf_op jit(solution)/shard_map/all_to_all | solution.py:504
  93.7 1.3 %finish.1 = (bf16[16,4,512]{2,1,0:T(4,128)(2,1)}, f32[16,16,512]{2,1,0:T(8,128)}, f32[32,16,512]{2,1,0:T(8,128)}) custom-call(bf16[16,9,4,512]{3,2,1,0:T(4,128)(2,1)S(1)} %all-to-all-done.3.got_ref, f32[16,512]{1,0:T(8,128)S(1)} %get-tuple-element.45.base_ref, ...), custom_call_target="tpu_custom_call", output_to_operand_aliasing={{0}: (6, {}), {1}: (7, {})} | custom-call | tf_op jit(solution)/shard_map/finish/pallas_call | solution.py:692
  (4 shorter events, 0.0 us)
Async XLA Ops:
  0.6 12.7 %copy-start.11 = (bf16[8,16,512]{2,1,0:T(8,128)(2,1)S(1)}, bf16[8,16,512]{2,1,0:T(8,128)(2,1)}, u32[]{:S(2)}) copy-start(bf16[8,16,512]{2,1,0:T(8,128)(2,1)} %gate_ref.2) | copy-start | bytes 393220
  2.8 10.5 %copy-start.2 = (bf16[512,512]{1,0:T(8,128)(2,1)S(1)}, bf16[512,512]{1,0:T(8,128)(2,1)}, u32[]{:S(2)}) copy-start(bf16[512,512]{1,0:T(8,128)(2,1)} %rank_ref.3) | copy-start | bytes 1572868
  2.9 10.5 %copy-start.4 = (bf16[8,16,512]{2,1,0:T(8,128)(2,1)S(1)}, bf16[8,16,512]{2,1,0:T(8,128)(2,1)}, u32[]{:S(2)}) copy-start(bf16[8,16,512]{2,1,0:T(8,128)(2,1)} %u_ref.5) | copy-start | bytes 393220
  2.9 10.5 %copy-start.6 = (bf16[512,32]{0,1:T(8,128)(2,1)S(1)}, bf16[512,32]{0,1:T(8,128)(2,1)}, u32[]{:S(2)}) copy-start(bf16[512,32]{0,1:T(8,128)(2,1)} %param.29) | copy-start | bytes 98308
  2.9 10.5 %copy-start.7 = (f32[4,512]{1,0:T(4,128)S(1)}, f32[4,512]{1,0:T(4,128)}, u32[]{:S(2)}) copy-start(f32[4,512]{1,0:T(4,128)} %cw_ref.3) | copy-start | bytes 24580
  2.9 10.5 %copy-start.15 = (f32[16,512]{1,0:T(8,128)S(1)}, f32[16,512]{1,0:T(8,128)}, u32[]{:S(2)}) copy-start(f32[16,512]{1,0:T(8,128)} %decay_ref.1) | copy-start | bytes 98308
  2.9 10.5 %copy-start.17 = (f32[512]{0:T(512)S(1)}, f32[512]{0:T(512)}, u32[]{:S(2)}) copy-start(f32[512]{0:T(512)} %param.31) | copy-start | bytes 6148
  2.9 10.5 %copy-start.18 = (f32[512]{0:T(512)S(1)}, f32[512]{0:T(512)}, u32[]{:S(2)}) copy-start(f32[512]{0:T(512)} %param.33) | copy-start | bytes 6148
  2.9 24.9 %all-to-all-start = ((bf16[16,24,512]{2,1,0:T(8,128)(2,1)}), bf16[16,24,512]{2,1,0:T(8,128)(2,1)S(1)}, u32[]{:S(2)}, u32[]{:S(2)}) async-start(bf16[16,24,512]{2,1,0:T(8,128)(2,1)} %pack.1), calls=%async_computation | async-start | bytes 786432 | tf_op jit(solution)/shard_map/all_to_all | solution.py:504
  13.3 0.7 copy-start.16
  13.3 0.7 copy-start.8
  13.3 0.7 copy-start.9
  13.3 0.7 copy-start.10
  14.0 13.8 %copy-start.3 = (bf16[16,3,512]{2,0,1:T(8,128)(2,1)S(1)}, bf16[16,3,512]{2,0,1:T(8,128)(2,1)}, u32[]{:S(2)}) copy-start(bf16[16,3,512]{2,0,1:T(8,128)(2,1)} %param.18) | copy-start | bytes 147460
  14.0 13.8 %copy-start.5 = (bf16[16,4,512]{2,1,0:T(4,128)(2,1)S(1)}, bf16[16,4,512]{2,1,0:T(4,128)(2,1)}, u32[]{:S(2)}) copy-start(bf16[16,4,512]{2,1,0:T(4,128)(2,1)} %u_ref.7) | copy-start | bytes 196612
  28.6 23.5 %copy-start.13 = (bf16[64,512]{1,0:T(8,128)(2,1)}, bf16[64,512]{1,0:T(8,128)(2,1)S(1)}, u32[]{:S(2)}) copy-start(bf16[64,512]{1,0:T(8,128)(2,1)S(1)} %get-tuple-element.44.x_ref) | copy-start | bytes 196612
  52.1 14.8 %copy-start = (bf16[512,512]{1,0:T(8,128)(2,1)S(1)}, bf16[512,512]{1,0:T(8,128)(2,1)}, u32[]{:S(2)}) copy-start(bf16[512,512]{1,0:T(8,128)(2,1)} %step_w_ref.3) | copy-start | bytes 1572868
  69.4 5.7 %copy-start.1 = (f32[16,16,512]{2,1,0:T(8,128)S(1)}, f32[16,16,512]{2,1,0:T(8,128)}, u32[]{:S(2)}) copy-start(f32[16,16,512]{2,1,0:T(8,128)} %state_ref.3) | copy-start | bytes 1572868
  69.4 5.7 %copy-start.12 = (bf16[16,4,512]{2,1,0:T(4,128)(2,1)S(1)}, bf16[16,4,512]{2,1,0:T(4,128)(2,1)}, u32[]{:S(2)}) copy-start(bf16[16,4,512]{2,1,0:T(4,128)(2,1)} %gate_ref.3) | copy-start | bytes 196612
  69.4 24.3 %all-to-all-start.3 = ((bf16[16,9,4,512]{3,2,1,0:T(4,128)(2,1)}), bf16[16,9,4,512]{3,2,1,0:T(4,128)(2,1)S(1)}, u32[]{:S(2)}, u32[]{:S(2)}) async-start(bf16[16,9,4,512]{3,2,1,0:T(4,128)(2,1)} %get-tuple-element.43), calls=%async_computation.3 | async-start | bytes 1179648 | tf_op jit(solution)/shard_map/all_to_all | solution.py:504
  75.1 0.8 copy-start.14

commit v5 on v4

--- a/solution.py
+++ b/solution.py
@@ -67,18 +67,29 @@
 
 
 def pack_kernel(
-    mig_ref, dest_ref, len_ref, conv_ref, state_ref, u_ref, pay_ref, scr, conv_scr, u_scr
+    mig_hbm, dest_hbm, len_hbm, conv_hbm, state_hbm, u_hbm, pay_ref, mig_ref, dest_ref, len_ref,
+    conv_ref, state_ref, u_ref, scr, conv_scr, u_scr, sems,
 ):
+    pairs = (
+        (mig_hbm, mig_ref), (conv_hbm, conv_ref), (state_hbm, state_ref), (u_hbm, u_ref),
+        (dest_hbm, dest_ref), (len_hbm, len_ref),
+    )
+    copies = [pltpu.make_async_copy(a, b, sems.at[n]) for n, (a, b) in enumerate(pairs)]
+    for copy in copies:
+        copy.start()
     groups = pay_ref.shape[0]
     _, reqs, channels = conv_ref.shape
     prompts, steps, _ = u_ref.shape
     states = state_ref.shape[1]
+    copies[0].wait()
     own, picks = picks_of(mig_ref, reqs)
     base = scr.at[groups]
     base[...] = jnp.zeros(base.shape, F32)
     lane = iota((1, channels), 1)
     ids = jnp.zeros((1, channels), jnp.int32)
     wanted = jnp.zeros((1, channels), jnp.int32)
+    for copy in copies[1:]:
+        copy.wait()
     for j in range(3):
         conv_scr[j * reqs : (j + 1) * reqs, :] = conv_ref[j].astype(F32)
     for k in range(MIG):
@@ -222,7 +233,7 @@
 
 def decode_kernel(
     items_ref, got_ref, conv_ref, u_ref, cw_ref, extra_ref, rank_ref, select_ref, prompt_low_ref,
-    prompt_sel_ref, pay_ref, x_ref, pass_ref, pool_scr, pay_scr, scr, x_scr,
+    prompt_sel_ref, pay_ref, x_ref, pass_ref, pool_scr, pay_scr, scr, x_scr, pass_scr,
 ):
     groups = got_ref.shape[0]
     reqs, steps, channels = u_ref.shape
@@ -249,7 +260,11 @@
     passed = (wanted == ids) & (place >= STATE_ROW) & (place < STATE_ROW + MIG)
     relay = jnp.dot(jnp.where(passed, 1.0, 0.0).astype(BF16), pool, preferred_element_type=F32)
     for d in range(groups):
-        pass_ref[d] = relay[d * MIG : (d + 1) * MIG].astype(BF16)
+        for l in range(channels // LANES):
+            pass_scr[d, l * MIG : (l + 1) * MIG, :] = relay[
+                d * MIG : (d + 1) * MIG, l * LANES : (l + 1) * LANES
+            ]
+    pass_ref[...] = pass_scr[...].astype(BF16)
     moved = items_ref[reqs : 2 * reqs, :] > 0.0
     moved_wide = jnp.concatenate([items_ref[reqs : 2 * reqs, :]] * (channels // LANES), axis=1) > 0.0
     needs = items_ref[:reqs, :]
@@ -347,11 +362,12 @@
     prompts, steps, channels = out_ref.shape
     states = decay_ref.shape[1] // 8
     reqs = plan_ref.shape[0] - 2 * prompts
-    groups, blocks, four, _ = pay_ref.shape
-    parts = states // four
+    lanes = channels // LANES
+    slot_rows = lanes * states
+    passing = pay_ref.at[:, pl.ds(PAIR * slot_rows, MIG * lanes)]
     plan_copy = pltpu.make_async_copy(plan_ref, plan_scr, sems.at[0])
     plan_copy.start()
-    passed = pltpu.make_async_copy(relay_ref, pay_ref.at[:, blocks - 1], sems.at[1])
+    passed = pltpu.make_async_copy(relay_ref, passing, sems.at[1])
     passed.start()
     take_tiles(rows_ref, 0, low_scr, sel_scr)
     step_scr[...] = steps_of(low_scr, step_w_ref, extra_ref[0:1, :])
@@ -369,13 +385,12 @@
     passed.wait()
     copies = []
     for i in range(prompts):
-        for l in range(channels // LANES):
-            cols = slice(l * LANES, (l + 1) * LANES)
-            for p in range(parts):
-                final_scr[i, p, :, cols] = h_scr[
-                    l, pl.ds(i + p * four * prompts, four, stride=prompts), :
-                ].astype(BF16)
-        place = pay_ref.at[dests[i], pl.ds(ranks[i] * parts, parts)]
+        for l in range(lanes):
+            final_scr[i, l * states : (l + 1) * states, :] = h_scr[
+                l, pl.ds(i, states, stride=prompts), :
+            ].astype(BF16)
+        first = pl.multiple_of(ranks[i] * slot_rows, slot_rows)
+        place = pay_ref.at[dests[i], pl.ds(first, slot_rows)]
         copies.append(pltpu.make_async_copy(final_scr.at[i], place, sems.at[2 + i]))
         copies[-1].start()
     for i in range(prompts):
@@ -456,17 +471,17 @@
     got_ref, base_ref, held_ref, weight_ref, keep_ref, pick_ref, _out, _final, out_ref, final_ref,
     prompt_state_ref, state_scr, moved_scr, out_scr, final_scr, sems,
 ):
-    groups, blocks, four, channels = got_ref.shape
-    slots, states, _ = state_scr.shape
+    groups = got_ref.shape[0]
+    slots, states, channels = state_scr.shape
     steps = base_ref.shape[0] // MIG
     lanes = channels // LANES
-    parts = states // four
     copies = []
     for s in range(groups):
         for q in range(PAIR):
-            for p in range(parts):
-                state_scr[s * PAIR + q, p * four : (p + 1) * four, :] = got_ref[
-                    s, q * parts + p
+            for l in range(lanes):
+                at = (q * lanes + l) * states
+                state_scr[s * PAIR + q, :, l * LANES : (l + 1) * LANES] = got_ref[
+                    s, at : at + states, :
                 ].astype(F32)
         if s % 4 == 3:
             here = pl.ds((s - 3) * PAIR, 4 * PAIR)
@@ -475,7 +490,9 @@
             )
             copies[-1].start()
     for n in range(states):
-        put_lanes(moved_scr, n * MIG, got_ref[n, blocks - 1].astype(F32))
+        arrived = got_ref[n, PAIR * lanes * states :, :].astype(F32)
+        for l in range(lanes):
+            moved_scr[l, n * MIG : (n + 1) * MIG, :] = arrived[l * MIG : (l + 1) * MIG]
     for k in range(MIG):
         pick = jnp.max(pick_ref[k : k + 1, :]).astype(jnp.int32)
         for l in range(lanes):
@@ -547,7 +564,7 @@
         return pl.CostEstimate(flops=flops, bytes_accessed=size, transcendentals=0)
 
     anywhere = pl.BlockSpec(memory_space=pl.ANY)
-    send_shape = (groups, PAIR * states // MIG + 1, MIG, channels)
+    send_shape = (groups, (PAIR * states + MIG) * tiles, LANES)
     dest = prompt_dest.reshape(prompts)
     conv_rows = jnp.transpose(resident_conv, (1, 0, 2))
     select_rows = jnp.transpose(select_weight)
@@ -555,12 +572,19 @@
     send_first = pl.pallas_call(
         pack_kernel,
         out_shape=struct((groups, ROWS0, channels), BF16),
-        in_specs=[SMEM] * 3 + [VMEM] * 3,
+        in_specs=[anywhere] * 6,
         out_specs=VMEM,
         scratch_shapes=[
+            pltpu.SMEM((reqs,), jnp.int32),
+            pltpu.SMEM((prompts,), jnp.int32),
+            pltpu.SMEM((prompts,), jnp.int32),
+            pltpu.VMEM((3, reqs, channels), BF16),
+            scratch((reqs, states, channels)),
+            pltpu.VMEM((prompts, steps, channels), BF16),
             scratch((groups + 1, ROWS0, channels)),
             scratch((3 * reqs, channels)),
             scratch((prompts * (steps + 8), channels)),
+            pltpu.SemaphoreType.DMA((6,)),
         ],
         compiler_params=ALL_VMEM,
         name="pack",
@@ -601,7 +625,7 @@
         out_shape=(
             struct((peers, 7, 4, LANES), BF16),
             struct((decode_rows, channels), BF16),
-            struct((groups, MIG, channels), BF16),
+            struct((groups, MIG * tiles, LANES), BF16),
         ),
         in_specs=[VMEM] * 10,
         out_specs=(VMEM,) * 3,
@@ -610,6 +634,7 @@
             scratch((peers, 32, LANES)),
             scratch((tiles, reqs * 8, LANES)),
             scratch((decode_rows, channels)),
+            scratch((groups, MIG * tiles, LANES)),
         ],
         compiler_params=PARAMS,
         name="decode_features",
@@ -644,7 +669,7 @@
             scratch((prompt_rows, channels)),
             scratch((tiles, prompts * states, LANES)),
             scratch((tiles, prompt_rows, LANES)),
-            pltpu.VMEM((prompts, states // MIG, MIG, channels), BF16),
+            pltpu.VMEM((prompts, tiles * states, LANES), BF16),
             pltpu.VMEM(prompt_inputs.shape, BF16),
             pltpu.SMEM((reqs + 2 * prompts,), jnp.int32),
             pltpu.SemaphoreType.DMA((prompts + 3,)),

time: 95.4 us -> 95.5 us (level)
  no operation moved by 1% of the time
where the time goes in v5:
time: 95.5 us; the launch traced here: 95 us
  blocking collectives  38.2 us (40%)
  waiting for transfers between devices  25.7 us (27%)
  starting transfers between devices  16 us (17%)
  Pallas kernels  12.1 us (13%)
  local copies, waits for them, and re-layouts  1.5 us (2%)
    all_to_all x2, blocking collectives, exchange(): return lax.all_to_all(value, axis, split_axis=0, concat_axis=0, tiled=True)  38.2 us
    all_to_all x2, waiting for transfers between devices, exchange(): return lax.all_to_all(value, axis, split_axis=0, concat_axis=0, tiled=True)  25.7 us
    all_to_all x2, starting transfers between devices, exchange(): return lax.all_to_all(value, axis, split_axis=0, concat_axis=0, tiled=True)  16 us
    pallas_call x1, Pallas kernels, on_device(): pl.pallas_call(decode_scan_kernel, out_shape=(struct(decode_inputs.shape,...  2.83 us
    pallas_call x1, Pallas kernels, on_device(): pl.pallas_call(prompt_kernel, out_shape=(struct((prompt_rows, rank), F32)...  2.5 us
    pallas_call x1, Pallas kernels, on_device(): pl.pallas_call(prefill_kernel, out_shape=(struct(prompt_inputs.shape, BF1...  2.43 us
    pallas_call x1, Pallas kernels, on_device(): pl.pallas_call(pack_kernel, out_shape=struct((groups, ROWS0, channels), B...  2.24 us
  transfers between devices with their start and end apart: 2, of which 2 were waited for; matrix products, arithmetic and copies ran while one was open for 1% of the time, Pallas kernels for 6%

profile of v5, /device:TPU:1, one launch (start us, length us, event | category | flops | bytes accessed | tf_op | source)
XLA Modules:
  0.0 95.0 jit_solution(13322630934545069580)
XLA Ops:
  0.6 0.0 copy-start.11
  0.6 2.2 %pack.1 = bf16[16,24,512]{2,1,0:T(8,128)(2,1)} custom-call(s32[16]{0:T(128)} %mig_hbm.1, s32[8]{0:T(128)} %bitcast.13, s32[8]{0:T(128)} %len_hbm.1, bf16[3,16,512]{2,1,0:T(8,128)(2,1)} %bitcast.9, f32[16,16,512]{2,1,0:T(8,128)} %state_ref.1, bf16[8,16,512]{2,1,0:T(8,128)(2,1)} %u_hbm.1), custom_call_target="tpu_custom_call" | custom-call | tf_op jit(solution)/shard_map/pack/pallas_call | solution.py:572
  2.9 0.0 copy-start.2
  2.9 0.0 copy-start.4
  2.9 0.0 copy-start.6
  2.9 0.0 copy-start.7
  2.9 0.0 copy-start.15
  2.9 0.0 copy-start.17
  3.0 0.0 copy-start.18
  3.0 10.4 %all-to-all-start = ((bf16[16,24,512]{2,1,0:T(8,128)(2,1)}), bf16[16,24,512]{2,1,0:T(8,128)(2,1)S(1)}, u32[]{:S(2)}, u32[]{:S(2)}) async-start(bf16[16,24,512]{2,1,0:T(8,128)(2,1)} %pack.1), calls=%async_computation | async-start | bytes 786432 | tf_op jit(solution)/shard_map/all_to_all | solution.py:521
  13.3 0.0 copy-start.8
  13.4 0.0 copy-start.9
  13.4 0.0 copy-start.10
  13.4 0.0 copy-done.11
  13.4 0.0 copy-done.2
  13.4 0.0 copy-done.4
  13.4 0.0 copy-done.6
  13.4 0.0 copy-done.7
  13.4 0.0 copy-done.15
  13.4 0.0 copy-done.17
  13.5 0.0 copy-done.18
  13.5 0.6 copy-done.16
  14.0 0.0 copy-done.8
  14.0 0.0 copy-done.9
  14.0 0.0 copy-done.10
  14.0 2.5 %prompt_features.1 = (f32[128,512]{1,0:T(8,128)S(1)}, f32[128,32]{1,0:T(8,128)S(1)}, bf16[128,512]{1,0:T(8,128)(2,1)S(1)}, f32[128,512]{1,0:T(8,128)S(1)}, f32[4...) custom-call(s32[16]{0:T(128)S(1)} %copy-done.8, ...), custom_call_target="tpu_custom_call" | custom-call | flops 1000000000 | bytes 2000000 | tf_op jit(solution)/shard_map/prompt_features/pallas_call | solution.py:594
  16.6 11.3 %all-to-all-done.got_ref = bf16[16,24,512]{2,1,0:T(8,128)(2,1)S(1)} async-done(((bf16[16,24,512]{2,1,0:T(8,128)(2,1)}), bf16[16,24,512]{2,1,0:T(8,128)(2,1)S(1)}, u32[]{:S(2)}, u32[]{:S(2)}) %all-to-all-start) | async-done | bytes 393248 | tf_op jit(solution)/shard_map/all_to_all | solution.py:521
  27.9 0.0 copy-done.3
  27.9 0.0 copy-done.5
  27.9 0.7 decode_features.1
  28.6 0.0 copy-start.13
  28.6 23.5 %all_to_all.20.got_ref = bf16[32,7,4,128]{3,2,1,0:T(4,128)(2,1)S(1)} all-to-all(bf16[32,7,4,128]{3,2,1,0:T(4,128)(2,1)S(1)} %get-tuple-element.37), channel_id=1, replica_groups=mesh['group'=16,'mp'=32] {'mp'}, dimensions={0} | all-to-all | bytes 458752 | tf_op jit(solution)/shard_map/all_to_all | solution.py:521
  52.1 0.0 copy-done.13
  52.1 0.1 sum_parts.1
  52.2 14.7 %all_to_all.21.rows_ref = bf16[32,7,4,128]{3,2,1,0:T(4,128)(2,1)S(1)} all-to-all(bf16[32,7,4,128]{3,2,1,0:T(4,128)(2,1)S(1)} %sum_parts.1), channel_id=1, replica_groups=mesh['group'=16,'mp'=32] {'mp'}, dimensions={0} | all-to-all | bytes 458752 | tf_op jit(solution)/shard_map/all_to_all | solution.py:521
  67.0 0.0 copy-done
  67.0 2.4 %prefill_scan.1 = (bf16[8,16,512]{2,1,0:T(8,128)(2,1)}, bf16[16,144,128]{2,1,0:T(8,128)(2,1)}) custom-call(s32[32]{0:T(128)S(1)} %get-tuple-element.32.plan_ref, bf16[32,7,4,128]{3,2,1,0:T(4,128)(2,1)S(1)} %all_to_all.21.rows_ref, bf16[128,512]{1,0:T(8,128)(2,1)S(1)} %get-tuple-element.38.x_ref, ...), custom_call_target="tpu_custom_call", output_to_operand_aliasing={{1}: (9, {})} | custom-call | tf_op jit(solution)/shard_map/prefill_scan/pallas_call | solution.py:657
  69.4 0.0 copy-start.1
  69.4 0.0 copy-start.12
  69.4 5.7 %all-to-all-start.3 = ((bf16[16,144,128]{2,1,0:T(8,128)(2,1)}), bf16[16,144,128]{2,1,0:T(8,128)(2,1)S(1)}, u32[]{:S(2)}, u32[]{:S(2)}) async-start(bf16[16,144,128]{2,1,0:T(8,128)(2,1)} %get-tuple-element.43), calls=%async_computation.3 | async-start | bytes 1179648 | tf_op jit(solution)/shard_map/all_to_all | solution.py:521
  75.1 0.0 copy-done.1
  75.1 0.0 copy-done.12
  75.1 0.0 copy-start.14
  75.1 0.8 copy-done.14
  75.9 2.8 %decode_scan.1 = (bf16[16,4,512]{2,1,0:T(4,128)(2,1)}, f32[16,16,512]{2,1,0:T(8,128)}, f32[16,512]{1,0:T(8,128)S(1)}, f32[4,16,512]{2,1,0:T(8,128)S(1)}, f32[16,...) custom-call(s32[32]{0:T(128)S(1)} %get-tuple-element.32.plan_ref, ...), custom_call_target="tpu_custom_call" | custom-call | flops 6000000000 | bytes 8000000 | tf_op jit(solution)/shard_map/decode_scan/pallas_call | solution.py:683
  78.8 0.6 convert_bitcast_fusion
  79.4 14.3 %all-to-all-done.3.got_ref = bf16[16,144,128]{2,1,0:T(8,128)(2,1)S(1)} async-done(((bf16[16,144,128]{2,1,0:T(8,128)(2,1)}), bf16[16,144,128]{2,1,0:T(8,128)(2,1)S(1)}, u32[]{:S(2)}, u32[]{:S(2)}) %all-to-all-start.3) | async-done | bytes 589856 | tf_op jit(solution)/shard_map/all_to_all | solution.py:521
  93.7 1.3 %finish.1 = (bf16[16,4,512]{2,1,0:T(4,128)(2,1)}, f32[16,16,512]{2,1,0:T(8,128)}, f32[32,16,512]{2,1,0:T(8,128)}) custom-call(bf16[16,144,128]{2,1,0:T(8,128)(2,1)S(1)} %all-to-all-done.3.got_ref, f32[16,512]{1,0:T(8,128)S(1)} %get-tuple-element.45.base_ref, ...), custom_call_target="tpu_custom_call", output_to_operand_aliasing={{0}: (6, {}), {1}: (7, {})} | custom-call | tf_op jit(solution)/shard_map/finish/pallas_call | solution.py:717
  (4 shorter events, 0.0 us)
Async XLA Ops:
  0.6 12.8 %copy-start.11 = (bf16[8,16,512]{2,1,0:T(8,128)(2,1)S(1)}, bf16[8,16,512]{2,1,0:T(8,128)(2,1)}, u32[]{:S(2)}) copy-start(bf16[8,16,512]{2,1,0:T(8,128)(2,1)} %gate_ref.2) | copy-start | bytes 393220
  2.9 10.5 %copy-start.2 = (bf16[512,512]{1,0:T(8,128)(2,1)S(1)}, bf16[512,512]{1,0:T(8,128)(2,1)}, u32[]{:S(2)}) copy-start(bf16[512,512]{1,0:T(8,128)(2,1)} %rank_ref.3) | copy-start | bytes 1572868
  2.9 10.5 %copy-start.4 = (bf16[8,16,512]{2,1,0:T(8,128)(2,1)S(1)}, bf16[8,16,512]{2,1,0:T(8,128)(2,1)}, u32[]{:S(2)}) copy-start(bf16[8,16,512]{2,1,0:T(8,128)(2,1)} %u_hbm.1) | copy-start | bytes 393220
  2.9 10.5 %copy-start.6 = (bf16[512,32]{0,1:T(8,128)(2,1)S(1)}, bf16[512,32]{0,1:T(8,128)(2,1)}, u32[]{:S(2)}) copy-start(bf16[512,32]{0,1:T(8,128)(2,1)} %param.29) | copy-start | bytes 98308
  2.9 10.5 %copy-start.7 = (f32[4,512]{1,0:T(4,128)S(1)}, f32[4,512]{1,0:T(4,128)}, u32[]{:S(2)}) copy-start(f32[4,512]{1,0:T(4,128)} %cw_ref.3) | copy-start | bytes 24580
  2.9 10.5 %copy-start.15 = (f32[16,512]{1,0:T(8,128)S(1)}, f32[16,512]{1,0:T(8,128)}, u32[]{:S(2)}) copy-start(f32[16,512]{1,0:T(8,128)} %decay_ref.1) | copy-start | bytes 98308
  2.9 10.5 %copy-start.17 = (f32[512]{0:T(512)S(1)}, f32[512]{0:T(512)}, u32[]{:S(2)}) copy-start(f32[512]{0:T(512)} %param.31) | copy-start | bytes 6148
  3.0 10.5 %copy-start.18 = (f32[512]{0:T(512)S(1)}, f32[512]{0:T(512)}, u32[]{:S(2)}) copy-start(f32[512]{0:T(512)} %param.33) | copy-start | bytes 6148
  3.0 24.9 %all-to-all-start = ((bf16[16,24,512]{2,1,0:T(8,128)(2,1)}), bf16[16,24,512]{2,1,0:T(8,128)(2,1)S(1)}, u32[]{:S(2)}, u32[]{:S(2)}) async-start(bf16[16,24,512]{2,1,0:T(8,128)(2,1)} %pack.1), calls=%async_computation | async-start | bytes 786432 | tf_op jit(solution)/shard_map/all_to_all | solution.py:521
  13.3 0.7 copy-start.16
  13.3 0.7 copy-start.8
  13.4 0.7 copy-start.9
  13.4 0.7 copy-start.10
  14.0 13.8 %copy-start.3 = (bf16[16,3,512]{2,0,1:T(8,128)(2,1)S(1)}, bf16[16,3,512]{2,0,1:T(8,128)(2,1)}, u32[]{:S(2)}) copy-start(bf16[16,3,512]{2,0,1:T(8,128)(2,1)} %param.18) | copy-start | bytes 147460
  14.0 13.8 %copy-start.5 = (bf16[16,4,512]{2,1,0:T(4,128)(2,1)S(1)}, bf16[16,4,512]{2,1,0:T(4,128)(2,1)}, u32[]{:S(2)}) copy-start(bf16[16,4,512]{2,1,0:T(4,128)(2,1)} %u_ref.5) | copy-start | bytes 196612
  28.6 23.5 %copy-start.13 = (bf16[64,512]{1,0:T(8,128)(2,1)}, bf16[64,512]{1,0:T(8,128)(2,1)S(1)}, u32[]{:S(2)}) copy-start(bf16[64,512]{1,0:T(8,128)(2,1)S(1)} %get-tuple-element.44.x_ref) | copy-start | bytes 196612
  52.1 14.8 %copy-start = (bf16[512,512]{1,0:T(8,128)(2,1)S(1)}, bf16[512,512]{1,0:T(8,128)(2,1)}, u32[]{:S(2)}) copy-start(bf16[512,512]{1,0:T(8,128)(2,1)} %step_w_ref.3) | copy-start | bytes 1572868
  69.4 5.7 %copy-start.1 = (f32[16,16,512]{2,1,0:T(8,128)S(1)}, f32[16,16,512]{2,1,0:T(8,128)}, u32[]{:S(2)}) copy-start(f32[16,16,512]{2,1,0:T(8,128)} %state_ref.1) | copy-start | bytes 1572868
  69.4 5.7 %copy-start.12 = (bf16[16,4,512]{2,1,0:T(4,128)(2,1)S(1)}, bf16[16,4,512]{2,1,0:T(4,128)(2,1)}, u32[]{:S(2)}) copy-start(bf16[16,4,512]{2,1,0:T(4,128)(2,1)} %gate_ref.3) | copy-start | bytes 196612
  69.4 24.3 %all-to-all-start.3 = ((bf16[16,144,128]{2,1,0:T(8,128)(2,1)}), bf16[16,144,128]{2,1,0:T(8,128)(2,1)S(1)}, u32[]{:S(2)}, u32[]{:S(2)}) async-start(bf16[16,144,128]{2,1,0:T(8,128)(2,1)} %get-tuple-element.43), calls=%async_computation.3 | async-start | bytes 1179648 | tf_op jit(solution)/shard_map/all_to_all | solution.py:521
  75.1 0.8 copy-start.14

commit v6 on v4

--- a/solution.py
+++ b/solution.py
@@ -67,7 +67,8 @@
 
 
 def pack_kernel(
-    mig_ref, dest_ref, len_ref, conv_ref, state_ref, u_ref, pay_ref, scr, conv_scr, u_scr
+    mig_ref, dest_ref, len_ref, conv_ref, state_ref, u_ref, pay_ref, scr, conv_scr, u_scr, out_scr,
+    sems,
 ):
     groups = pay_ref.shape[0]
     _, reqs, channels = conv_ref.shape
@@ -111,8 +112,17 @@
         state = state_ref[picks[k]]
         for n in range(states):
             scr[n, STATE_ROW + k : STATE_ROW + k + 1, :] = state[n : n + 1, :]
+    copies = []
     for d in range(groups):
-        pay_ref[d] = scr[d].astype(BF16)
+        out_scr[d] = scr[d].astype(BF16)
+        if d % 4 == 3:
+            here = pl.ds(d - 3, 4)
+            copies.append(
+                pltpu.make_async_copy(out_scr.at[here], pay_ref.at[here], sems.at[d // 4])
+            )
+            copies[-1].start()
+    for copy in copies:
+        copy.wait()
 
 
 def put_lanes(ref, start, value):
@@ -340,11 +350,12 @@
 
 
 def prefill_kernel(
-    plan_ref, rows_ref, x_ref, gate_ref, step_w_ref, decay_ref, extra_ref, relay_ref,
-    items_ref, _empty, out_ref, pay_ref, low_scr, sel_scr, step_scr, x_scr, h_scr, y_scr,
-    final_scr, out_scr, plan_scr, sems,
+    plan_ref, rows_ref, x_ref, step_w_ref, decay_ref, extra_ref, relay_ref, items_ref, _empty,
+    sum_ref, pay_ref, low_scr, sel_scr, step_scr, x_scr, sum_scr, h_scr, final_scr, plan_scr, sems,
 ):
-    prompts, steps, channels = out_ref.shape
+    prompts = final_scr.shape[0]
+    total_rows, channels = sum_scr.shape
+    steps = total_rows // prompts
     states = decay_ref.shape[1] // 8
     reqs = plan_ref.shape[0] - 2 * prompts
     groups, blocks, four, _ = pay_ref.shape
@@ -356,18 +367,48 @@
     take_tiles(rows_ref, 0, low_scr, sel_scr)
     step_scr[...] = steps_of(low_scr, step_w_ref, extra_ref[0:1, :])
     x_scr[...] = x_ref[...].astype(F32)
-    h_scr[...] = jnp.zeros(h_scr.shape, F32)
     lengths = items_ref[2 * reqs :, :]
     skip = extra_ref[1:2, :]
+    lanes = range(channels // LANES)
     for t in range(steps):
-        scan(
-            t, prompts, t < lengths, x_scr, gate_ref, sel_scr, step_scr, decay_ref, skip, h_scr,
-            y_scr, steps,
-        )
+        rows = slice(t * prompts, (t + 1) * prompts)
+        for l in lanes:
+            cols = slice(l * LANES, (l + 1) * LANES)
+            x_l = x_scr[rows, cols]
+            step_l = jnp.where(t < lengths, step_scr[rows, cols], 0.0)
+            step_scr[rows, cols] = step_l
+            sum_scr[rows, cols] = skip[:, cols] * x_l
+            x_scr[rows, cols] = step_l * x_l
+    for first in range(0, states, 4):
+        names = range(first, first + 4)
+        decay = [[decay_ref[l, prompts * n : prompts * (n + 1), :] for l in lanes] for n in names]
+        held = [[None for _ in lanes] for _ in names]
+        for t in range(steps):
+            rows = slice(t * prompts, (t + 1) * prompts)
+            pair = sel_scr[rows, :]
+            shape = (prompts, LANES)
+            bs = [jnp.broadcast_to(pair[:, n : n + 1], shape) for n in names]
+            cs = [jnp.broadcast_to(pair[:, states + n : states + n + 1], shape) for n in names]
+            for l in lanes:
+                cols = slice(l * LANES, (l + 1) * LANES)
+                step_l, drive = step_scr[rows, cols], x_scr[rows, cols]
+                y = sum_scr[rows, cols]
+                for n in range(4):
+                    h = drive * bs[n]
+                    if t:
+                        h = h + jnp.exp2(step_l * decay[n][l]) * held[n][l]
+                    held[n][l] = h
+                    y = y + cs[n] * h
+                sum_scr[rows, cols] = y
+        for n in range(4):
+            for l in lanes:
+                at = (first + n) * prompts
+                h_scr[l, at : at + prompts, :] = held[n][l]
+    copies = [pltpu.make_async_copy(sum_scr, sum_ref, sems.at[2 + prompts])]
+    copies[0].start()
     plan_copy.wait()
     dests, ranks = slots_of(plan_scr, prompts, reqs)
     passed.wait()
-    copies = []
     for i in range(prompts):
         for l in range(channels // LANES):
             cols = slice(l * LANES, (l + 1) * LANES)
@@ -378,20 +419,14 @@
         place = pay_ref.at[dests[i], pl.ds(ranks[i] * parts, parts)]
         copies.append(pltpu.make_async_copy(final_scr.at[i], place, sems.at[2 + i]))
         copies[-1].start()
-    for i in range(prompts):
-        for l in range(channels // LANES):
-            cols = slice(l * LANES, (l + 1) * LANES)
-            out_scr[i, :, cols] = y_scr[l, i * steps : (i + 1) * steps, :].astype(BF16)
-    copies.append(pltpu.make_async_copy(out_scr, out_ref, sems.at[2 + prompts]))
-    copies[-1].start()
     for copy in copies:
         copy.wait()
 
 
 def decode_scan_kernel(
     plan_ref, rows_ref, x_ref, u_ref, gate_ref, state_ref, step_w_ref, decay_ref, extra_ref,
-    got_ref, out_ref, final_ref, base_ref, held_ref, weight_ref, keep_ref, pick_ref,
-    final_conv_ref, prompt_conv_ref, low_scr, sel_scr, step_scr, x_scr, gate_scr, scr, h_scr, y_scr,
+    got_ref, sum_ref, prompt_gate_ref, items_ref, out_ref, final_ref, base_ref, held_ref, weight_ref,
+    keep_ref, pick_ref, final_conv_ref, prompt_conv_ref, prefill_ref, prefill_scr, low_scr, sel_scr, step_scr, x_scr, gate_scr, scr, h_scr, y_scr,
     conv_scr,
 ):
     reqs, steps, channels = gate_ref.shape
@@ -450,6 +485,16 @@
                 at = TAIL_ROW + 3 * q + j
                 conv_scr[j, s * PAIR + q : s * PAIR + q + 1, :] = block[at : at + 1]
     prompt_conv_ref[...] = conv_scr[...].astype(BF16)
+    prompts, length, _ = prefill_ref.shape
+    lengths = items_ref[2 * reqs :, :]
+    for l in range(lanes):
+        cols = slice(l * LANES, (l + 1) * LANES)
+        for t in range(length):
+            rows = slice(t * prompts, (t + 1) * prompts)
+            out = jnp.where(t < lengths, sum_ref[rows, cols] * prompt_gate_ref[rows, cols], 0.0)
+            prefill_scr[l, pl.ds(t, prompts, stride=length), :] = out
+        for i in range(prompts):
+            prefill_ref[i, :, cols] = prefill_scr[l, i * length : (i + 1) * length, :].astype(BF16)
 
 
 def finish_kernel(
@@ -556,11 +601,13 @@
         pack_kernel,
         out_shape=struct((groups, ROWS0, channels), BF16),
         in_specs=[SMEM] * 3 + [VMEM] * 3,
-        out_specs=VMEM,
+        out_specs=anywhere,
         scratch_shapes=[
             scratch((groups + 1, ROWS0, channels)),
             scratch((3 * reqs, channels)),
             scratch((prompts * (steps + 8), channels)),
+            pltpu.VMEM((groups, ROWS0, channels), BF16),
+            pltpu.SemaphoreType.DMA((groups // 4,)),
         ],
         compiler_params=ALL_VMEM,
         name="pack",
@@ -629,33 +676,31 @@
     )(parts)
     rows = exchange(shares, "mp")
 
-    prefill_out, send_final = pl.pallas_call(
+    prompt_sum, send_final = pl.pallas_call(
         prefill_kernel,
-        out_shape=(
-            struct(prompt_inputs.shape, BF16),
-            struct(send_shape, BF16),
-        ),
-        in_specs=[anywhere] + [VMEM] * 8 + [anywhere],
-        out_specs=(anywhere,) * 2,
+        out_shape=(struct((prompt_rows, channels), F32), struct(send_shape, BF16)),
+        in_specs=[anywhere] + [VMEM] * 7 + [anywhere],
+        out_specs=(anywhere, anywhere),
         scratch_shapes=[
             scratch((prompt_rows, rank)),
             scratch((prompt_rows, LANES)),
             scratch((prompt_rows, channels)),
             scratch((prompt_rows, channels)),
+            scratch((prompt_rows, channels)),
             scratch((tiles, prompts * states, LANES)),
-            scratch((tiles, prompt_rows, LANES)),
             pltpu.VMEM((prompts, states // MIG, MIG, channels), BF16),
-            pltpu.VMEM(prompt_inputs.shape, BF16),
             pltpu.SMEM((reqs + 2 * prompts,), jnp.int32),
             pltpu.SemaphoreType.DMA((prompts + 3,)),
         ],
-        input_output_aliases={9: 1},
+        input_output_aliases={8: 1},
         compiler_params=PARAMS,
         name="prefill_scan",
-    )(plan, rows, prompt_x, gate_rows, step_weight, decay, extra, relay, items, empty)
+    )(plan, rows, prompt_x, step_weight, decay, extra, relay, items, empty)
     got_final = exchange(send_final, "group")
 
-    early_out, early_final, base, held, weight, keep, pick, final_conv, prompt_conv = pl.pallas_call(
+    (
+        early_out, early_final, base, held, weight, keep, pick, final_conv, prompt_conv, prefill_out,
+    ) = pl.pallas_call(
         decode_scan_kernel,
         out_shape=(
             struct(decode_inputs.shape, BF16),
@@ -667,10 +712,12 @@
             struct((8, LANES), F32),
             struct((3, reqs, channels), F32),
             struct((3, groups * PAIR, channels), BF16),
+            struct(prompt_inputs.shape, BF16),
         ),
-        in_specs=[SMEM] + [VMEM] * 9,
-        out_specs=(VMEM,) * 9,
+        in_specs=[SMEM] + [VMEM] * 12,
+        out_specs=(VMEM,) * 10,
         scratch_shapes=[
+            scratch((tiles, prompt_rows, LANES)),
             scratch((decode_rows, rank)),
             scratch((decode_rows, LANES)),
             scratch((decode_rows, channels)),
@@ -686,7 +733,7 @@
         name="decode_scan",
     )(
         plan, rows, decode_x, decode_inputs, decode_gates, resident_state, step_weight, decay,
-        extra, got_first,
+        extra, got_first, prompt_sum, gate_rows, items,
     )
 
     decode_out, final_state, prompt_state = pl.pallas_call(

time: 95.4 us -> 95.9 us (level)
  local copies, waits for them, and re-layouts: 1.5 us -> 4.77 us
  waiting for transfers between devices: 25.7 us -> 23.1 us
    unnamed x38 -> x46, local copies, waits for them, and re-layouts: 1.5 us -> 4.77 us
    all_to_all x2, waiting for transfers between devices: 25.7 us -> 23.1 us  [exchange(): return lax.all_to_all(value, axis, split_axis=0, concat_axis=0, tiled=True)]
where the time goes in v6:
time: 95.9 us; the launch traced here: 95.3 us
  blocking collectives  38.2 us (40%)
  waiting for transfers between devices  23.1 us (24%)
  starting transfers between devices  15.9 us (17%)
  Pallas kernels  11.9 us (12%)
  local copies, waits for them, and re-layouts  4.77 us (5%)
    all_to_all x2, blocking collectives, exchange(): return lax.all_to_all(value, axis, split_axis=0, concat_axis=0, tiled=True)  38.2 us
    all_to_all x2, waiting for transfers between devices, exchange(): return lax.all_to_all(value, axis, split_axis=0, concat_axis=0, tiled=True)  23.1 us
    all_to_all x2, starting transfers between devices, exchange(): return lax.all_to_all(value, axis, split_axis=0, concat_axis=0, tiled=True)  15.9 us
    unnamed x46, local copies, waits for them, and re-layouts  4.77 us
    pallas_call x1, Pallas kernels, on_device(): pl.pallas_call(decode_scan_kernel, out_shape=(struct(decode_inputs.shape,...  2.87 us
    pallas_call x1, Pallas kernels, on_device(): pl.pallas_call(prompt_kernel, out_shape=(struct((prompt_rows, rank), F32)...  2.45 us
    pallas_call x1, Pallas kernels, on_device(): pl.pallas_call(prefill_kernel, out_shape=(struct((prompt_rows, channels),...  2.27 us
    pallas_call x1, Pallas kernels, on_device(): pl.pallas_call(pack_kernel, out_shape=struct((groups, ROWS0, channels), B...  2.21 us
  transfers between devices with their start and end apart: 2, of which 2 were waited for; matrix products, arithmetic and copies ran while one was open for 1% of the time, Pallas kernels for 6%

profile of v6, /device:TPU:1, one launch (start us, length us, event | category | flops | bytes accessed | tf_op | source)
XLA Modules:
  0.0 95.3 jit_solution(1269520979883876839)
XLA Ops:
  0.6 0.0 copy-start.13
  0.6 2.2 %pack.1 = bf16[16,24,512]{2,1,0:T(8,128)(2,1)} custom-call(s32[16]{0:T(128)} %mig_ref.3, s32[8]{0:T(128)} %bitcast.13, s32[8]{0:T(128)} %len_ref.3, bf16[3,16,512]{2,1,0:T(8,128)(2,1)} %bitcast.9, f32[16,16,512]{2,1,0:T(8,128)} %state_ref.3, bf16[8,16,512]{2,1,0:T(8,128)(2,1)} %u_ref.5), custom_call_target="tpu_custom_call" | custom-call | tf_op jit(solution)/shard_map/pack/pallas_call | solution.py:600
  2.9 0.0 copy-start.1
  2.9 0.0 copy-start.4
  2.9 0.0 copy-start.6
  2.9 0.0 copy-start.7
  2.9 0.0 copy-start.17
  2.9 0.0 copy-start.19
  2.9 0.0 copy-start.20
  2.9 10.4 %all-to-all-start = ((bf16[16,24,512]{2,1,0:T(8,128)(2,1)}), bf16[16,24,512]{2,1,0:T(8,128)(2,1)S(1)}, u32[]{:S(2)}, u32[]{:S(2)}) async-start(bf16[16,24,512]{2,1,0:T(8,128)(2,1)} %pack.1), calls=%async_computation | async-start | bytes 786432 | tf_op jit(solution)/shard_map/all_to_all | solution.py:549
  13.3 0.0 copy-start.8
  13.3 0.0 copy-start.9
  13.3 0.0 copy-start.10
  13.3 0.0 copy-done.13
  13.4 0.0 copy-done.1
  13.4 0.0 copy-done.4
  13.4 0.0 copy-done.6
  13.4 0.0 copy-done.7
  13.4 0.0 copy-done.17
  13.4 0.0 copy-done.19
  13.4 0.0 copy-done.20
  13.4 0.6 copy-done.18
  14.0 0.0 copy-done.8
  14.0 0.0 copy-done.9
  14.0 0.0 copy-done.10
  14.0 2.4 %prompt_features.1 = (f32[128,512]{1,0:T(8,128)S(1)}, f32[128,32]{1,0:T(8,128)S(1)}, bf16[128,512]{1,0:T(8,128)(2,1)S(1)}, f32[128,512]{1,0:T(8,128)S(1)}, f32[4...) custom-call(s32[16]{0:T(128)S(1)} %copy-done.8, ...), custom_call_target="tpu_custom_call" | custom-call | flops 1000000000 | bytes 2000000 | tf_op jit(solution)/shard_map/prompt_features/pallas_call | solution.py:617
  16.5 0.7 copy-done.21
  17.2 10.7 %all-to-all-done.got_ref = bf16[16,24,512]{2,1,0:T(8,128)(2,1)S(1)} async-done(((bf16[16,24,512]{2,1,0:T(8,128)(2,1)}), bf16[16,24,512]{2,1,0:T(8,128)(2,1)S(1)}, u32[]{:S(2)}, u32[]{:S(2)}) %all-to-all-start) | async-done | bytes 393248 | tf_op jit(solution)/shard_map/all_to_all | solution.py:549
  27.9 0.0 copy-done.3
  27.9 0.7 decode_features.1
  28.6 0.0 copy-start.15
  28.6 23.5 %all_to_all.20.got_ref = bf16[32,7,4,128]{3,2,1,0:T(4,128)(2,1)S(1)} all-to-all(bf16[32,7,4,128]{3,2,1,0:T(4,128)(2,1)S(1)} %get-tuple-element.38), channel_id=1, replica_groups=mesh['group'=16,'mp'=32] {'mp'}, dimensions={0} | all-to-all | bytes 458752 | tf_op jit(solution)/shard_map/all_to_all | solution.py:549
  52.1 0.1 sum_parts.1
  52.2 14.7 %all_to_all.21.rows_ref = bf16[32,7,4,128]{3,2,1,0:T(4,128)(2,1)S(1)} all-to-all(bf16[32,7,4,128]{3,2,1,0:T(4,128)(2,1)S(1)} %sum_parts.1), channel_id=1, replica_groups=mesh['group'=16,'mp'=32] {'mp'}, dimensions={0} | all-to-all | bytes 458752 | tf_op jit(solution)/shard_map/all_to_all | solution.py:549
  66.9 2.3 %prefill_scan.1 = (f32[128,512]{1,0:T(8,128)S(1)}, bf16[16,9,4,512]{3,2,1,0:T(4,128)(2,1)}) custom-call(s32[32]{0:T(128)S(1)} %get-tuple-element.33.plan_ref, bf16[32,7,4,128]{3,2,1,0:T(4,128)(2,1)S(1)} %all_to_all.21.rows_ref, bf16[128,512]{1,0:T(8,128)(2,1)S(1)} %get-tuple-element.39.x_ref, ...), custom_call_target="tpu_custom_call", output_to_operand_aliasing={{1}: (8, {})} | custom-call | tf_op jit(solution)/shard_map/prefill_scan/pallas_call | solution.py:679
  69.2 0.0 copy-start.11
  69.2 0.0 copy-start
  69.2 0.0 copy-start.14
  69.2 0.7 copy-done.11
  69.9 5.5 %all-to-all-start.3 = ((bf16[16,9,4,512]{3,2,1,0:T(4,128)(2,1)}), bf16[16,9,4,512]{3,2,1,0:T(4,128)(2,1)S(1)}, u32[]{:S(2)}, u32[]{:S(2)}) async-start(bf16[16,9,4,512]{3,2,1,0:T(4,128)(2,1)} %get-tuple-element.43), calls=%async_computation.3 | async-start | bytes 1179648 | tf_op jit(solution)/shard_map/all_to_all | solution.py:549
  75.4 0.0 copy-start.12
  75.4 0.9 copy-done.12
  76.4 0.8 copy-done.16
  77.2 0.9 copy-done.22
  78.2 2.9 %decode_scan.1 = (bf16[16,4,512]{2,1,0:T(4,128)(2,1)}, f32[16,16,512]{2,1,0:T(8,128)}, f32[16,512]{1,0:T(8,128)S(1)}, f32[4,16,512]{2,1,0:T(8,128)S(1)}, f32[16,...) custom-call(s32[32]{0:T(128)S(1)} %get-tuple-element.33.plan_ref, ...), custom_call_target="tpu_custom_call" | custom-call | flops 6000000000 | bytes 8000000 | tf_op jit(solution)/shard_map/decode_scan/pallas_call | solution.py:703
  81.0 0.6 convert_bitcast_fusion
  81.7 12.4 %all-to-all-done.3.got_ref = bf16[16,9,4,512]{3,2,1,0:T(4,128)(2,1)S(1)} async-done(((bf16[16,9,4,512]{3,2,1,0:T(4,128)(2,1)}), bf16[16,9,4,512]{3,2,1,0:T(4,128)(2,1)S(1)}, u32[]{:S(2)}, u32[]{:S(2)}) %all-to-all-start.3) | async-done | bytes 589856 | tf_op jit(solution)/shard_map/all_to_all | solution.py:549
  94.1 1.3 %finish.1 = (bf16[16,4,512]{2,1,0:T(4,128)(2,1)}, f32[16,16,512]{2,1,0:T(8,128)}, f32[32,16,512]{2,1,0:T(8,128)}) custom-call(bf16[16,9,4,512]{3,2,1,0:T(4,128)(2,1)S(1)} %all-to-all-done.3.got_ref, f32[16,512]{1,0:T(8,128)S(1)} %get-tuple-element.47.base_ref, ...), custom_call_target="tpu_custom_call", output_to_operand_aliasing={{0}: (6, {}), {1}: (7, {})} | custom-call | tf_op jit(solution)/shard_map/finish/pallas_call | solution.py:739
  (12 shorter events, 0.0 us)
Async XLA Ops:
  0.6 12.7 %copy-start.13 = (bf16[8,16,512]{2,1,0:T(8,128)(2,1)S(1)}, bf16[8,16,512]{2,1,0:T(8,128)(2,1)}, u32[]{:S(2)}) copy-start(bf16[8,16,512]{2,1,0:T(8,128)(2,1)} %gate_ref.2) | copy-start | bytes 393220
  2.9 10.5 %copy-start.1 = (bf16[512,512]{1,0:T(8,128)(2,1)S(1)}, bf16[512,512]{1,0:T(8,128)(2,1)}, u32[]{:S(2)}) copy-start(bf16[512,512]{1,0:T(8,128)(2,1)} %rank_ref.3) | copy-start | bytes 1572868
  2.9 10.5 %copy-start.4 = (bf16[8,16,512]{2,1,0:T(8,128)(2,1)S(1)}, bf16[8,16,512]{2,1,0:T(8,128)(2,1)}, u32[]{:S(2)}) copy-start(bf16[8,16,512]{2,1,0:T(8,128)(2,1)} %u_ref.5) | copy-start | bytes 393220
  2.9 10.5 %copy-start.6 = (bf16[512,32]{0,1:T(8,128)(2,1)S(1)}, bf16[512,32]{0,1:T(8,128)(2,1)}, u32[]{:S(2)}) copy-start(bf16[512,32]{0,1:T(8,128)(2,1)} %param.29) | copy-start | bytes 98308
  2.9 10.5 %copy-start.7 = (f32[4,512]{1,0:T(4,128)S(1)}, f32[4,512]{1,0:T(4,128)}, u32[]{:S(2)}) copy-start(f32[4,512]{1,0:T(4,128)} %cw_ref.3) | copy-start | bytes 24580
  2.9 10.5 %copy-start.17 = (f32[16,512]{1,0:T(8,128)S(1)}, f32[16,512]{1,0:T(8,128)}, u32[]{:S(2)}) copy-start(f32[16,512]{1,0:T(8,128)} %decay_ref.1) | copy-start | bytes 98308
  2.9 10.5 %copy-start.19 = (f32[512]{0:T(512)S(1)}, f32[512]{0:T(512)}, u32[]{:S(2)}) copy-start(f32[512]{0:T(512)} %param.31) | copy-start | bytes 6148
  2.9 10.5 %copy-start.20 = (f32[512]{0:T(512)S(1)}, f32[512]{0:T(512)}, u32[]{:S(2)}) copy-start(f32[512]{0:T(512)} %param.33) | copy-start | bytes 6148
  2.9 24.9 %all-to-all-start = ((bf16[16,24,512]{2,1,0:T(8,128)(2,1)}), bf16[16,24,512]{2,1,0:T(8,128)(2,1)S(1)}, u32[]{:S(2)}, u32[]{:S(2)}) async-start(bf16[16,24,512]{2,1,0:T(8,128)(2,1)} %pack.1), calls=%async_computation | async-start | bytes 786432 | tf_op jit(solution)/shard_map/all_to_all | solution.py:549
  13.3 0.7 copy-start.18
  13.3 0.7 copy-start.8
  13.3 0.7 copy-start.9
  13.3 0.7 copy-start.10
  14.0 13.8 %copy-start.3 = (bf16[16,3,512]{2,0,1:T(8,128)(2,1)S(1)}, bf16[16,3,512]{2,0,1:T(8,128)(2,1)}, u32[]{:S(2)}) copy-start(bf16[16,3,512]{2,0,1:T(8,128)(2,1)} %param.18) | copy-start | bytes 147460
  14.0 13.8 %copy-start.5 = (bf16[16,4,512]{2,1,0:T(4,128)(2,1)S(1)}, bf16[16,4,512]{2,1,0:T(4,128)(2,1)}, u32[]{:S(2)}) copy-start(bf16[16,4,512]{2,1,0:T(4,128)(2,1)} %u_ref.7) | copy-start | bytes 196612
  16.5 0.7 copy-start.21
  28.6 23.5 %copy-start.15 = (bf16[64,512]{1,0:T(8,128)(2,1)}, bf16[64,512]{1,0:T(8,128)(2,1)S(1)}, u32[]{:S(2)}) copy-start(bf16[64,512]{1,0:T(8,128)(2,1)S(1)} %get-tuple-element.44.x_ref) | copy-start | bytes 196612
  52.1 14.8 %copy-start.2 = (bf16[512,512]{1,0:T(8,128)(2,1)S(1)}, bf16[512,512]{1,0:T(8,128)(2,1)}, u32[]{:S(2)}) copy-start(bf16[512,512]{1,0:T(8,128)(2,1)} %step_w_ref.3) | copy-start | bytes 1572868
  69.2 0.7 copy-start.11
  69.2 6.2 %copy-start = (f32[16,16,512]{2,1,0:T(8,128)S(1)}, f32[16,16,512]{2,1,0:T(8,128)}, u32[]{:S(2)}) copy-start(f32[16,16,512]{2,1,0:T(8,128)} %state_ref.3) | copy-start | bytes 1572868
  69.2 6.2 %copy-start.14 = (bf16[16,4,512]{2,1,0:T(4,128)(2,1)S(1)}, bf16[16,4,512]{2,1,0:T(4,128)(2,1)}, u32[]{:S(2)}) copy-start(bf16[16,4,512]{2,1,0:T(4,128)(2,1)} %gate_ref.3) | copy-start | bytes 196612
  69.9 24.2 %all-to-all-start.3 = ((bf16[16,9,4,512]{3,2,1,0:T(4,128)(2,1)}), bf16[16,9,4,512]{3,2,1,0:T(4,128)(2,1)S(1)}, u32[]{:S(2)}, u32[]{:S(2)}) async-start(bf16[16,9,4,512]{3,2,1,0:T(4,128)(2,1)} %get-tuple-element.43), calls=%async_computation.3 | async-start | bytes 1179648 | tf_op jit(solution)/shard_map/all_to_all | solution.py:549
  75.4 1.0 copy-start.12
  76.4 0.8 copy-start.16
  77.2 0.9 copy-start.22

commit v7 on v4

--- a/solution.py
+++ b/solution.py
@@ -341,7 +341,7 @@
 
 def prefill_kernel(
     plan_ref, rows_ref, x_ref, gate_ref, step_w_ref, decay_ref, extra_ref, relay_ref,
-    items_ref, _empty, out_ref, pay_ref, low_scr, sel_scr, step_scr, x_scr, h_scr, y_scr,
+    items_ref, _empty, out_ref, pay_ref, low_scr, sel_scr, step_scr, x_scr, sum_scr, h_scr, y_scr,
     final_scr, out_scr, plan_scr, sems,
 ):
     prompts, steps, channels = out_ref.shape
@@ -356,14 +356,49 @@
     take_tiles(rows_ref, 0, low_scr, sel_scr)
     step_scr[...] = steps_of(low_scr, step_w_ref, extra_ref[0:1, :])
     x_scr[...] = x_ref[...].astype(F32)
-    h_scr[...] = jnp.zeros(h_scr.shape, F32)
     lengths = items_ref[2 * reqs :, :]
     skip = extra_ref[1:2, :]
+    lanes = range(channels // LANES)
     for t in range(steps):
-        scan(
-            t, prompts, t < lengths, x_scr, gate_ref, sel_scr, step_scr, decay_ref, skip, h_scr,
-            y_scr, steps,
-        )
+        rows = slice(t * prompts, (t + 1) * prompts)
+        for l in lanes:
+            cols = slice(l * LANES, (l + 1) * LANES)
+            x_l = x_scr[rows, cols]
+            step_l = jnp.where(t < lengths, step_scr[rows, cols], 0.0)
+            step_scr[rows, cols] = step_l
+            sum_scr[rows, cols] = skip[:, cols] * x_l
+            x_scr[rows, cols] = step_l * x_l
+    for first in range(0, states, 4):
+        names = range(first, first + 4)
+        decay = [[decay_ref[l, prompts * n : prompts * (n + 1), :] for l in lanes] for n in names]
+        held = [[None for _ in lanes] for _ in names]
+        for t in range(steps):
+            rows = slice(t * prompts, (t + 1) * prompts)
+            pair = sel_scr[rows, :]
+            shape = (prompts, LANES)
+            bs = [jnp.broadcast_to(pair[:, n : n + 1], shape) for n in names]
+            cs = [jnp.broadcast_to(pair[:, states + n : states + n + 1], shape) for n in names]
+            for l in lanes:
+                cols = slice(l * LANES, (l + 1) * LANES)
+                step_l, drive = step_scr[rows, cols], x_scr[rows, cols]
+                y = sum_scr[rows, cols]
+                for n in range(4):
+                    h = drive * bs[n]
+                    if t:
+                        h = h + jnp.exp2(step_l * decay[n][l]) * held[n][l]
+                    held[n][l] = h
+                    y = y + cs[n] * h
+                sum_scr[rows, cols] = y
+        for n in range(4):
+            for l in lanes:
+                at = (first + n) * prompts
+                h_scr[l, at : at + prompts, :] = held[n][l]
+    for t in range(steps):
+        rows = slice(t * prompts, (t + 1) * prompts)
+        for l in lanes:
+            cols = slice(l * LANES, (l + 1) * LANES)
+            out = jnp.where(t < lengths, sum_scr[rows, cols] * gate_ref[rows, cols], 0.0)
+            y_scr[l, pl.ds(t, prompts, stride=steps), :] = out
     plan_copy.wait()
     dests, ranks = slots_of(plan_scr, prompts, reqs)
     passed.wait()
@@ -640,6 +675,7 @@
         scratch_shapes=[
             scratch((prompt_rows, rank)),
             scratch((prompt_rows, LANES)),
+            scratch((prompt_rows, channels)),
             scratch((prompt_rows, channels)),
             scratch((prompt_rows, channels)),
             scratch((tiles, prompts * states, LANES)),

time: 95.4 us -> 95.4 us (level)
  no operation moved by 1% of the time
where the time goes in v7:
time: 95.4 us; the launch traced here: 94.9 us
  blocking collectives  38.2 us (40%)
  waiting for transfers between devices  25.7 us (27%)
  starting transfers between devices  16 us (17%)
  Pallas kernels  12 us (13%)
  local copies, waits for them, and re-layouts  1.5 us (2%)
    all_to_all x2, blocking collectives, exchange(): return lax.all_to_all(value, axis, split_axis=0, concat_axis=0, tiled=True)  38.2 us
    all_to_all x2, waiting for transfers between devices, exchange(): return lax.all_to_all(value, axis, split_axis=0, concat_axis=0, tiled=True)  25.7 us
    all_to_all x2, starting transfers between devices, exchange(): return lax.all_to_all(value, axis, split_axis=0, concat_axis=0, tiled=True)  16 us
    pallas_call x1, Pallas kernels, on_device(): pl.pallas_call(decode_scan_kernel, out_shape=(struct(decode_inputs.shape,...  2.83 us
    pallas_call x1, Pallas kernels, on_device(): pl.pallas_call(prompt_kernel, out_shape=(struct((prompt_rows, rank), F32)...  2.45 us
    pallas_call x1, Pallas kernels, on_device(): pl.pallas_call(prefill_kernel, out_shape=(struct(prompt_inputs.shape, BF1...  2.42 us
    pallas_call x1, Pallas kernels, on_device(): pl.pallas_call(pack_kernel, out_shape=struct((groups, ROWS0, channels), B...  2.21 us
  transfers between devices with their start and end apart: 2, of which 2 were waited for; matrix products, arithmetic and copies ran while one was open for 1% of the time, Pallas kernels for 6%

profile of v7, /device:TPU:1, one launch (start us, length us, event | category | flops | bytes accessed | tf_op | source)
XLA Modules:
  0.0 94.9 jit_solution(18160049045307938146)
XLA Ops:
  0.6 0.0 copy-start.11
  0.6 2.2 %pack.1 = bf16[16,24,512]{2,1,0:T(8,128)(2,1)} custom-call(s32[16]{0:T(128)} %mig_ref.3, s32[8]{0:T(128)} %bitcast.13, s32[8]{0:T(128)} %len_ref.3, bf16[3,16,512]{2,1,0:T(8,128)(2,1)} %bitcast.9, f32[16,16,512]{2,1,0:T(8,128)} %state_ref.3, bf16[8,16,512]{2,1,0:T(8,128)(2,1)} %u_ref.5), custom_call_target="tpu_custom_call" | custom-call | tf_op jit(solution)/shard_map/pack/pallas_call | solution.py:590
  2.8 0.0 copy-start.2
  2.8 0.0 copy-start.4
  2.9 0.0 copy-start.6
  2.9 0.0 copy-start.7
  2.9 0.0 copy-start.15
  2.9 0.0 copy-start.17
  2.9 0.0 copy-start.18
  2.9 10.4 %all-to-all-start = ((bf16[16,24,512]{2,1,0:T(8,128)(2,1)}), bf16[16,24,512]{2,1,0:T(8,128)(2,1)S(1)}, u32[]{:S(2)}, u32[]{:S(2)}) async-start(bf16[16,24,512]{2,1,0:T(8,128)(2,1)} %pack.1), calls=%async_computation | async-start | bytes 786432 | tf_op jit(solution)/shard_map/all_to_all | solution.py:539
  13.3 0.0 copy-start.8
  13.3 0.0 copy-start.9
  13.3 0.0 copy-start.10
  13.3 0.0 copy-done.11
  13.3 0.0 copy-done.2
  13.3 0.0 copy-done.4
  13.3 0.0 copy-done.6
  13.4 0.0 copy-done.7
  13.4 0.0 copy-done.15
  13.4 0.0 copy-done.17
  13.4 0.0 copy-done.18
  13.4 0.6 copy-done.16
  14.0 0.0 copy-done.8
  14.0 0.0 copy-done.9
  14.0 0.0 copy-done.10
  14.0 2.4 %prompt_features.1 = (f32[128,512]{1,0:T(8,128)S(1)}, f32[128,32]{1,0:T(8,128)S(1)}, bf16[128,512]{1,0:T(8,128)(2,1)S(1)}, f32[128,512]{1,0:T(8,128)S(1)}, f32[4...) custom-call(s32[16]{0:T(128)S(1)} %copy-done.8, ...), custom_call_target="tpu_custom_call" | custom-call | flops 1000000000 | bytes 2000000 | tf_op jit(solution)/shard_map/prompt_features/pallas_call | solution.py:605
  16.4 11.4 %all-to-all-done.got_ref = bf16[16,24,512]{2,1,0:T(8,128)(2,1)S(1)} async-done(((bf16[16,24,512]{2,1,0:T(8,128)(2,1)}), bf16[16,24,512]{2,1,0:T(8,128)(2,1)S(1)}, u32[]{:S(2)}, u32[]{:S(2)}) %all-to-all-start) | async-done | bytes 393248 | tf_op jit(solution)/shard_map/all_to_all | solution.py:539
  27.8 0.0 copy-done.3
  27.8 0.0 copy-done.5
  27.8 0.7 decode_features.1
  28.6 0.0 copy-start.13
  28.6 23.5 %all_to_all.20.got_ref = bf16[32,7,4,128]{3,2,1,0:T(4,128)(2,1)S(1)} all-to-all(bf16[32,7,4,128]{3,2,1,0:T(4,128)(2,1)S(1)} %get-tuple-element.37), channel_id=1, replica_groups=mesh['group'=16,'mp'=32] {'mp'}, dimensions={0} | all-to-all | bytes 458752 | tf_op jit(solution)/shard_map/all_to_all | solution.py:539
  52.0 0.0 copy-done.13
  52.0 0.1 sum_parts.1
  52.1 14.7 %all_to_all.21.rows_ref = bf16[32,7,4,128]{3,2,1,0:T(4,128)(2,1)S(1)} all-to-all(bf16[32,7,4,128]{3,2,1,0:T(4,128)(2,1)S(1)} %sum_parts.1), channel_id=1, replica_groups=mesh['group'=16,'mp'=32] {'mp'}, dimensions={0} | all-to-all | bytes 458752 | tf_op jit(solution)/shard_map/all_to_all | solution.py:539
  66.9 0.0 copy-done
  66.9 2.4 %prefill_scan.1 = (bf16[8,16,512]{2,1,0:T(8,128)(2,1)}, bf16[16,9,4,512]{3,2,1,0:T(4,128)(2,1)}) custom-call(s32[32]{0:T(128)S(1)} %get-tuple-element.32.plan_ref, bf16[32,7,4,128]{3,2,1,0:T(4,128)(2,1)S(1)} %all_to_all.21.rows_ref, bf16[128,512]{1,0:T(8,128)(2,1)S(1)} %get-tuple-element.38.x_ref, ...), custom_call_target="tpu_custom_call", output_to_operand_aliasing={{1}: (9, {})} | custom-call | tf_op jit(solution)/shard_map/prefill_scan/pallas_call | solution.py:667
  69.3 0.0 copy-start.1
  69.3 0.0 copy-start.12
  69.3 5.7 %all-to-all-start.3 = ((bf16[16,9,4,512]{3,2,1,0:T(4,128)(2,1)}), bf16[16,9,4,512]{3,2,1,0:T(4,128)(2,1)S(1)}, u32[]{:S(2)}, u32[]{:S(2)}) async-start(bf16[16,9,4,512]{3,2,1,0:T(4,128)(2,1)} %get-tuple-element.43), calls=%async_computation.3 | async-start | bytes 1179648 | tf_op jit(solution)/shard_map/all_to_all | solution.py:539
  75.0 0.0 copy-done.1
  75.0 0.0 copy-done.12
  75.0 0.0 copy-start.14
  75.0 0.8 copy-done.14
  75.8 2.8 %decode_scan.1 = (bf16[16,4,512]{2,1,0:T(4,128)(2,1)}, f32[16,16,512]{2,1,0:T(8,128)}, f32[16,512]{1,0:T(8,128)S(1)}, f32[4,16,512]{2,1,0:T(8,128)S(1)}, f32[16,...) custom-call(s32[32]{0:T(128)S(1)} %get-tuple-element.32.plan_ref, ...), custom_call_target="tpu_custom_call" | custom-call | flops 6000000000 | bytes 8000000 | tf_op jit(solution)/shard_map/decode_scan/pallas_call | solution.py:694
  78.7 0.6 convert_bitcast_fusion
  79.3 14.3 %all-to-all-done.3.got_ref = bf16[16,9,4,512]{3,2,1,0:T(4,128)(2,1)S(1)} async-done(((bf16[16,9,4,512]{3,2,1,0:T(4,128)(2,1)}), bf16[16,9,4,512]{3,2,1,0:T(4,128)(2,1)S(1)}, u32[]{:S(2)}, u32[]{:S(2)}) %all-to-all-start.3) | async-done | bytes 589856 | tf_op jit(solution)/shard_map/all_to_all | solution.py:539
  93.6 1.3 %finish.1 = (bf16[16,4,512]{2,1,0:T(4,128)(2,1)}, f32[16,16,512]{2,1,0:T(8,128)}, f32[32,16,512]{2,1,0:T(8,128)}) custom-call(bf16[16,9,4,512]{3,2,1,0:T(4,128)(2,1)S(1)} %all-to-all-done.3.got_ref, f32[16,512]{1,0:T(8,128)S(1)} %get-tuple-element.45.base_ref, ...), custom_call_target="tpu_custom_call", output_to_operand_aliasing={{0}: (6, {}), {1}: (7, {})} | custom-call | tf_op jit(solution)/shard_map/finish/pallas_call | solution.py:728
  (4 shorter events, 0.0 us)
Async XLA Ops:
  0.6 12.7 %copy-start.11 = (bf16[8,16,512]{2,1,0:T(8,128)(2,1)S(1)}, bf16[8,16,512]{2,1,0:T(8,128)(2,1)}, u32[]{:S(2)}) copy-start(bf16[8,16,512]{2,1,0:T(8,128)(2,1)} %gate_ref.2) | copy-start | bytes 393220
  2.8 10.5 %copy-start.2 = (bf16[512,512]{1,0:T(8,128)(2,1)S(1)}, bf16[512,512]{1,0:T(8,128)(2,1)}, u32[]{:S(2)}) copy-start(bf16[512,512]{1,0:T(8,128)(2,1)} %rank_ref.3) | copy-start | bytes 1572868
  2.8 10.5 %copy-start.4 = (bf16[8,16,512]{2,1,0:T(8,128)(2,1)S(1)}, bf16[8,16,512]{2,1,0:T(8,128)(2,1)}, u32[]{:S(2)}) copy-start(bf16[8,16,512]{2,1,0:T(8,128)(2,1)} %u_ref.5) | copy-start | bytes 393220
  2.9 10.5 %copy-start.6 = (bf16[512,32]{0,1:T(8,128)(2,1)S(1)}, bf16[512,32]{0,1:T(8,128)(2,1)}, u32[]{:S(2)}) copy-start(bf16[512,32]{0,1:T(8,128)(2,1)} %param.29) | copy-start | bytes 98308
  2.9 10.5 %copy-start.7 = (f32[4,512]{1,0:T(4,128)S(1)}, f32[4,512]{1,0:T(4,128)}, u32[]{:S(2)}) copy-start(f32[4,512]{1,0:T(4,128)} %cw_ref.3) | copy-start | bytes 24580
  2.9 10.5 %copy-start.15 = (f32[16,512]{1,0:T(8,128)S(1)}, f32[16,512]{1,0:T(8,128)}, u32[]{:S(2)}) copy-start(f32[16,512]{1,0:T(8,128)} %decay_ref.1) | copy-start | bytes 98308
  2.9 10.5 %copy-start.17 = (f32[512]{0:T(512)S(1)}, f32[512]{0:T(512)}, u32[]{:S(2)}) copy-start(f32[512]{0:T(512)} %param.31) | copy-start | bytes 6148
  2.9 10.5 %copy-start.18 = (f32[512]{0:T(512)S(1)}, f32[512]{0:T(512)}, u32[]{:S(2)}) copy-start(f32[512]{0:T(512)} %param.33) | copy-start | bytes 6148
  2.9 24.9 %all-to-all-start = ((bf16[16,24,512]{2,1,0:T(8,128)(2,1)}), bf16[16,24,512]{2,1,0:T(8,128)(2,1)S(1)}, u32[]{:S(2)}, u32[]{:S(2)}) async-start(bf16[16,24,512]{2,1,0:T(8,128)(2,1)} %pack.1), calls=%async_computation | async-start | bytes 786432 | tf_op jit(solution)/shard_map/all_to_all | solution.py:539
  13.3 0.7 copy-start.16
  13.3 0.7 copy-start.8
  13.3 0.7 copy-start.9
  13.3 0.7 copy-start.10
  14.0 13.8 %copy-start.3 = (bf16[16,3,512]{2,0,1:T(8,128)(2,1)S(1)}, bf16[16,3,512]{2,0,1:T(8,128)(2,1)}, u32[]{:S(2)}) copy-start(bf16[16,3,512]{2,0,1:T(8,128)(2,1)} %param.18) | copy-start | bytes 147460
  14.0 13.8 %copy-start.5 = (bf16[16,4,512]{2,1,0:T(4,128)(2,1)S(1)}, bf16[16,4,512]{2,1,0:T(4,128)(2,1)}, u32[]{:S(2)}) copy-start(bf16[16,4,512]{2,1,0:T(4,128)(2,1)} %u_ref.7) | copy-start | bytes 196612
  28.6 23.5 %copy-start.13 = (bf16[64,512]{1,0:T(8,128)(2,1)}, bf16[64,512]{1,0:T(8,128)(2,1)S(1)}, u32[]{:S(2)}) copy-start(bf16[64,512]{1,0:T(8,128)(2,1)S(1)} %get-tuple-element.44.x_ref) | copy-start | bytes 196612
  52.0 14.8 %copy-start = (bf16[512,512]{1,0:T(8,128)(2,1)S(1)}, bf16[512,512]{1,0:T(8,128)(2,1)}, u32[]{:S(2)}) copy-start(bf16[512,512]{1,0:T(8,128)(2,1)} %step_w_ref.3) | copy-start | bytes 1572868
  69.3 5.7 %copy-start.1 = (f32[16,16,512]{2,1,0:T(8,128)S(1)}, f32[16,16,512]{2,1,0:T(8,128)}, u32[]{:S(2)}) copy-start(f32[16,16,512]{2,1,0:T(8,128)} %state_ref.3) | copy-start | bytes 1572868
  69.3 5.7 %copy-start.12 = (bf16[16,4,512]{2,1,0:T(4,128)(2,1)S(1)}, bf16[16,4,512]{2,1,0:T(4,128)(2,1)}, u32[]{:S(2)}) copy-start(bf16[16,4,512]{2,1,0:T(4,128)(2,1)} %gate_ref.3) | copy-start | bytes 196612
  69.3 24.3 %all-to-all-start.3 = ((bf16[16,9,4,512]{3,2,1,0:T(4,128)(2,1)}), bf16[16,9,4,512]{3,2,1,0:T(4,128)(2,1)S(1)}, u32[]{:S(2)}, u32[]{:S(2)}) async-start(bf16[16,9,4,512]{3,2,1,0:T(4,128)(2,1)} %get-tuple-element.43), calls=%async_computation.3 | async-start | bytes 1179648 | tf_op jit(solution)/shard_map/all_to_all | solution.py:539
  75.0 0.8 copy-start.14
